TPU v7x, 32 devices: a whole 2x2x4 slice. The times are simulated.
32 devices in a mesh: batch: 4 (over z), rows: 4 (over y, x), section: 2 (over core).
Axes of the slice: x: 2, y: 2, z: 4, core: 2. Of those that a mesh axis runs over, the one named last changes fastest.
Arguments:
- features: bfloat16 [16, 16, 32, 1536], P('batch', 'rows'), may hold values from -6 to 6, as said below
- dw_kernel: bfloat16 [7, 7, 1536], replicated, may hold values from -0.875 to 0.875
- ln_gain: bfloat16 [1536], replicated, may hold values from 0.25 to 1.75
- widening_pointwise_matrix: bfloat16 [1536, 3072], P(None, 'section'), may hold values from -0.15625 to 0.15625
- w_reduce: bfloat16 [3072, 1536], P('section'), may hold values from -0.109375 to 0.109375
- layer_branch_scale: bfloat16 [1536], replicated, may hold values from 0.5 to 2
- p_expand: bfloat16 [1536, 2048], P(None, 'section'), may hold values from -0.15625 to 0.15625
- p_kernel: bfloat16 [9, 2048, 256], P(None, 'section'), may hold values from -0.046875 to 0.046875
- region_ids: int32 [16, 16, 32], P('batch', 'rows'), may hold values from 0 to 63, as said below
- owner_slot: int32 [4, 256], P('batch'), may hold values from 0 to 255, each once within a row
- partner: int32 [16, 64], P('batch'), may hold values from 0 to 63
- key_embed: bfloat16 [1024, 256], P(('batch', 'rows')), may hold values from -6 to 6
Outputs:
- region_embed: float32 [1024, 256], P(('batch', 'rows'))
- region_loss: float32 [1024], P(('batch', 'rows'))
Inputs may be any that keep to these rules, and one draw needn't show every extreme that they name: `features`: exactly one image other than image 0 has all its entries zero. `region_ids`: each image uses regions 0 to K - 1 for its own K of at least 16, every one of them on some pixel; image 0 uses all 64. `owner_slot`: each row is a permutation of the slots of one batch index.
All inputs are finite; a program needn't handle non-finite values.
Results may differ from a plain program's by a relative error of at most 0.0024.
Values may be sent and summed in bfloat16 or wider, within the bound.
No kernel may reach another device: no remote copies, remote signals or barrier semaphores. Data moves between devices by JAX's collectives and lax.ppermute only.
A program may use at most 128 MiB of HBM per device.

v0:
```python
import functools

import jax
import jax.numpy as jnp
from jax import lax
from jax.experimental import pallas as pl
from jax.experimental.pallas import tpu as pltpu
from jax.sharding import PartitionSpec as P

REG = 64
LANES = 128
STRIP = 4
CHUNKS = 2

sharpness_divisor = 0.1
ln_eps = 1e-06
norm_eps = 1e-06

VMEM = pl.BlockSpec(memory_space=pltpu.VMEM)
SMEM = pl.BlockSpec(memory_space=pltpu.SMEM)
f32 = jnp.float32
bf16 = jnp.bfloat16


def call(kernel, outs, in_specs, scratch, limit, flops, nbytes):
    return pl.pallas_call(
        kernel,
        out_shape=outs,
        in_specs=in_specs,
        out_specs=[VMEM] * len(outs),
        scratch_shapes=scratch,
        compiler_params=pltpu.CompilerParams(vmem_limit_bytes=limit),
        cost_estimate=pl.CostEstimate(flops=flops, bytes_accessed=nbytes, transcendentals=0),
    )


def dot(a, b):
    return jnp.dot(a, b, preferred_element_type=f32)


def dot_nt(a, b):
    return lax.dot_general(a, b, (((1,), (1,)), ((), ())), preferred_element_type=f32)


def gelu(x):
    return 0.5 * x * (1.0 + lax.erf(x * 0.7071067811865476))


def split(x):
    hi = x.astype(bf16)
    return hi, (x - hi.astype(f32)).astype(bf16)


def blank_kernel(_, out_ref):
    out_ref[...] = jnp.full(out_ref.shape, -1.0, f32)


def pack_kernel(pos_ref, ids_ref, key_ref, blank_ref, tail_ref, line):
    section = pos_ref[3]
    keys, depth = key_ref.shape
    shard_rows, width = ids_ref.shape[1:]
    line[...] = blank_ref[...]
    for i in range(ids_ref.shape[0]):
        line[i * shard_rows : (i + 1) * shard_rows, 0:width] = ids_ref[i].astype(f32)
    tail_ref[...] = jnp.zeros(tail_ref.shape, bf16)
    tail_ref[:, depth : depth + LANES] = line[...].astype(bf16)
    tail_ref[0 : keys // 2, 0:depth] = key_ref[pl.ds(pl.multiple_of(section * (keys // 2), keys // 2), keys // 2), :]


def join_kernel(*refs):
    start = 0
    for ref in refs[:-1]:
        refs[-1][start : start + ref.shape[0], :] = ref[...]
        start += ref.shape[0]


def join(*arrays):
    rows = sum(x.shape[0] for x in arrays)
    shape = jax.ShapeDtypeStruct((rows, arrays[0].shape[1]), arrays[0].dtype)
    joined = call(join_kernel, [shape], [VMEM] * len(arrays), [], 1 << 20, 0, rows * 1024)(*arrays)
    return joined[0]


def add_kernel(a_ref, b_ref, out_ref, send_ref):
    out_ref[...] = a_ref[...] + b_ref[...]
    send_ref[...] = out_ref[...].astype(bf16)


def conv_kernel(geo, pos_ref, *refs):
    order, shard_rows, width, out_rows, first_lane = geo
    shards = len(order)
    blocks = dict(zip(order, refs[:shards]))
    w_ref, taps, img_ref, xpad, wide = refs[shards:]
    chunk = taps.shape[1]
    row, first_row, col0 = pos_ref[0], pos_ref[1], pos_ref[2]
    height = shards * shard_rows
    pixels = shard_rows * width
    cols = xpad.shape[1]
    out_pixels = out_rows * width
    step_rows = STRIP

    xpad[0:3] = jnp.zeros((3, cols, LANES), f32)
    xpad[height + 3 : height + 6] = jnp.zeros((3, cols, LANES), f32)
    for y in range(3, height + 3):
        xpad[y, 0:8] = jnp.zeros((8, LANES), f32)
        xpad[y, 8 + width : 16 + width] = jnp.zeros((8, LANES), f32)

    def group(g, carry):
        lanes = pl.ds(pl.multiple_of(g * LANES, LANES), LANES)
        for k in range(shards):
            value = blocks[k][0:pixels, lanes].astype(f32).reshape(shard_rows, width, LANES)
            xpad[pl.ds(3 + (row ^ k) * shard_rows, shard_rows), 8 : 8 + width, :] = value
        start = pos_ref[3] * (w_ref.shape[2] // 2) + first_lane + g * LANES
        for dy in range(7):
            w = w_ref[dy, :, pl.ds(pl.multiple_of(start, LANES), LANES)].astype(f32)
            for dx in range(7):
                wide[dy * 7 + dx] = jnp.broadcast_to(w[dx : dx + 1], (8, LANES))

        def strip(i, carry):
            top = first_row + i * step_rows
            acc = [jnp.zeros((width // 8, 8, LANES), f32) for _ in range(step_rows)]
            for r in range(step_rows + 6):
                for dx in range(7):
                    v = xpad[top + r, pl.ds(col0 + dx, width), :].reshape(width // 8, 8, LANES)
                    for j in range(step_rows):
                        dy = r - j
                        if 0 <= dy < 7:
                            acc[j] = acc[j] + v * wide[dy * 7 + dx][None]
            for j in range(step_rows):
                start = pl.multiple_of((i * step_rows + j) * width, width)
                taps[pl.ds(start, width), lanes] = acc[j].reshape(width, LANES)
            return carry

        return lax.fori_loop(0, out_rows // step_rows, strip, carry)

    lax.fori_loop(0, chunk // LANES, group, 0)

    for k in range(shards):
        start = (row ^ k) * pixels - first_row * width

        @pl.when((start >= 0) & (start < out_pixels))
        def _():
            img_ref[pl.ds(pl.multiple_of(start, pixels), pixels), :] = blocks[k][0:pixels, :]


def block_kernel(geo, pos_ref, *refs):
    first, pixels, chunks = geo
    own, other, img = refs[:chunks], refs[chunks : 2 * chunks], refs[2 * chunks : 3 * chunks]
    gain_ref, scale_ref, w1_ref, w2_ref, z_ref, normed, inner, wide = refs[3 * chunks :]
    chans, hid = w1_ref.shape
    half = chans // 2
    width = half // chunks
    section = pos_ref[3]
    rows = slice(first, first + pixels)
    gains = gain_ref[...].astype(f32).reshape(1, chans)
    scales = scale_ref[...].astype(f32).reshape(1, chans)
    gains = [gains[:, n * width : (n + 1) * width] for n in range(2 * chunks)]
    gains_own = [jnp.where(section == 0, gains[c], gains[chunks + c]) for c in range(chunks)]
    gains_other = [jnp.where(section == 0, gains[chunks + c], gains[c]) for c in range(chunks)]
    block = 32
    for r in range(pixels // block):
        part = slice(first + r * block, first + (r + 1) * block)
        values = [ref[part, :] for ref in own + other]
        mean = sum(jnp.sum(v, axis=1, keepdims=True) for v in values) * (1.0 / chans)
        values = [v - mean for v in values]
        spread = sum(jnp.sum(v * v, axis=1, keepdims=True) for v in values) * (1.0 / chans)
        inv = lax.rsqrt(spread + ln_eps)
        values = [(v * inv * g).astype(bf16) for v, g in zip(values, gains_own + gains_other)]
        to = slice(r * block, (r + 1) * block)
        for c in range(chunks):
            for side, value in ((section, values[c]), (1 - section, values[chunks + c])):
                start = pl.multiple_of(side * half + c * width, LANES)
                normed[to, pl.ds(start, width)] = value
    step = 256

    def widen(i):
        cols = slice(i * step, (i + 1) * step)
        return dot(normed[...], w1_ref[:, cols])

    wide[0] = widen(0)
    for i in range(hid // step):
        if i + 1 < hid // step:
            wide[(i + 1) % 2] = widen(i + 1)
        inner[:, i * step : (i + 1) * step] = gelu(wide[i % 2]).astype(bf16)
    step = width if width % 256 else 256

    def narrow(i):
        return dot(inner[...], w2_ref[:, i * step : (i + 1) * step])

    ahead = narrow(0)
    for i in range(chans // step):
        z = ahead
        if i + 1 < chans // step:
            ahead = narrow(i + 1)
        cols = slice(i * step, (i + 1) * step)
        side, start = divmod(i * step, half)
        c, start = divmod(start, width)
        keep = jnp.where(section == side, 1.0, 0.0)
        z_ref[:, cols] = z * scales[:, cols] + img[c][rows, start : start + step].astype(f32) * keep


def expand_kernel(z_ref, other_ref, pe_ref, out_ref, block):
    block[...] = (z_ref[...] + other_ref[...]).astype(bf16)
    step = 256
    for i in range(pe_ref.shape[1] // step):
        cols = slice(i * step, (i + 1) * step)
        out_ref[:, cols] = jnp.maximum(dot(block[...], pe_ref[:, cols]), 0.0).astype(bf16)


def prep_kernel(geo, pos_ref, *refs):
    order, shard_rows, width, out_pixels, parts = geo
    shards = len(order)
    ids = [refs[order.index(k)] for k in range(shards)]
    hot_ref, flat = refs[shards:]
    row, first_row = pos_ref[0], pos_ref[1]
    pixels = shard_rows * width
    depth = ids[0].shape[1] - LANES
    ids = [ref[pixels:, depth : depth + LANES].astype(f32) for ref in ids]
    image = row // parts
    flat[...] = jnp.full(flat.shape, -1.0, f32)
    for k in range(shards):
        start = pl.multiple_of((1 + (row ^ k)) * pixels, LANES)
        number = lax.broadcasted_iota(jnp.int32, ids[k].shape, 0)
        inside = lax.broadcasted_iota(jnp.int32, ids[k].shape, 1) < width
        for y in range(shard_rows):
            keep = inside & (number == image * shard_rows + y)
            mine = jnp.sum(jnp.where(keep, ids[k], 0.0), axis=0, keepdims=True)
            mine = jnp.broadcast_to(mine, (8, LANES))
            mine = pltpu.roll(mine, y * width, 1) if y else mine
            line = mine if y == 0 else line + mine
        flat[0:8, pl.ds(start, pixels)] = line
    total = flat.shape[1]
    whole = jnp.broadcast_to(flat[0:1, :], (8, total))
    lane = lax.broadcasted_iota(jnp.int32, (8, total), 1)
    col = lane % width
    region = lax.broadcasted_iota(jnp.int32, (REG, out_pixels), 0).astype(f32)
    start = pl.multiple_of(pixels + first_row * width, LANES)
    for dy in range(3):
        for dx in range(3):
            off = (dy - 1) * width + dx - 1
            moved = whole if off == 0 else pltpu.roll(whole, off % total, 1)
            if dx == 0:
                moved = jnp.where(col == width - 1, -1.0, moved)
            if dx == 2:
                moved = jnp.where(col == 0, -1.0, moved)
            flat[8:16, :] = moved
            line = flat[8:9, pl.ds(start, out_pixels)]
            tap = dy * 3 + dx
            hot_ref[tap * REG : (tap + 1) * REG, :] = jnp.where(region == line, 1.0, 0.0).astype(bf16)


def unpack_kernel(geo, *refs):
    order, pixels = geo
    keys_ref = refs[-1]
    count = keys_ref.shape[0] // len(order)
    for k, ref in zip(order, refs):
        keys_ref[k * count : (k + 1) * count, :] = ref[pixels : pixels + count, 0 : keys_ref.shape[1]]


def owner_kernel(geo, pos_ref, *refs):
    order, shard_rows, pixels, images, batches, per_key = geo
    shards = len(order)
    ids = [refs[order.index(k)] for k in range(shards)]
    owner_ref, partner_ref, pick_ref, own_ref = refs[shards:]
    row, batch, first_slot = pos_ref[0], pos_ref[4], pos_ref[5]
    depth = ids[0].shape[1] - LANES
    ids = [ref[pixels:, depth : depth + LANES].astype(f32) for ref in ids]
    owned, slots = pick_ref.shape
    slot = lax.broadcasted_iota(jnp.int32, (owned, slots), 1)
    want = lax.broadcasted_iota(jnp.int32, (owned, slots), 0) + first_slot
    pick = owner_ref[...] == want
    pick_ref[...] = jnp.where(pick, 1.0, 0.0).astype(bf16)
    one_region = lax.broadcasted_iota(jnp.int32, (REG, LANES), 0).astype(f32)
    tallies = []
    for i in range(images):
        tally = jnp.zeros((REG, LANES), f32)
        for k in range(shards):
            for y in range(i * shard_rows, (i + 1) * shard_rows):
                tally = tally + jnp.where(one_region == ids[k][y : y + 1, :], 1.0, 0.0)
        tallies.append(tally)
    tally = jnp.concatenate(tallies, axis=0).astype(bf16)
    count = dot_nt(jnp.ones((8, LANES), bf16), tally)[0:1]
    mates = jnp.concatenate([partner_ref[i : i + 1, :] for i in range(images)], axis=1)
    mate = (batch * images + slot // REG) * REG + mates
    block = mate // per_key
    within = mate % per_key
    core = (within // (per_key // 2)) ^ pos_ref[3]
    apart = (block // shards) ^ batch
    turn = core
    for n in range(batches.bit_length() - 1):
        turn = turn * 2 + ((apart >> n) & 1)
    place = turn * shards + ((block % shards) ^ row)
    place = place * (per_key // 2) + within % (per_key // 2)
    place = jnp.sum(jnp.where(pick, place, 0).astype(f32), axis=1, keepdims=True)
    number = jnp.sum(jnp.where(pick, count, 0.0), axis=1, keepdims=True)
    side = lax.broadcasted_iota(jnp.int32, (owned, LANES), 1)
    own_ref[...] = jnp.where(side == 0, place, jnp.where(side == 1, number, 0.0))


def project_kernel(z_ref, other_ref, first_ref, pe_ref, pk_ref, hot_ref, out_ref, block, hidden, sums):
    before = first_ref.shape[0]
    pixels = z_ref.shape[0]
    taps = pk_ref.shape[0]
    block[...] = (z_ref[...] + other_ref[...]).astype(bf16)
    step = 256
    acc = jnp.zeros((2 * REG, out_ref.shape[1]), f32)
    tiles = pe_ref.shape[1] // step

    def collect(i):
        cols = slice(i * step, (i + 1) * step)
        hidden[i, 0:before, :] = first_ref[:, cols]
        h = jnp.maximum(dot(block[...], pe_ref[:, cols]), 0.0)
        hidden[i, before : before + pixels, :] = h.astype(bf16)
        sums[i % 2] = dot(hot_ref[...], hidden[i])

    collect(0)
    for i in range(tiles):
        if i + 1 < tiles:
            collect(i + 1)
        cols = slice(i * step, (i + 1) * step)
        for t in range(taps):
            both = jnp.concatenate(split(sums[i % 2, t * REG : (t + 1) * REG, :]), axis=0)
            acc = acc + dot(both, pk_ref[t, cols, :])
    out_ref[...] = acc[0:REG] + acc[REG:]


def keys_kernel(*refs):
    keys_ref, length_ref = refs[-2:]
    keys = jnp.concatenate([ref[...] for ref in refs[:-2]], axis=0).astype(f32).T
    keys_ref[...] = keys.astype(bf16)
    length_ref[...] = lax.rsqrt(jnp.sum(keys * keys, axis=0, keepdims=True) + norm_eps)


def loss_kernel(geo, *refs):
    shards, parts = geo
    sums, row = refs[1 : shards + 1], refs[0][0]
    pick_ref, own_ref, keys_ref, length_ref, embed_ref, loss_ref, table = refs[shards + 1 :]
    if parts > 1:
        table[...] = jnp.zeros(table.shape, f32)
    for k in range(shards):
        place = pl.ds(pl.multiple_of(((row ^ k) // parts) * REG, REG), REG)
        value = sums[k][...].astype(f32)
        table[place, :] = value if parts == 1 else table[place, :] + value
    pick = pick_ref[...]
    hi, lo = split(table[...])
    ordered = dot(pick, hi) + dot(pick, lo)
    unit = ordered * lax.rsqrt(jnp.sum(ordered * ordered, axis=1, keepdims=True) + norm_eps)
    embed_ref[...] = unit
    owned = unit.shape[0]
    both = dot(jnp.concatenate(split(unit), axis=0), keys_ref[...])
    logits = both[0:owned] + both[owned:]
    logits = logits * (length_ref[...] / sharpness_divisor)
    total = jnp.log(jnp.sum(jnp.exp(logits), axis=1, keepdims=True))
    column = lax.broadcasted_iota(jnp.int32, logits.shape, 1).astype(f32)
    match = jnp.sum(jnp.where(column == own_ref[:, 0:1], logits, 0.0), axis=1, keepdims=True)
    loss = jnp.where(own_ref[:, 1:2] > 0.5, total - match, 0.0)
    line = lax.broadcasted_iota(jnp.int32, (owned, owned), 0)
    other = lax.broadcasted_iota(jnp.int32, (owned, owned), 1)
    loss_ref[...] = jnp.sum(jnp.where(line == other, loss, 0.0), axis=0, keepdims=True)


def swap(x, axis, bit):
    return lax.ppermute(x, axis, [(i, i ^ bit) for i in range(lax.axis_size(axis))])


def body(
    features,
    dw_kernel,
    ln_gain,
    widening_pointwise_matrix,
    w_reduce,
    layer_branch_scale,
    p_expand,
    p_kernel,
    region_ids,
    owner_slot,
    partner,
    key_embed,
):
    images, shard_rows, width, chans = features.shape
    shards = lax.axis_size("rows")
    batches = lax.axis_size("batch")
    row = lax.axis_index("rows")
    batch = lax.axis_index("batch")
    section = lax.axis_index("section")
    half = chans // lax.axis_size("section")
    parts = shards // images
    out_rows = shards * shard_rows // parts
    pixels = shard_rows * width
    out_pixels = out_rows * width
    slots = images * REG
    owned = slots // shards
    out_dim = p_kernel.shape[2]
    mib = 1 << 20
    span = half // CHUNKS

    w1, w2, pe, pk = widening_pointwise_matrix, w_reduce, p_expand, p_kernel
    first_row = (row % parts) * out_rows
    spot = jnp.stack(
        [row, first_row, jnp.int32(5), section, batch, row * owned]
    ).astype(jnp.int32)

    per_key, depth = key_embed.shape
    tail = max(-(-images * shard_rows // 16) * 16, per_key // 2)
    def after(here, *done):
        return lax.optimization_barrier((here, *done))[0]

    parcels = []
    for c in range(CHUNKS):
        blocks = []
        for k in range(shards):
            place = ((row ^ k) // parts, 0, 0, section * half + c * span)
            part = lax.dynamic_slice(features, place, (1, shard_rows, width, span))
            blocks.append(part.reshape(pixels, span))
        parcels.append(blocks)
    (blank,) = call(
        blank_kernel, [jax.ShapeDtypeStruct((tail, LANES), f32)], [VMEM], [], mib, 10**10, 10**4
    )(parcels[0][0])
    parcels[0] = after(parcels[0], blank)
    (riders,) = call(
        pack_kernel,
        [jax.ShapeDtypeStruct((tail, span), bf16)],
        [SMEM] + [VMEM] * 3,
        [pltpu.VMEM((tail, LANES), f32)],
        mib,
        0,
        10**6,
    )(spot, region_ids, key_embed, blank)
    parcels[-1] = [jnp.concatenate([part, riders], axis=0) for part in parcels[-1]]
    got = [
        [blocks[0]] + [swap(blocks[k], "rows", k) for k in range(1, shards)] for blocks in parcels
    ]
    order = list(range(shards))
    last = [got[-1][k] for k in order]

    own, other, img = [], [], []
    for c in range(CHUNKS):
        here = after(spot, *own) if c else spot
        taps, image = call(
            functools.partial(conv_kernel, (order, shard_rows, width, out_rows, c * span)),
            [
                jax.ShapeDtypeStruct((out_pixels, span), f32),
                jax.ShapeDtypeStruct((out_pixels, span), bf16),
            ],
            [SMEM] + [VMEM] * (shards + 1),
            [
                pltpu.VMEM((shards * shard_rows + 6, width + 16, LANES), f32),
                pltpu.VMEM((49, 8, LANES), f32),
            ],
            3 * mib,
            out_pixels * span * 98 * 100,
            out_pixels * span * 10,
        )(here, *[got[c][k] for k in order], dw_kernel)
        own.append(taps)
        img.append(image)
        other.append(swap(taps, "section", 1))

    (keys,) = call(
        functools.partial(unpack_kernel, (order, pixels)),
        [jax.ShapeDtypeStruct((shards * per_key // 2, depth), bf16)],
        [VMEM] * shards,
        [],
        mib,
        10**6,
        10**6,
    )(*after(last, *own))
    bits = [1 << n for n in reversed(range(batches.bit_length() - 1))]
    pieces = [keys, swap(keys, "batch", bits[0])]

    hid = w1.shape[1]
    part_pixels = out_pixels // 2
    z, z_other = [], []
    for p in range(2):
        here = after(spot, pieces[-1], *z) if p else after(spot, keys)
        (mine,) = call(
            functools.partial(block_kernel, (p * part_pixels, part_pixels, CHUNKS)),
            [jax.ShapeDtypeStruct((part_pixels, chans), f32)],
            [SMEM] + [VMEM] * (3 * CHUNKS + 4),
            [
                pltpu.VMEM((part_pixels, chans), bf16),
                pltpu.VMEM((part_pixels, hid), bf16),
                pltpu.VMEM((2, part_pixels, 256), f32),
            ],
            8 * mib,
            4 * part_pixels * hid * chans,
            4 * hid * chans,
        )(here, *own, *other, *img, ln_gain, layer_branch_scale, w1, w2)
        z.append(mine)
        z_other.append(swap(mine, "section", 1))
    for bit in bits[1:]:
        pieces.append(swap(join(*pieces), "batch", bit))

    hidden = pe.shape[1]
    (hid_a,) = call(
        expand_kernel,
        [jax.ShapeDtypeStruct((part_pixels, hidden), bf16)],
        [VMEM] * 3,
        [pltpu.VMEM((part_pixels, chans), bf16)],
        6 * mib,
        2 * part_pixels * hidden * chans,
        2 * hidden * chans,
    )(z[0], z_other[0], pe)
    (hot,) = call(
        functools.partial(prep_kernel, (order, shard_rows, width, out_pixels, parts)),
        [jax.ShapeDtypeStruct((9 * REG, out_pixels), bf16)],
        [SMEM] + [VMEM] * shards,
        [pltpu.VMEM((16, (shards + 2) * pixels), f32)],
        2 * mib,
        10**8,
        10**6,
    )(after(spot, hid_a), *last)
    (pooled,) = call(
        project_kernel,
        [jax.ShapeDtypeStruct((REG, out_dim), f32)],
        [VMEM] * 6,
        [
            pltpu.VMEM((part_pixels, chans), bf16),
            pltpu.VMEM((hidden // 256, out_pixels, 256), bf16),
            pltpu.VMEM((2, 9 * REG, 256), f32),
        ],
        8 * mib,
        2 * part_pixels * hidden * chans + 4 * 9 * REG * hidden * out_pixels,
        4 * hidden * chans,
    )(z[1], z_other[1], hid_a, pe, pk, hot)
    pick, facts = call(
        functools.partial(owner_kernel, (order, shard_rows, pixels, images, batches, per_key)),
        [jax.ShapeDtypeStruct((owned, slots), bf16), jax.ShapeDtypeStruct((owned, LANES), f32)],
        [SMEM] + [VMEM] * (shards + 2),
        [],
        2 * mib,
        10**8,
        10**6,
    )(after(spot, pooled), *last, owner_slot, partner)
    total, send = call(
        add_kernel,
        [jax.ShapeDtypeStruct((REG, out_dim), f32), jax.ShapeDtypeStruct((REG, out_dim), bf16)],
        [VMEM] * 2,
        [],
        mib,
        10**5,
        10**5,
    )(pooled, swap(pooled, "section", 1))
    sums = [swap(send, "rows", k) if k else total for k in range(shards)]
    pieces[-1] = after(pieces[-1], pooled)
    pieces.append(swap(join(*pieces), "section", 1))
    count = sum(x.shape[0] for x in pieces)
    keys, length = call(
        keys_kernel,
        [jax.ShapeDtypeStruct((depth, count), bf16), jax.ShapeDtypeStruct((1, count), f32)],
        [VMEM] * len(pieces),
        [],
        4 * mib,
        10**9,
        10**6,
    )(*pieces)

    embed, loss = call(
        functools.partial(loss_kernel, (shards, parts)),
        [jax.ShapeDtypeStruct((owned, out_dim), f32), jax.ShapeDtypeStruct((1, owned), f32)],
        [SMEM] + [VMEM] * (len(sums) + 4),
        [pltpu.VMEM((slots, out_dim), f32)],
        6 * mib,
        10**8,
        10**6,
    )(spot, *sums, pick, facts, keys, length)
    return embed, loss.reshape(owned)


def solution(mesh):
    in_specs = (
        P("batch", "rows", None, None),
        P(),
        P(),
        P(None, "section"),
        P("section", None),
        P(),
        P(None, "section"),
        P(None, "section", None),
        P("batch", "rows", None),
        P("batch", None),
        P("batch", None),
        P(("batch", "rows"), None),
    )
    out_specs = (P(("batch", "rows"), None), P(("batch", "rows")))
    return jax.shard_map(body, mesh=mesh, in_specs=in_specs, out_specs=out_specs, check_vma=False)
```

profile of v0, /device:TPU:0, one launch (start us, length us, event | category | flops | bytes accessed | tf_op | source)
XLA Modules:
  0.0 49.4 jit_solution(14904888373757180750)
XLA Ops:
  0.7 1.3 %constant_dynamic-slice_fusion = (bf16[1,4,32,384]{3,2,1,0:T(8,128)(2,1)S(1)}, bf16[1,4,32,384]{3,2,1,0:T(8,128)(2,1)S(1)}, bf16[1,4,32,384]{3,2,1,0:T(8,128)(2,...) fusion(bf16[4,4,32,1536]{3,2,1,0:T(8,128)(2,1)} %param.12, ...), kind=kLoop, calls=%fused_computation.4 | loop fusion | bytes 1572888 | tf_op jit(solution)/shard_map/dynamic_slice | solution.py:413
  2.0 0.0 copy-start.1
  2.0 0.0 copy-start.4
  2.0 0.0 copy-start.7
  2.0 3.0 %collective-permute-start.3 = (bf16[128,384]{1,0:T(8,128)(2,1)S(1)}, bf16[128,384]{1,0:T(8,128)(2,1)S(1)}, u32[]{:S(2)}, u32[]{:S(2)}) collective-permute-start(bf16[128,384]{1,0:T(8,128)(2,1)S(1)} %bitcast.27), channel_id=1, source_target_pairs={{0,2},{2,0},{4,6},{6,4},{1,3},{3,1},{5,7},{7,5},{8,10},{10,8},{12,... | collective-permute-start | bytes 294920 | tf_op jit(solution)/shard_map/ppermute | solution.py:363
  5.0 1.5 %collective-permute-start.4 = (bf16[128,384]{1,0:T(8,128)(2,1)S(1)}, bf16[128,384]{1,0:T(8,128)(2,1)S(1)}, u32[]{:S(2)}, u32[]{:S(2)}) collective-permute-start(bf16[128,384]{1,0:T(8,128)(2,1)S(1)} %bitcast.26), channel_id=1, source_target_pairs={{0,4},{2,6},{4,0},{6,2},{1,5},{3,7},{5,1},{7,3},{8,12},{10,14},{12... | collective-permute-start | bytes 294920 | tf_op jit(solution)/shard_map/ppermute | solution.py:363
  6.5 0.0 collective-permute-start.5
  6.6 0.1 stack.20.pos_ref.refs_0_
  6.6 0.0 copy-done.1
  6.7 0.0 copy-done.4
  6.7 0.6 %shard_map.132 = bf16[32,384]{1,0:T(8,128)(2,1)S(1)} custom-call(s32[6]{0:T(128)S(1)} %stack.20.pos_ref.refs_0_, s32[4,4,32]{2,1,0:T(4,128)S(1)} %copy-done.4, bf16[64,256]{1,0:T(8,128)(2,1)S(1)} %copy-done.1, f32[32,128]{1,0:T(8,128)S(1)} %shard_map.131.blank_ref), custom_call_target="tpu_custom_call" | custom-call | bytes 1000000 | tf_op jit(solution)/shard_map/pallas_call | solution.py:420
  7.2 0.0 slice-start.2
  7.2 0.1 pad_maximum_fusion
  7.3 2.0 %collective-permute-start = (bf16[160,384]{1,0:T(8,128)(2,1)S(1)}, bf16[160,384]{1,0:T(8,128)(2,1)S(1)}, u32[]{:S(2)}, u32[]{:S(2)}) collective-permute-start(bf16[160,384]{1,0:T(8,128)(2,1)S(1)} %get-tuple-element.63), channel_id=1, source_target_pairs={{0,2},{2,0},{4,6},{6,4},{1,3},{3,1},{5,7},{7,5},{8,10},{10,8},{12,... | collective-permute-start | bytes 368648 | tf_op jit(solution)/shard_map/ppermute | solution.py:363
  9.3 1.5 %collective-permute-start.1 = (bf16[160,384]{1,0:T(8,128)(2,1)S(1)}, bf16[160,384]{1,0:T(8,128)(2,1)S(1)}, u32[]{:S(2)}, u32[]{:S(2)}) collective-permute-start(bf16[160,384]{1,0:T(8,128)(2,1)S(1)} %get-tuple-element.64), channel_id=1, source_target_pairs={{0,4},{2,6},{4,0},{6,2},{1,5},{3,7},{5,1},{7,3},{8,12},{10,14},{12... | collective-permute-start | bytes 368648 | tf_op jit(solution)/shard_map/ppermute | solution.py:363
  10.8 0.0 collective-permute-done.3.refs_1_
  10.8 0.5 %collective-permute-start.2 = (bf16[160,384]{1,0:T(8,128)(2,1)S(1)}, bf16[160,384]{1,0:T(8,128)(2,1)S(1)}, u32[]{:S(2)}, u32[]{:S(2)}) collective-permute-start(bf16[160,384]{1,0:T(8,128)(2,1)S(1)} %get-tuple-element.62), channel_id=1, source_target_pairs={{0,6},{2,4},{4,2},{6,0},{1,7},{3,5},{5,3},{7,1},{8,14},{10,12},{12... | collective-permute-start | bytes 368648 | tf_op jit(solution)/shard_map/ppermute | solution.py:363
  11.3 0.0 collective-permute-done.4.refs_2_
  11.3 1.5 %collective-permute-done.5.refs_3_ = bf16[128,384]{1,0:T(8,128)(2,1)S(1)} collective-permute-done((bf16[128,384]{1,0:T(8,128)(2,1)S(1)}, bf16[128,384]{1,0:T(8,128)(2,1)S(1)}, u32[]{:S(2)}, u32[]{:S(2)}) %collective-permute-start.5) | collective-permute-done | bytes 98336 | tf_op jit(solution)/shard_map/ppermute | solution.py:363
  12.9 0.0 copy-done.7
  12.9 3.5 %shard_map.133 = (f32[512,384]{1,0:T(8,128)S(1)}, bf16[512,384]{1,0:T(8,128)(2,1)S(1)}) custom-call(s32[6]{0:T(128)S(1)} %stack.20.pos_ref.refs_0_, bf16[128,384]{1,0:T(8,128)(2,1)S(1)} %bitcast.20, bf16[128,384]{1,0:T(8,128)(2,1)S(1)} %collective-permute-done.3.refs_1_, bf16[128,384]{1,0:T(8,128)(2,1)S(1)} %collective-permute-done.4.refs_2_, ...), custom_call_target="tpu_custom_call" | custom-call | flops 1926758400 | bytes 1966080 | tf_op jit(solution)/shard_map/pallas_call | solution.py:439
  16.4 0.1 collective-permute-start.7
  16.4 0.0 collective-permute-done.refs_1_
  16.5 0.6 %collective-permute-done.1.refs_2_ = bf16[160,384]{1,0:T(8,128)(2,1)S(1)} collective-permute-done((bf16[160,384]{1,0:T(8,128)(2,1)S(1)}, bf16[160,384]{1,0:T(8,128)(2,1)S(1)}, u32[]{:S(2)}, u32[]{:S(2)}) %collective-permute-start.1) | collective-permute-done | bytes 122912 | tf_op jit(solution)/shard_map/ppermute | solution.py:363
  17.0 0.0 collective-permute-done.2.refs_3_
  17.0 3.5 %shard_map.134 = (f32[512,384]{1,0:T(8,128)S(1)}, bf16[512,384]{1,0:T(8,128)(2,1)S(1)}) custom-call(s32[6]{0:T(128)S(1)} %stack.20.pos_ref.refs_0_, bf16[160,384]{1,0:T(8,128)(2,1)S(1)} %get-tuple-element.35.refs_0_, bf16[160,384]{1,0:T(8,128)(2,1)S(1)} %collective-permute-done.refs_1_, bf16[160,384]{1,0:T(8,128)(2,1)S(1)} %collective-permute-done.1.refs_2_, ...), custom_call_target="tpu_custom_call" | custom-call | flops 1926758400 | bytes 1966080 | tf_op jit(solution)/shard_map/pallas_call | solution.py:439
  20.5 0.1 collective-permute-start.8
  20.6 2.7 %collective-permute-start.6 = (bf16[128,256]{1,0:T(8,128)(2,1)S(1)}, bf16[128,256]{1,0:T(8,128)(2,1)S(1)}, u32[]{:S(2)}, u32[]{:S(2)}) collective-permute-start(bf16[128,256]{1,0:T(8,128)(2,1)S(1)} %shard_map.135.refs_0_), channel_id=1, source_target_pairs={{0,16},{8,24},{16,0},{24,8},{1,17},{9,25},{17,1},{25,9},{2,18},{10... | collective-permute-start | bytes 196616 | tf_op jit(solution)/shard_map/ppermute | solution.py:363
  23.3 0.0 collective-permute-done.7.refs_2_
  23.3 0.0 collective-permute-done.8.refs_3_
  23.3 0.0 slice-done.2
  23.3 0.0 slice-done.3
  23.3 0.0 slice-done
  23.3 0.0 slice-done.1
  23.3 0.0 slice-start.4
  23.4 4.2 %shard_map.136.z_ref = f32[256,1536]{1,0:T(8,128)S(1)} custom-call(s32[6]{0:T(128)S(1)} %stack.20.pos_ref.refs_0_, f32[512,384]{1,0:T(8,128)S(1)} %get-tuple-element.32.refs_0_, f32[512,384]{1,0:T(8,128)S(1)} %get-tuple-element.34.refs_1_, f32[512,384]{1,0:T(8,128)S(1)} %collective-permute-done.7.refs_2_, f32[512,384]{1,0:T(8,128)S(1)} %collective-permute-done.8.refs_3_, ...), custom_call_target="tpu_custom_call" | custom-call | flops 2415919104 | bytes 9437184 | tf_op jit(solution)/shard_map/pallas_call | solution.py:475
  27.5 0.0 slice-start.5
  27.5 0.2 collective-permute-start.10
  27.8 0.0 collective-permute-done.6.refs_1_
  27.8 4.2 %shard_map.137.z_ref = f32[256,1536]{1,0:T(8,128)S(1)} custom-call(s32[6]{0:T(128)S(1)} %stack.20.pos_ref.refs_0_, f32[512,384]{1,0:T(8,128)S(1)} %get-tuple-element.32.refs_0_, f32[512,384]{1,0:T(8,128)S(1)} %get-tuple-element.34.refs_1_, f32[512,384]{1,0:T(8,128)S(1)} %collective-permute-done.7.refs_2_, f32[512,384]{1,0:T(8,128)S(1)} %collective-permute-done.8.refs_3_, ...), custom_call_target="tpu_custom_call" | custom-call | flops 2415919104 | bytes 9437184 | tf_op jit(solution)/shard_map/pallas_call | solution.py:475
  31.9 0.4 collective-permute-start.9
  32.4 1.6 %collective-permute-start.15 = (bf16[256,256]{1,0:T(8,128)(2,1)S(1)}, bf16[256,256]{1,0:T(8,128)(2,1)S(1)}, u32[]{:S(2)}, u32[]{:S(2)}) collective-permute-start(bf16[256,256]{1,0:T(8,128)(2,1)S(1)} %shard_map.143), channel_id=1, source_target_pairs={{0,8},{8,0},{16,24},{24,16},{1,9},{9,1},{17,25},{25,17},{2,10},{10... | collective-permute-start | bytes 393224 | tf_op jit(solution)/shard_map/ppermute | solution.py:363
  34.0 0.0 collective-permute-done.10.other_ref
  34.0 1.0 %shard_map.138.first_ref = bf16[256,1024]{1,0:T(8,128)(2,1)S(1)} custom-call(f32[256,1536]{1,0:T(8,128)S(1)} %shard_map.136.z_ref, f32[256,1536]{1,0:T(8,128)S(1)} %collective-permute-done.10.other_ref, bf16[1536,1024]{1,0:T(8,128)(2,1)S(1)} %copy-done), custom_call_target="tpu_custom_call" | custom-call | flops 805306368 | bytes 3145728 | tf_op jit(solution)/shard_map/pallas_call | solution.py:494
  35.0 0.9 %shard_map.139.hot_ref = bf16[576,512]{1,0:T(8,128)(2,1)S(1)} custom-call(s32[6]{0:T(128)S(1)} %stack.20.pos_ref.refs_0_, bf16[160,384]{1,0:T(8,128)(2,1)S(1)} %get-tuple-element.35.refs_0_, bf16[160,384]{1,0:T(8,128)(2,1)S(1)} %collective-permute-done.refs_1_, bf16[160,384]{1,0:T(8,128)(2,1)S(1)} %collective-permute-done.1.refs_2_, ...), custom_call_target="tpu_custom_call" | custom-call | flops 100000000 | bytes 1000000 | tf_op jit(solution)/shard_map/pallas_call | solution.py:503
  35.9 0.0 copy-start.5
  35.9 0.0 copy-start.6
  35.9 0.0 collective-permute-done.9.other_ref
  35.9 3.1 %shard_map.140.a_ref = f32[64,256]{1,0:T(8,128)S(1)} custom-call(f32[256,1536]{1,0:T(8,128)S(1)} %shard_map.137.z_ref, f32[256,1536]{1,0:T(8,128)S(1)} %collective-permute-done.9.other_ref, bf16[256,1024]{1,0:T(8,128)(2,1)S(1)} %shard_map.138.first_ref, bf16[1536,1024]{1,0:T(8,128)(2,1)S(1)} %copy-done, bf16[9,1024,256]{2,1,0:T(8,128)(2,1)S(1)} %bitcast.18, ...), custom_call_target="tpu_custom_call" | custom-call | flops 2013265920 | bytes 6291456 | tf_op jit(solution)/shard_map/pallas_call | solution.py:512
  39.1 0.0 collective-permute-done.15.refs_2_
  39.1 0.1 collective-permute-start.16
  39.2 0.5 %collective-permute-start.11 = (f32[64,256]{1,0:T(8,128)S(1)}, f32[64,256]{1,0:T(8,128)S(1)}, u32[]{:S(2)}, u32[]{:S(2)}) collective-permute-start(f32[64,256]{1,0:T(8,128)S(1)} %shard_map.140.a_ref), channel_id=1, source_target_pairs={{0,1},{1,0},{2,3},{3,2},{4,5},{5,4},{6,7},{7,6},{8,9},{9,8},{10,11... | collective-permute-start | bytes 196616 | tf_op jit(solution)/shard_map/ppermute | solution.py:363
  39.7 0.0 copy-done.5
  39.7 1.0 %shard_map.142 = (bf16[64,256]{1,0:T(8,128)(2,1)S(1)}, f32[64,128]{1,0:T(8,128)S(1)}) custom-call(s32[6]{0:T(128)S(1)} %stack.20.pos_ref.refs_0_, bf16[160,384]{1,0:T(8,128)(2,1)S(1)} %get-tuple-element.35.refs_0_, bf16[160,384]{1,0:T(8,128)(2,1)S(1)} %collective-permute-done.refs_1_, bf16[160,384]{1,0:T(8,128)(2,1)S(1)} %collective-permute-done.1.refs_2_, ...), custom_call_target="tpu_custom_call" | custom-call | flops 100000000 | bytes 1000000 | tf_op jit(solution)/shard_map/pallas_call | solution.py:525
  40.7 0.1 collective-permute-done.11.b_ref
  40.8 1.0 %collective-permute-start.12 = (bf16[64,256]{1,0:T(8,128)(2,1)S(1)}, bf16[64,256]{1,0:T(8,128)(2,1)S(1)}, u32[]{:S(2)}, u32[]{:S(2)}) collective-permute-start(bf16[64,256]{1,0:T(8,128)(2,1)S(1)} %get-tuple-element.45), channel_id=1, source_target_pairs={{0,2},{2,0},{4,6},{6,4},{1,3},{3,1},{5,7},{7,5},{8,10},{10,8},{12,... | collective-permute-start | bytes 98312 | tf_op jit(solution)/shard_map/ppermute | solution.py:363
  41.8 1.0 %collective-permute-start.13 = (bf16[64,256]{1,0:T(8,128)(2,1)S(1)}, bf16[64,256]{1,0:T(8,128)(2,1)S(1)}, u32[]{:S(2)}, u32[]{:S(2)}) collective-permute-start(bf16[64,256]{1,0:T(8,128)(2,1)S(1)} %get-tuple-element.45), channel_id=1, source_target_pairs={{0,4},{2,6},{4,0},{6,2},{1,5},{3,7},{5,1},{7,3},{8,12},{10,14},{12... | collective-permute-start | bytes 98312 | tf_op jit(solution)/shard_map/ppermute | solution.py:363
  42.8 1.6 %collective-permute-start.14 = (bf16[64,256]{1,0:T(8,128)(2,1)S(1)}, bf16[64,256]{1,0:T(8,128)(2,1)S(1)}, u32[]{:S(2)}, u32[]{:S(2)}) collective-permute-start(bf16[64,256]{1,0:T(8,128)(2,1)S(1)} %get-tuple-element.45), channel_id=1, source_target_pairs={{0,6},{2,4},{4,2},{6,0},{1,7},{3,5},{5,3},{7,1},{8,14},{10,12},{12... | collective-permute-start | bytes 98312 | tf_op jit(solution)/shard_map/ppermute | solution.py:363
  44.4 0.0 collective-permute-done.16.refs_3_
  44.4 0.2 shard_map.145
  44.6 0.2 collective-permute-done.12.refs_2_
  44.8 0.9 %collective-permute-done.13.refs_3_ = bf16[64,256]{1,0:T(8,128)(2,1)S(1)} collective-permute-done((bf16[64,256]{1,0:T(8,128)(2,1)S(1)}, bf16[64,256]{1,0:T(8,128)(2,1)S(1)}, u32[]{:S(2)}, u32[]{:S(2)}) %collective-permute-start.13) | collective-permute-done | bytes 32800 | tf_op jit(solution)/shard_map/ppermute | solution.py:363
  45.7 1.9 %collective-permute-done.14.refs_4_ = bf16[64,256]{1,0:T(8,128)(2,1)S(1)} collective-permute-done((bf16[64,256]{1,0:T(8,128)(2,1)S(1)}, bf16[64,256]{1,0:T(8,128)(2,1)S(1)}, u32[]{:S(2)}, u32[]{:S(2)}) %collective-permute-start.14) | collective-permute-done | bytes 32800 | tf_op jit(solution)/shard_map/ppermute | solution.py:363
  47.6 1.8 %shard_map.146 = (f32[64,256]{1,0:T(8,128)}, f32[1,64]{1,0:T(1,128)}) custom-call(s32[6]{0:T(128)S(1)} %stack.20.pos_ref.refs_0_, f32[64,256]{1,0:T(8,128)S(1)} %get-tuple-element.44.refs_1_, bf16[64,256]{1,0:T(8,128)(2,1)S(1)} %collective-permute-done.12.refs_2_, bf16[64,256]{1,0:T(8,128)(2,1)S(1)} %collective-permute-done.13.refs_3_, ...), custom_call_target="tpu_custom_call" | custom-call | flops 100000000 | bytes 1000000 | tf_op jit(solution)/shard_map/pallas_call | solution.py:557
  (20 shorter events, 0.1 us)
Async XLA Ops:
  2.0 4.7 %copy-start.1 = (bf16[64,256]{1,0:T(8,128)(2,1)S(1)}, bf16[64,256]{1,0:T(8,128)(2,1)}, u32[]{:S(2)}) copy-start(bf16[64,256]{1,0:T(8,128)(2,1)} %key_ref.1) | copy-start | bytes 98308
  2.0 4.7 %copy-start.4 = (s32[4,4,32]{2,1,0:T(4,128)S(1)}, s32[4,4,32]{2,1,0:T(4,128)}, u32[]{:S(2)}) copy-start(s32[4,4,32]{2,1,0:T(4,128)} %ids_ref.1) | copy-start | bytes 6148
  2.0 10.9 %copy-start.7 = (bf16[7,7,1536]{2,1,0:T(8,128)(2,1)S(1)}, bf16[7,7,1536]{2,1,0:T(8,128)(2,1)}, u32[]{:S(2)}) copy-start(bf16[7,7,1536]{2,1,0:T(8,128)(2,1)} %refs_4_.4) | copy-start | bytes 451588
  2.0 8.8 %collective-permute-start.3 = (bf16[128,384]{1,0:T(8,128)(2,1)S(1)}, bf16[128,384]{1,0:T(8,128)(2,1)S(1)}, u32[]{:S(2)}, u32[]{:S(2)}) collective-permute-start(bf16[128,384]{1,0:T(8,128)(2,1)S(1)} %bitcast.27), channel_id=1, source_target_pairs={{0,2},{2,0},{4,6},{6,4},{1,3},{3,1},{5,7},{7,5},{8,10},{10,8},{12,... | collective-permute-start | bytes 294920 | tf_op jit(solution)/shard_map/ppermute | solution.py:363
  5.0 6.3 %collective-permute-start.4 = (bf16[128,384]{1,0:T(8,128)(2,1)S(1)}, bf16[128,384]{1,0:T(8,128)(2,1)S(1)}, u32[]{:S(2)}, u32[]{:S(2)}) collective-permute-start(bf16[128,384]{1,0:T(8,128)(2,1)S(1)} %bitcast.26), channel_id=1, source_target_pairs={{0,4},{2,6},{4,0},{6,2},{1,5},{3,7},{5,1},{7,3},{8,12},{10,14},{12... | collective-permute-start | bytes 294920 | tf_op jit(solution)/shard_map/ppermute | solution.py:363
  6.5 6.3 %collective-permute-start.5 = (bf16[128,384]{1,0:T(8,128)(2,1)S(1)}, bf16[128,384]{1,0:T(8,128)(2,1)S(1)}, u32[]{:S(2)}, u32[]{:S(2)}) collective-permute-start(bf16[128,384]{1,0:T(8,128)(2,1)S(1)} %bitcast.25), channel_id=1, source_target_pairs={{0,6},{2,4},{4,2},{6,0},{1,7},{3,5},{5,3},{7,1},{8,14},{10,12},{12... | collective-permute-start | bytes 294920 | tf_op jit(solution)/shard_map/ppermute | solution.py:363
  7.2 16.1 %slice-start.2 = ((s8[4718592]{0:T(1024)(128)(4,1)}), s8[524288]{0:T(1024)(128)(4,1)S(1)}, s32[]{:S(2)}) async-start(s8[4718592]{0:T(1024)(128)(4,1)} %bitcast.15), calls=%async_computation.2 | async-start | bytes 1048576
  7.3 9.2 %collective-permute-start = (bf16[160,384]{1,0:T(8,128)(2,1)S(1)}, bf16[160,384]{1,0:T(8,128)(2,1)S(1)}, u32[]{:S(2)}, u32[]{:S(2)}) collective-permute-start(bf16[160,384]{1,0:T(8,128)(2,1)S(1)} %get-tuple-element.63), channel_id=1, source_target_pairs={{0,2},{2,0},{4,6},{6,4},{1,3},{3,1},{5,7},{7,5},{8,10},{10,8},{12,... | collective-permute-start | bytes 368648 | tf_op jit(solution)/shard_map/ppermute | solution.py:363
  9.3 7.7 %collective-permute-start.1 = (bf16[160,384]{1,0:T(8,128)(2,1)S(1)}, bf16[160,384]{1,0:T(8,128)(2,1)S(1)}, u32[]{:S(2)}, u32[]{:S(2)}) collective-permute-start(bf16[160,384]{1,0:T(8,128)(2,1)S(1)} %get-tuple-element.64), channel_id=1, source_target_pairs={{0,4},{2,6},{4,0},{6,2},{1,5},{3,7},{5,1},{7,3},{8,12},{10,14},{12... | collective-permute-start | bytes 368648 | tf_op jit(solution)/shard_map/ppermute | solution.py:363
  10.8 12.5 %slice-start.3 = ((s8[4718592]{0:T(1024)(128)(4,1)}), s8[4194304]{0:T(1024)(128)(4,1)S(1)}, s32[]{:S(2)}) async-start(s8[4718592]{0:T(1024)(128)(4,1)} %bitcast.15), calls=%async_computation.3 | async-start | bytes 8388608
  10.8 6.2 %collective-permute-start.2 = (bf16[160,384]{1,0:T(8,128)(2,1)S(1)}, bf16[160,384]{1,0:T(8,128)(2,1)S(1)}, u32[]{:S(2)}, u32[]{:S(2)}) collective-permute-start(bf16[160,384]{1,0:T(8,128)(2,1)S(1)} %get-tuple-element.62), channel_id=1, source_target_pairs={{0,6},{2,4},{4,2},{6,0},{1,7},{3,5},{5,3},{7,1},{8,14},{10,12},{12... | collective-permute-start | bytes 368648 | tf_op jit(solution)/shard_map/ppermute | solution.py:363
  12.9 10.4 %slice-start = ((s8[4718592]{0:T(1024)(128)(4,1)}), s8[4194304]{0:T(1024)(128)(4,1)S(1)}, s32[]{:S(2)}) async-start(s8[4718592]{0:T(1024)(128)(4,1)} %bitcast.13), calls=%async_computation | async-start | bytes 8388608
  16.4 6.9 %collective-permute-start.7 = (f32[512,384]{1,0:T(8,128)S(1)}, f32[512,384]{1,0:T(8,128)S(1)}, u32[]{:S(2)}, u32[]{:S(2)}) collective-permute-start(f32[512,384]{1,0:T(8,128)S(1)} %get-tuple-element.32.refs_0_), channel_id=1, source_target_pairs={{0,1},{1,0},{2,3},{3,2},{4,5},{5,4},{6,7},{7,6},{8,9},{9,8},{10,11... | collective-permute-start | bytes 2359304 | tf_op jit(solution)/shard_map/ppermute | solution.py:363
  17.0 6.3 %slice-start.1 = ((s8[4718592]{0:T(1024)(128)(4,1)}), s8[524288]{0:T(1024)(128)(4,1)S(1)}, s32[]{:S(2)}) async-start(s8[4718592]{0:T(1024)(128)(4,1)} %bitcast.13), calls=%async_computation.1 | async-start | bytes 1048576
  17.0 6.3 %copy-start.2 = (bf16[1536]{0:T(1024)(128)(2,1)S(1)}, bf16[1536]{0:T(1024)(128)(2,1)}, u32[]{:S(2)}) copy-start(bf16[1536]{0:T(1024)(128)(2,1)} %refs_6_.3) | copy-start | bytes 9220
  17.0 6.3 %copy-start.3 = (bf16[1536]{0:T(1024)(128)(2,1)S(1)}, bf16[1536]{0:T(1024)(128)(2,1)}, u32[]{:S(2)}) copy-start(bf16[1536]{0:T(1024)(128)(2,1)} %refs_7_.3) | copy-start | bytes 9220
  20.5 2.8 %collective-permute-start.8 = (f32[512,384]{1,0:T(8,128)S(1)}, f32[512,384]{1,0:T(8,128)S(1)}, u32[]{:S(2)}, u32[]{:S(2)}) collective-permute-start(f32[512,384]{1,0:T(8,128)S(1)} %get-tuple-element.34.refs_1_), channel_id=1, source_target_pairs={{0,1},{1,0},{2,3},{3,2},{4,5},{5,4},{6,7},{7,6},{8,9},{9,8},{10,11... | collective-permute-start | bytes 2359304 | tf_op jit(solution)/shard_map/ppermute | solution.py:363
  20.6 7.1 %collective-permute-start.6 = (bf16[128,256]{1,0:T(8,128)(2,1)S(1)}, bf16[128,256]{1,0:T(8,128)(2,1)S(1)}, u32[]{:S(2)}, u32[]{:S(2)}) collective-permute-start(bf16[128,256]{1,0:T(8,128)(2,1)S(1)} %shard_map.135.refs_0_), channel_id=1, source_target_pairs={{0,16},{8,24},{16,0},{24,8},{1,17},{9,25},{17,1},{25,9},{2,18},{10... | collective-permute-start | bytes 196616 | tf_op jit(solution)/shard_map/ppermute | solution.py:363
  23.3 12.5 %slice-start.4 = ((s8[4718592]{0:T(1024)(128)(4,1)}), s8[4194304]{0:T(1024)(128)(4,1)S(1)}, s32[]{:S(2)}) async-start(s8[4718592]{0:T(1024)(128)(4,1)} %bitcast.17), calls=%async_computation.4 | async-start | bytes 8388608
  27.5 8.4 %slice-start.5 = ((s8[4718592]{0:T(1024)(128)(4,1)}), s8[524288]{0:T(1024)(128)(4,1)S(1)}, s32[]{:S(2)}) async-start(s8[4718592]{0:T(1024)(128)(4,1)} %bitcast.17), calls=%async_computation.5 | async-start | bytes 1048576
  27.5 6.5 %collective-permute-start.10 = (f32[256,1536]{1,0:T(8,128)S(1)}, f32[256,1536]{1,0:T(8,128)S(1)}, u32[]{:S(2)}, u32[]{:S(2)}) collective-permute-start(f32[256,1536]{1,0:T(8,128)S(1)} %shard_map.136.z_ref), channel_id=1, source_target_pairs={{0,1},{1,0},{2,3},{3,2},{4,5},{5,4},{6,7},{7,6},{8,9},{9,8},{10,11... | collective-permute-start | bytes 4718600 | tf_op jit(solution)/shard_map/ppermute | solution.py:363
  27.8 6.2 %copy-start = (bf16[1536,1024]{1,0:T(8,128)(2,1)S(1)}, bf16[1536,1024]{1,0:T(8,128)(2,1)}, u32[]{:S(2)}) copy-start(bf16[1536,1024]{1,0:T(8,128)(2,1)} %pe_ref.3) | copy-start | bytes 9437188
  31.9 4.0 %collective-permute-start.9 = (f32[256,1536]{1,0:T(8,128)S(1)}, f32[256,1536]{1,0:T(8,128)S(1)}, u32[]{:S(2)}, u32[]{:S(2)}) collective-permute-start(f32[256,1536]{1,0:T(8,128)S(1)} %shard_map.137.z_ref), channel_id=1, source_target_pairs={{0,1},{1,0},{2,3},{3,2},{4,5},{5,4},{6,7},{7,6},{8,9},{9,8},{10,11... | collective-permute-start | bytes 4718600 | tf_op jit(solution)/shard_map/ppermute | solution.py:363
  32.4 6.7 %collective-permute-start.15 = (bf16[256,256]{1,0:T(8,128)(2,1)S(1)}, bf16[256,256]{1,0:T(8,128)(2,1)S(1)}, u32[]{:S(2)}, u32[]{:S(2)}) collective-permute-start(bf16[256,256]{1,0:T(8,128)(2,1)S(1)} %shard_map.143), channel_id=1, source_target_pairs={{0,8},{8,0},{16,24},{24,16},{1,9},{9,1},{17,25},{25,17},{2,10},{10... | collective-permute-start | bytes 393224 | tf_op jit(solution)/shard_map/ppermute | solution.py:363
  35.9 3.8 %copy-start.5 = (s32[4,64]{1,0:T(4,128)S(1)}, s32[4,64]{1,0:T(4,128)}, u32[]{:S(2)}) copy-start(s32[4,64]{1,0:T(4,128)} %refs_5_.1) | copy-start | bytes 3076
  35.9 3.8 %copy-start.6 = (s32[1,256]{1,0:T(1,128)S(1)}, s32[1,256]{1,0:T(1,128)}, u32[]{:S(2)}) copy-start(s32[1,256]{1,0:T(1,128)} %refs_4_.5) | copy-start | bytes 3076
  39.1 5.3 %collective-permute-start.16 = (bf16[512,256]{1,0:T(8,128)(2,1)S(1)}, bf16[512,256]{1,0:T(8,128)(2,1)S(1)}, u32[]{:S(2)}, u32[]{:S(2)}) collective-permute-start(bf16[512,256]{1,0:T(8,128)(2,1)S(1)} %shard_map.144), channel_id=1, source_target_pairs={{0,1},{1,0},{2,3},{3,2},{4,5},{5,4},{6,7},{7,6},{8,9},{9,8},{10,11... | collective-permute-start | bytes 786440 | tf_op jit(solution)/shard_map/ppermute | solution.py:363
  39.2 1.6 %collective-permute-start.11 = (f32[64,256]{1,0:T(8,128)S(1)}, f32[64,256]{1,0:T(8,128)S(1)}, u32[]{:S(2)}, u32[]{:S(2)}) collective-permute-start(f32[64,256]{1,0:T(8,128)S(1)} %shard_map.140.a_ref), channel_id=1, source_target_pairs={{0,1},{1,0},{2,3},{3,2},{4,5},{5,4},{6,7},{7,6},{8,9},{9,8},{10,11... | collective-permute-start | bytes 196616 | tf_op jit(solution)/shard_map/ppermute | solution.py:363
  40.8 4.0 %collective-permute-start.12 = (bf16[64,256]{1,0:T(8,128)(2,1)S(1)}, bf16[64,256]{1,0:T(8,128)(2,1)S(1)}, u32[]{:S(2)}, u32[]{:S(2)}) collective-permute-start(bf16[64,256]{1,0:T(8,128)(2,1)S(1)} %get-tuple-element.45), channel_id=1, source_target_pairs={{0,2},{2,0},{4,6},{6,4},{1,3},{3,1},{5,7},{7,5},{8,10},{10,8},{12,... | collective-permute-start | bytes 98312 | tf_op jit(solution)/shard_map/ppermute | solution.py:363
  41.8 3.9 %collective-permute-start.13 = (bf16[64,256]{1,0:T(8,128)(2,1)S(1)}, bf16[64,256]{1,0:T(8,128)(2,1)S(1)}, u32[]{:S(2)}, u32[]{:S(2)}) collective-permute-start(bf16[64,256]{1,0:T(8,128)(2,1)S(1)} %get-tuple-element.45), channel_id=1, source_target_pairs={{0,4},{2,6},{4,0},{6,2},{1,5},{3,7},{5,1},{7,3},{8,12},{10,14},{12... | collective-permute-start | bytes 98312 | tf_op jit(solution)/shard_map/ppermute | solution.py:363
  42.8 4.8 %collective-permute-start.14 = (bf16[64,256]{1,0:T(8,128)(2,1)S(1)}, bf16[64,256]{1,0:T(8,128)(2,1)S(1)}, u32[]{:S(2)}, u32[]{:S(2)}) collective-permute-start(bf16[64,256]{1,0:T(8,128)(2,1)S(1)} %get-tuple-element.45), channel_id=1, source_target_pairs={{0,6},{2,4},{4,2},{6,0},{1,7},{3,5},{5,3},{7,1},{8,14},{10,12},{12... | collective-permute-start | bytes 98312 | tf_op jit(solution)/shard_map/ppermute | solution.py:363
where the time goes:
time: 49.5 us; the launch traced here: 49.4 us
  Pallas kernels  23.8 us (48%)
  starting transfers between devices  17.8 us (36%)
  waiting for transfers between devices  5.24 us (11%)
  local copies, waits for them, and re-layouts  1.48 us (3%)
  between operations  0.98 us (2%)
    ppermute x17, starting transfers between devices, swap(): lax.ppermute(x, axis, [(i, i ^ bit) for i in range(lax.axis_size(axis))])  17.8 us
    pallas_call x2, Pallas kernels, body(): call(functools.partial(block_kernel, (p * part_pixels, part_pixels, CHUNK...  8.31 us
    pallas_call x2, Pallas kernels, body(): call(functools.partial(conv_kernel, (order, shard_rows, width, out_rows,...  6.96 us
    ppermute x17, waiting for transfers between devices, swap(): lax.ppermute(x, axis, [(i, i ^ bit) for i in range(lax.axis_size(axis))])  5.24 us
    pallas_call x1, Pallas kernels, body(): call(project_kernel, [jax.ShapeDtypeStruct((REG, out_dim), f32)], [VMEM]...  3.14 us
    pallas_call x1, Pallas kernels, body(): call(functools.partial(loss_kernel, (shards, parts)), [jax.ShapeDtypeStru...  1.78 us
    dynamic_slice x1, local copies, waits for them, and re-layouts, body(): part = lax.dynamic_slice(features, place, (1, shard_rows, width, span))  1.32 us
  transfers between devices with their start and end apart: 17, of which 6 were waited for; matrix products, arithmetic and copies ran while one was open for 0% of the time, Pallas kernels for 45%

commit v1 on v0

--- a/solution.py
+++ b/solution.py
@@ -87,7 +87,7 @@
 
 
 def conv_kernel(geo, pos_ref, *refs):
-    order, shard_rows, width, out_rows, first_lane = geo
+    order, shard_rows, width, out_rows, first_lane, lane0 = geo
     shards = len(order)
     blocks = dict(zip(order, refs[:shards]))
     w_ref, taps, img_ref, xpad, wide = refs[shards:]
@@ -108,7 +108,7 @@
     def group(g, carry):
         lanes = pl.ds(pl.multiple_of(g * LANES, LANES), LANES)
         for k in range(shards):
-            value = blocks[k][0:pixels, lanes].astype(f32).reshape(shard_rows, width, LANES)
+            value = blocks[k][0:pixels, pl.ds(pl.multiple_of(lane0 + g * LANES, LANES), LANES)].astype(f32).reshape(shard_rows, width, LANES)
             xpad[pl.ds(3 + (row ^ k) * shard_rows, shard_rows), 8 : 8 + width, :] = value
         start = pos_ref[3] * (w_ref.shape[2] // 2) + first_lane + g * LANES
         for dy in range(7):
@@ -140,23 +140,25 @@
 
         @pl.when((start >= 0) & (start < out_pixels))
         def _():
-            img_ref[pl.ds(pl.multiple_of(start, pixels), pixels), :] = blocks[k][0:pixels, :]
+            img_ref[pl.ds(pl.multiple_of(start, pixels), pixels), :] = blocks[k][0:pixels, lane0 : lane0 + chunk]
 
 
 def block_kernel(geo, pos_ref, *refs):
-    first, pixels, chunks = geo
+    first, pixels, widths = geo
+    chunks = len(widths)
     own, other, img = refs[:chunks], refs[chunks : 2 * chunks], refs[2 * chunks : 3 * chunks]
     gain_ref, scale_ref, w1_ref, w2_ref, z_ref, normed, inner, wide = refs[3 * chunks :]
     chans, hid = w1_ref.shape
     half = chans // 2
-    width = half // chunks
+    starts = [sum(widths[:c]) for c in range(chunks)]
     section = pos_ref[3]
     rows = slice(first, first + pixels)
     gains = gain_ref[...].astype(f32).reshape(1, chans)
     scales = scale_ref[...].astype(f32).reshape(1, chans)
-    gains = [gains[:, n * width : (n + 1) * width] for n in range(2 * chunks)]
-    gains_own = [jnp.where(section == 0, gains[c], gains[chunks + c]) for c in range(chunks)]
-    gains_other = [jnp.where(section == 0, gains[chunks + c], gains[c]) for c in range(chunks)]
+    low = [gains[:, n : n + w] for n, w in zip(starts, widths)]
+    high = [gains[:, half + n : half + n + w] for n, w in zip(starts, widths)]
+    gains_own = [jnp.where(section == 0, x, y) for x, y in zip(low, high)]
+    gains_other = [jnp.where(section == 0, y, x) for x, y in zip(low, high)]
     block = 32
     for r in range(pixels // block):
         part = slice(first + r * block, first + (r + 1) * block)
@@ -169,8 +171,8 @@
         to = slice(r * block, (r + 1) * block)
         for c in range(chunks):
             for side, value in ((section, values[c]), (1 - section, values[chunks + c])):
-                start = pl.multiple_of(side * half + c * width, LANES)
-                normed[to, pl.ds(start, width)] = value
+                start = pl.multiple_of(side * half + starts[c], LANES)
+                normed[to, pl.ds(start, widths[c])] = value
     step = 256
 
     def widen(i):
@@ -182,21 +184,21 @@
         if i + 1 < hid // step:
             wide[(i + 1) % 2] = widen(i + 1)
         inner[:, i * step : (i + 1) * step] = gelu(wide[i % 2]).astype(bf16)
-    step = width if width % 256 else 256
-
-    def narrow(i):
-        return dot(inner[...], w2_ref[:, i * step : (i + 1) * step])
-
-    ahead = narrow(0)
+
+    def image(start):
+        found = []
+        for c in range(chunks):
+            low, high = max(start, starts[c]), min(start + step, starts[c] + widths[c])
+            if low < high:
+                found.append(img[c][rows, low - starts[c] : high - starts[c]])
+        return found[0] if len(found) == 1 else jnp.concatenate(found, axis=1)
+
     for i in range(chans // step):
-        z = ahead
-        if i + 1 < chans // step:
-            ahead = narrow(i + 1)
         cols = slice(i * step, (i + 1) * step)
         side, start = divmod(i * step, half)
-        c, start = divmod(start, width)
         keep = jnp.where(section == side, 1.0, 0.0)
-        z_ref[:, cols] = z * scales[:, cols] + img[c][rows, start : start + step].astype(f32) * keep
+        z = dot(inner[...], w2_ref[:, cols]) * scales[:, cols]
+        z_ref[:, cols] = z + image(start).astype(f32) * keep
 
 
 def expand_kernel(z_ref, other_ref, pe_ref, out_ref, block):
@@ -297,29 +299,24 @@
     own_ref[...] = jnp.where(side == 0, place, jnp.where(side == 1, number, 0.0))
 
 
-def project_kernel(z_ref, other_ref, first_ref, pe_ref, pk_ref, hot_ref, out_ref, block, hidden, sums):
+def project_kernel(z_ref, other_ref, first_ref, pe_ref, pk_ref, hot_ref, out_ref, block, hidden):
     before = first_ref.shape[0]
     pixels = z_ref.shape[0]
     taps = pk_ref.shape[0]
     block[...] = (z_ref[...] + other_ref[...]).astype(bf16)
     step = 256
     acc = jnp.zeros((2 * REG, out_ref.shape[1]), f32)
-    tiles = pe_ref.shape[1] // step
-
-    def collect(i):
+    for i in range(pe_ref.shape[1] // step):
         cols = slice(i * step, (i + 1) * step)
         hidden[i, 0:before, :] = first_ref[:, cols]
         h = jnp.maximum(dot(block[...], pe_ref[:, cols]), 0.0)
         hidden[i, before : before + pixels, :] = h.astype(bf16)
-        sums[i % 2] = dot(hot_ref[...], hidden[i])
-
-    collect(0)
-    for i in range(tiles):
-        if i + 1 < tiles:
-            collect(i + 1)
-        cols = slice(i * step, (i + 1) * step)
+        sums = dot(hot_ref[...], hidden[i])
+        hi = sums.astype(bf16)
+        lo = (sums - hi.astype(f32)).astype(bf16)
         for t in range(taps):
-            both = jnp.concatenate(split(sums[i % 2, t * REG : (t + 1) * REG, :]), axis=0)
+            rows = slice(t * REG, (t + 1) * REG)
+            both = jnp.concatenate([hi[rows], lo[rows]], axis=0)
             acc = acc + dot(both, pk_ref[t, cols, :])
     out_ref[...] = acc[0:REG] + acc[REG:]
 
@@ -433,14 +430,15 @@
     order = list(range(shards))
     last = [got[-1][k] for k in order]
 
+    cuts = [(c, 0, span) for c in range(CHUNKS)]
     own, other, img = [], [], []
-    for c in range(CHUNKS):
-        here = after(spot, *own) if c else spot
+    for c, lane0, wide in cuts:
+        here = after(spot, *own) if own else spot
         taps, image = call(
-            functools.partial(conv_kernel, (order, shard_rows, width, out_rows, c * span)),
+            functools.partial(conv_kernel, (order, shard_rows, width, out_rows, c * span + lane0, lane0)),
             [
-                jax.ShapeDtypeStruct((out_pixels, span), f32),
-                jax.ShapeDtypeStruct((out_pixels, span), bf16),
+                jax.ShapeDtypeStruct((out_pixels, wide), f32),
+                jax.ShapeDtypeStruct((out_pixels, wide), bf16),
             ],
             [SMEM] + [VMEM] * (shards + 1),
             [
@@ -448,8 +446,8 @@
                 pltpu.VMEM((49, 8, LANES), f32),
             ],
             3 * mib,
-            out_pixels * span * 98 * 100,
-            out_pixels * span * 10,
+            out_pixels * wide * 98 * 100,
+            out_pixels * wide * 10,
         )(here, *[got[c][k] for k in order], dw_kernel)
         own.append(taps)
         img.append(image)
@@ -473,9 +471,9 @@
     for p in range(2):
         here = after(spot, pieces[-1], *z) if p else after(spot, keys)
         (mine,) = call(
-            functools.partial(block_kernel, (p * part_pixels, part_pixels, CHUNKS)),
+            functools.partial(block_kernel, (p * part_pixels, part_pixels, [w for _, _, w in cuts])),
             [jax.ShapeDtypeStruct((part_pixels, chans), f32)],
-            [SMEM] + [VMEM] * (3 * CHUNKS + 4),
+            [SMEM] + [VMEM] * (3 * len(cuts) + 4),
             [
                 pltpu.VMEM((part_pixels, chans), bf16),
                 pltpu.VMEM((part_pixels, hid), bf16),
@@ -516,7 +514,6 @@
         [
             pltpu.VMEM((part_pixels, chans), bf16),
             pltpu.VMEM((hidden // 256, out_pixels, 256), bf16),
-            pltpu.VMEM((2, 9 * REG, 256), f32),
         ],
         8 * mib,
         2 * part_pixels * hidden * chans + 4 * 9 * REG * hidden * out_pixels,

time: 49.5 us -> 48.6 us (0.982)
  Pallas kernels: 23.8 us -> 22.9 us
    pallas_call x2, Pallas kernels: 8.31 us -> 7.61 us  [body(): call(functools.partial(block_kernel, (p * part_pixels, part_pixels, [w fo...]
  transfers between devices with their start and end apart: 17 -> 17, of which waited for: 6 -> 6; matrix products, arithmetic and copies ran while one was open for 0% -> 0% of each run, Pallas kernels for 45% -> 44%
where the time goes in v1:
time: 48.6 us; the launch traced here: 48.4 us
  Pallas kernels  22.9 us (47%)
  starting transfers between devices  17.8 us (37%)
  waiting for transfers between devices  5.25 us (11%)
  local copies, waits for them, and re-layouts  1.48 us (3%)
  between operations  0.98 us (2%)
    ppermute x17, starting transfers between devices, swap(): lax.ppermute(x, axis, [(i, i ^ bit) for i in range(lax.axis_size(axis))])  17.8 us
    pallas_call x2, Pallas kernels, body(): call(functools.partial(block_kernel, (p * part_pixels, part_pixels, [w fo...  7.61 us
    pallas_call x2, Pallas kernels, body(): call(functools.partial(conv_kernel, (order, shard_rows, width, out_rows,...  6.96 us
    ppermute x17, waiting for transfers between devices, swap(): lax.ppermute(x, axis, [(i, i ^ bit) for i in range(lax.axis_size(axis))])  5.25 us
    pallas_call x1, Pallas kernels, body(): call(project_kernel, [jax.ShapeDtypeStruct((REG, out_dim), f32)], [VMEM]...  2.86 us
    pallas_call x1, Pallas kernels, body(): call(functools.partial(loss_kernel, (shards, parts)), [jax.ShapeDtypeStru...  1.78 us
    dynamic_slice x1, local copies, waits for them, and re-layouts, body(): part = lax.dynamic_slice(features, place, (1, shard_rows, width, span))  1.32 us
    pallas_call x1, Pallas kernels, body(): call(expand_kernel, [jax.ShapeDtypeStruct((part_pixels, hidden), bf16)],...  0.98 us
  transfers between devices with their start and end apart: 17, of which 6 were waited for; matrix products, arithmetic and copies ran while one was open for 0% of the time, Pallas kernels for 44%

profile of v1, /device:TPU:0, one launch (start us, length us, event | category | flops | bytes accessed | tf_op | source)
XLA Modules:
  0.0 48.4 jit_solution(8277388312790435862)
XLA Ops:
  0.7 1.3 %constant_dynamic-slice_fusion = (bf16[1,4,32,384]{3,2,1,0:T(8,128)(2,1)S(1)}, bf16[1,4,32,384]{3,2,1,0:T(8,128)(2,1)S(1)}, bf16[1,4,32,384]{3,2,1,0:T(8,128)(2,...) fusion(bf16[4,4,32,1536]{3,2,1,0:T(8,128)(2,1)} %param.12, ...), kind=kLoop, calls=%fused_computation.4 | loop fusion | bytes 1572888 | tf_op jit(solution)/shard_map/dynamic_slice | solution.py:410
  2.0 0.0 copy-start.1
  2.0 0.0 copy-start.4
  2.0 0.0 copy-start.7
  2.0 3.0 %collective-permute-start.3 = (bf16[128,384]{1,0:T(8,128)(2,1)S(1)}, bf16[128,384]{1,0:T(8,128)(2,1)S(1)}, u32[]{:S(2)}, u32[]{:S(2)}) collective-permute-start(bf16[128,384]{1,0:T(8,128)(2,1)S(1)} %bitcast.27), channel_id=1, source_target_pairs={{0,2},{2,0},{4,6},{6,4},{1,3},{3,1},{5,7},{7,5},{8,10},{10,8},{12,... | collective-permute-start | bytes 294920 | tf_op jit(solution)/shard_map/ppermute | solution.py:360
  5.0 1.5 %collective-permute-start.4 = (bf16[128,384]{1,0:T(8,128)(2,1)S(1)}, bf16[128,384]{1,0:T(8,128)(2,1)S(1)}, u32[]{:S(2)}, u32[]{:S(2)}) collective-permute-start(bf16[128,384]{1,0:T(8,128)(2,1)S(1)} %bitcast.26), channel_id=1, source_target_pairs={{0,4},{2,6},{4,0},{6,2},{1,5},{3,7},{5,1},{7,3},{8,12},{10,14},{12... | collective-permute-start | bytes 294920 | tf_op jit(solution)/shard_map/ppermute | solution.py:360
  6.5 0.0 collective-permute-start.5
  6.6 0.1 stack.20.pos_ref.refs_0_
  6.6 0.0 copy-done.1
  6.7 0.0 copy-done.4
  6.7 0.6 %shard_map.132 = bf16[32,384]{1,0:T(8,128)(2,1)S(1)} custom-call(s32[6]{0:T(128)S(1)} %stack.20.pos_ref.refs_0_, s32[4,4,32]{2,1,0:T(4,128)S(1)} %copy-done.4, bf16[64,256]{1,0:T(8,128)(2,1)S(1)} %copy-done.1, f32[32,128]{1,0:T(8,128)S(1)} %shard_map.131.blank_ref), custom_call_target="tpu_custom_call" | custom-call | bytes 1000000 | tf_op jit(solution)/shard_map/pallas_call | solution.py:417
  7.2 0.0 slice-start.2
  7.2 0.1 pad_maximum_fusion
  7.3 2.0 %collective-permute-start = (bf16[160,384]{1,0:T(8,128)(2,1)S(1)}, bf16[160,384]{1,0:T(8,128)(2,1)S(1)}, u32[]{:S(2)}, u32[]{:S(2)}) collective-permute-start(bf16[160,384]{1,0:T(8,128)(2,1)S(1)} %get-tuple-element.63), channel_id=1, source_target_pairs={{0,2},{2,0},{4,6},{6,4},{1,3},{3,1},{5,7},{7,5},{8,10},{10,8},{12,... | collective-permute-start | bytes 368648 | tf_op jit(solution)/shard_map/ppermute | solution.py:360
  9.3 1.5 %collective-permute-start.1 = (bf16[160,384]{1,0:T(8,128)(2,1)S(1)}, bf16[160,384]{1,0:T(8,128)(2,1)S(1)}, u32[]{:S(2)}, u32[]{:S(2)}) collective-permute-start(bf16[160,384]{1,0:T(8,128)(2,1)S(1)} %get-tuple-element.64), channel_id=1, source_target_pairs={{0,4},{2,6},{4,0},{6,2},{1,5},{3,7},{5,1},{7,3},{8,12},{10,14},{12... | collective-permute-start | bytes 368648 | tf_op jit(solution)/shard_map/ppermute | solution.py:360
  10.8 0.0 collective-permute-done.3.refs_1_
  10.8 0.5 %collective-permute-start.2 = (bf16[160,384]{1,0:T(8,128)(2,1)S(1)}, bf16[160,384]{1,0:T(8,128)(2,1)S(1)}, u32[]{:S(2)}, u32[]{:S(2)}) collective-permute-start(bf16[160,384]{1,0:T(8,128)(2,1)S(1)} %get-tuple-element.62), channel_id=1, source_target_pairs={{0,6},{2,4},{4,2},{6,0},{1,7},{3,5},{5,3},{7,1},{8,14},{10,12},{12... | collective-permute-start | bytes 368648 | tf_op jit(solution)/shard_map/ppermute | solution.py:360
  11.3 0.0 collective-permute-done.4.refs_2_
  11.3 1.5 %collective-permute-done.5.refs_3_ = bf16[128,384]{1,0:T(8,128)(2,1)S(1)} collective-permute-done((bf16[128,384]{1,0:T(8,128)(2,1)S(1)}, bf16[128,384]{1,0:T(8,128)(2,1)S(1)}, u32[]{:S(2)}, u32[]{:S(2)}) %collective-permute-start.5) | collective-permute-done | bytes 98336 | tf_op jit(solution)/shard_map/ppermute | solution.py:360
  12.9 3.5 %shard_map.133 = (f32[512,384]{1,0:T(8,128)S(1)}, bf16[512,384]{1,0:T(8,128)(2,1)S(1)}) custom-call(s32[6]{0:T(128)S(1)} %stack.20.pos_ref.refs_0_, bf16[128,384]{1,0:T(8,128)(2,1)S(1)} %bitcast.20, bf16[128,384]{1,0:T(8,128)(2,1)S(1)} %collective-permute-done.3.refs_1_, bf16[128,384]{1,0:T(8,128)(2,1)S(1)} %collective-permute-done.4.refs_2_, ...), custom_call_target="tpu_custom_call" | custom-call | flops 1926758400 | bytes 1966080 | tf_op jit(solution)/shard_map/pallas_call | solution.py:437
  16.4 0.1 collective-permute-start.7
  16.4 0.0 collective-permute-done.refs_1_
  16.5 0.6 %collective-permute-done.1.refs_2_ = bf16[160,384]{1,0:T(8,128)(2,1)S(1)} collective-permute-done((bf16[160,384]{1,0:T(8,128)(2,1)S(1)}, bf16[160,384]{1,0:T(8,128)(2,1)S(1)}, u32[]{:S(2)}, u32[]{:S(2)}) %collective-permute-start.1) | collective-permute-done | bytes 122912 | tf_op jit(solution)/shard_map/ppermute | solution.py:360
  17.0 0.0 collective-permute-done.2.refs_3_
  17.0 3.5 %shard_map.134 = (f32[512,384]{1,0:T(8,128)S(1)}, bf16[512,384]{1,0:T(8,128)(2,1)S(1)}) custom-call(s32[6]{0:T(128)S(1)} %stack.20.pos_ref.refs_0_, bf16[160,384]{1,0:T(8,128)(2,1)S(1)} %get-tuple-element.35.refs_0_, bf16[160,384]{1,0:T(8,128)(2,1)S(1)} %collective-permute-done.refs_1_, bf16[160,384]{1,0:T(8,128)(2,1)S(1)} %collective-permute-done.1.refs_2_, ...), custom_call_target="tpu_custom_call" | custom-call | flops 1926758400 | bytes 1966080 | tf_op jit(solution)/shard_map/pallas_call | solution.py:437
  20.5 0.1 collective-permute-start.8
  20.6 2.7 %collective-permute-start.6 = (bf16[128,256]{1,0:T(8,128)(2,1)S(1)}, bf16[128,256]{1,0:T(8,128)(2,1)S(1)}, u32[]{:S(2)}, u32[]{:S(2)}) collective-permute-start(bf16[128,256]{1,0:T(8,128)(2,1)S(1)} %shard_map.135.refs_0_), channel_id=1, source_target_pairs={{0,16},{8,24},{16,0},{24,8},{1,17},{9,25},{17,1},{25,9},{2,18},{10... | collective-permute-start | bytes 196616 | tf_op jit(solution)/shard_map/ppermute | solution.py:360
  23.3 0.0 collective-permute-done.7.refs_2_
  23.3 0.0 collective-permute-done.8.refs_3_
  23.3 0.0 slice-done.2
  23.3 0.0 slice-done.3
  23.3 0.0 slice-done
  23.3 0.0 slice-done.1
  23.3 0.0 copy-done.2
  23.3 0.0 copy-done.3
  23.3 0.0 slice-start.4
  23.4 3.8 %shard_map.136.z_ref = f32[256,1536]{1,0:T(8,128)S(1)} custom-call(s32[6]{0:T(128)S(1)} %stack.20.pos_ref.refs_0_, f32[512,384]{1,0:T(8,128)S(1)} %get-tuple-element.32.refs_0_, f32[512,384]{1,0:T(8,128)S(1)} %get-tuple-element.34.refs_1_, f32[512,384]{1,0:T(8,128)S(1)} %collective-permute-done.7.refs_2_, f32[512,384]{1,0:T(8,128)S(1)} %collective-permute-done.8.refs_3_, ...), custom_call_target="tpu_custom_call" | custom-call | flops 2415919104 | bytes 9437184 | tf_op jit(solution)/shard_map/pallas_call | solution.py:473
  27.2 0.0 slice-start.5
  27.2 0.2 collective-permute-start.10
  27.4 0.0 collective-permute-done.6.refs_1_
  27.4 3.8 %shard_map.137.z_ref = f32[256,1536]{1,0:T(8,128)S(1)} custom-call(s32[6]{0:T(128)S(1)} %stack.20.pos_ref.refs_0_, f32[512,384]{1,0:T(8,128)S(1)} %get-tuple-element.32.refs_0_, f32[512,384]{1,0:T(8,128)S(1)} %get-tuple-element.34.refs_1_, f32[512,384]{1,0:T(8,128)S(1)} %collective-permute-done.7.refs_2_, f32[512,384]{1,0:T(8,128)S(1)} %collective-permute-done.8.refs_3_, ...), custom_call_target="tpu_custom_call" | custom-call | flops 2415919104 | bytes 9437184 | tf_op jit(solution)/shard_map/pallas_call | solution.py:473
  31.2 0.4 collective-permute-start.9
  31.7 1.6 %collective-permute-start.15 = (bf16[256,256]{1,0:T(8,128)(2,1)S(1)}, bf16[256,256]{1,0:T(8,128)(2,1)S(1)}, u32[]{:S(2)}, u32[]{:S(2)}) collective-permute-start(bf16[256,256]{1,0:T(8,128)(2,1)S(1)} %shard_map.143), channel_id=1, source_target_pairs={{0,8},{8,0},{16,24},{24,16},{1,9},{9,1},{17,25},{25,17},{2,10},{10... | collective-permute-start | bytes 393224 | tf_op jit(solution)/shard_map/ppermute | solution.py:360
  33.3 0.0 collective-permute-done.10.other_ref
  33.3 1.0 %shard_map.138.first_ref = bf16[256,1024]{1,0:T(8,128)(2,1)S(1)} custom-call(f32[256,1536]{1,0:T(8,128)S(1)} %shard_map.136.z_ref, f32[256,1536]{1,0:T(8,128)S(1)} %collective-permute-done.10.other_ref, bf16[1536,1024]{1,0:T(8,128)(2,1)S(1)} %copy-done), custom_call_target="tpu_custom_call" | custom-call | flops 805306368 | bytes 3145728 | tf_op jit(solution)/shard_map/pallas_call | solution.py:492
  34.3 0.9 %shard_map.139.hot_ref = bf16[576,512]{1,0:T(8,128)(2,1)S(1)} custom-call(s32[6]{0:T(128)S(1)} %stack.20.pos_ref.refs_0_, bf16[160,384]{1,0:T(8,128)(2,1)S(1)} %get-tuple-element.35.refs_0_, bf16[160,384]{1,0:T(8,128)(2,1)S(1)} %collective-permute-done.refs_1_, bf16[160,384]{1,0:T(8,128)(2,1)S(1)} %collective-permute-done.1.refs_2_, ...), custom_call_target="tpu_custom_call" | custom-call | flops 100000000 | bytes 1000000 | tf_op jit(solution)/shard_map/pallas_call | solution.py:501
  35.2 0.0 copy-start.5
  35.2 0.0 copy-start.6
  35.2 0.0 collective-permute-done.9.other_ref
  35.2 2.9 %shard_map.140.a_ref = f32[64,256]{1,0:T(8,128)S(1)} custom-call(f32[256,1536]{1,0:T(8,128)S(1)} %shard_map.137.z_ref, f32[256,1536]{1,0:T(8,128)S(1)} %collective-permute-done.9.other_ref, bf16[256,1024]{1,0:T(8,128)(2,1)S(1)} %shard_map.138.first_ref, bf16[1536,1024]{1,0:T(8,128)(2,1)S(1)} %copy-done, bf16[9,1024,256]{2,1,0:T(8,128)(2,1)S(1)} %bitcast.18, ...), custom_call_target="tpu_custom_call" | custom-call | flops 2013265920 | bytes 6291456 | tf_op jit(solution)/shard_map/pallas_call | solution.py:510
  38.1 0.0 collective-permute-done.15.refs_2_
  38.1 0.1 collective-permute-start.16
  38.2 0.5 %collective-permute-start.11 = (f32[64,256]{1,0:T(8,128)S(1)}, f32[64,256]{1,0:T(8,128)S(1)}, u32[]{:S(2)}, u32[]{:S(2)}) collective-permute-start(f32[64,256]{1,0:T(8,128)S(1)} %shard_map.140.a_ref), channel_id=1, source_target_pairs={{0,1},{1,0},{2,3},{3,2},{4,5},{5,4},{6,7},{7,6},{8,9},{9,8},{10,11... | collective-permute-start | bytes 196616 | tf_op jit(solution)/shard_map/ppermute | solution.py:360
  38.7 1.0 %shard_map.142 = (bf16[64,256]{1,0:T(8,128)(2,1)S(1)}, f32[64,128]{1,0:T(8,128)S(1)}) custom-call(s32[6]{0:T(128)S(1)} %stack.20.pos_ref.refs_0_, bf16[160,384]{1,0:T(8,128)(2,1)S(1)} %get-tuple-element.35.refs_0_, bf16[160,384]{1,0:T(8,128)(2,1)S(1)} %collective-permute-done.refs_1_, bf16[160,384]{1,0:T(8,128)(2,1)S(1)} %collective-permute-done.1.refs_2_, ...), custom_call_target="tpu_custom_call" | custom-call | flops 100000000 | bytes 1000000 | tf_op jit(solution)/shard_map/pallas_call | solution.py:522
  39.7 0.1 collective-permute-done.11.b_ref
  39.8 1.0 %collective-permute-start.12 = (bf16[64,256]{1,0:T(8,128)(2,1)S(1)}, bf16[64,256]{1,0:T(8,128)(2,1)S(1)}, u32[]{:S(2)}, u32[]{:S(2)}) collective-permute-start(bf16[64,256]{1,0:T(8,128)(2,1)S(1)} %get-tuple-element.45), channel_id=1, source_target_pairs={{0,2},{2,0},{4,6},{6,4},{1,3},{3,1},{5,7},{7,5},{8,10},{10,8},{12,... | collective-permute-start | bytes 98312 | tf_op jit(solution)/shard_map/ppermute | solution.py:360
  40.9 1.0 %collective-permute-start.13 = (bf16[64,256]{1,0:T(8,128)(2,1)S(1)}, bf16[64,256]{1,0:T(8,128)(2,1)S(1)}, u32[]{:S(2)}, u32[]{:S(2)}) collective-permute-start(bf16[64,256]{1,0:T(8,128)(2,1)S(1)} %get-tuple-element.45), channel_id=1, source_target_pairs={{0,4},{2,6},{4,0},{6,2},{1,5},{3,7},{5,1},{7,3},{8,12},{10,14},{12... | collective-permute-start | bytes 98312 | tf_op jit(solution)/shard_map/ppermute | solution.py:360
  41.8 1.6 %collective-permute-start.14 = (bf16[64,256]{1,0:T(8,128)(2,1)S(1)}, bf16[64,256]{1,0:T(8,128)(2,1)S(1)}, u32[]{:S(2)}, u32[]{:S(2)}) collective-permute-start(bf16[64,256]{1,0:T(8,128)(2,1)S(1)} %get-tuple-element.45), channel_id=1, source_target_pairs={{0,6},{2,4},{4,2},{6,0},{1,7},{3,5},{5,3},{7,1},{8,14},{10,12},{12... | collective-permute-start | bytes 98312 | tf_op jit(solution)/shard_map/ppermute | solution.py:360
  43.4 0.0 collective-permute-done.16.refs_3_
  43.4 0.2 shard_map.145
  43.6 0.2 collective-permute-done.12.refs_2_
  43.8 0.9 %collective-permute-done.13.refs_3_ = bf16[64,256]{1,0:T(8,128)(2,1)S(1)} collective-permute-done((bf16[64,256]{1,0:T(8,128)(2,1)S(1)}, bf16[64,256]{1,0:T(8,128)(2,1)S(1)}, u32[]{:S(2)}, u32[]{:S(2)}) %collective-permute-start.13) | collective-permute-done | bytes 32800 | tf_op jit(solution)/shard_map/ppermute | solution.py:360
  44.8 1.9 %collective-permute-done.14.refs_4_ = bf16[64,256]{1,0:T(8,128)(2,1)S(1)} collective-permute-done((bf16[64,256]{1,0:T(8,128)(2,1)S(1)}, bf16[64,256]{1,0:T(8,128)(2,1)S(1)}, u32[]{:S(2)}, u32[]{:S(2)}) %collective-permute-start.14) | collective-permute-done | bytes 32800 | tf_op jit(solution)/shard_map/ppermute | solution.py:360
  46.6 1.8 %shard_map.146 = (f32[64,256]{1,0:T(8,128)}, f32[1,64]{1,0:T(1,128)}) custom-call(s32[6]{0:T(128)S(1)} %stack.20.pos_ref.refs_0_, f32[64,256]{1,0:T(8,128)S(1)} %get-tuple-element.44.refs_1_, bf16[64,256]{1,0:T(8,128)(2,1)S(1)} %collective-permute-done.12.refs_2_, bf16[64,256]{1,0:T(8,128)(2,1)S(1)} %collective-permute-done.13.refs_3_, ...), custom_call_target="tpu_custom_call" | custom-call | flops 100000000 | bytes 1000000 | tf_op jit(solution)/shard_map/pallas_call | solution.py:554
  (20 shorter events, 0.1 us)
Async XLA Ops:
  2.0 4.7 %copy-start.1 = (bf16[64,256]{1,0:T(8,128)(2,1)S(1)}, bf16[64,256]{1,0:T(8,128)(2,1)}, u32[]{:S(2)}) copy-start(bf16[64,256]{1,0:T(8,128)(2,1)} %key_ref.1) | copy-start | bytes 98308
  2.0 4.7 %copy-start.4 = (s32[4,4,32]{2,1,0:T(4,128)S(1)}, s32[4,4,32]{2,1,0:T(4,128)}, u32[]{:S(2)}) copy-start(s32[4,4,32]{2,1,0:T(4,128)} %ids_ref.1) | copy-start | bytes 6148
  2.0 10.9 %copy-start.7 = (bf16[7,7,1536]{2,1,0:T(8,128)(2,1)S(1)}, bf16[7,7,1536]{2,1,0:T(8,128)(2,1)}, u32[]{:S(2)}) copy-start(bf16[7,7,1536]{2,1,0:T(8,128)(2,1)} %refs_4_.4) | copy-start | bytes 451588
  2.0 8.8 %collective-permute-start.3 = (bf16[128,384]{1,0:T(8,128)(2,1)S(1)}, bf16[128,384]{1,0:T(8,128)(2,1)S(1)}, u32[]{:S(2)}, u32[]{:S(2)}) collective-permute-start(bf16[128,384]{1,0:T(8,128)(2,1)S(1)} %bitcast.27), channel_id=1, source_target_pairs={{0,2},{2,0},{4,6},{6,4},{1,3},{3,1},{5,7},{7,5},{8,10},{10,8},{12,... | collective-permute-start | bytes 294920 | tf_op jit(solution)/shard_map/ppermute | solution.py:360
  5.0 6.3 %collective-permute-start.4 = (bf16[128,384]{1,0:T(8,128)(2,1)S(1)}, bf16[128,384]{1,0:T(8,128)(2,1)S(1)}, u32[]{:S(2)}, u32[]{:S(2)}) collective-permute-start(bf16[128,384]{1,0:T(8,128)(2,1)S(1)} %bitcast.26), channel_id=1, source_target_pairs={{0,4},{2,6},{4,0},{6,2},{1,5},{3,7},{5,1},{7,3},{8,12},{10,14},{12... | collective-permute-start | bytes 294920 | tf_op jit(solution)/shard_map/ppermute | solution.py:360
  6.5 6.3 %collective-permute-start.5 = (bf16[128,384]{1,0:T(8,128)(2,1)S(1)}, bf16[128,384]{1,0:T(8,128)(2,1)S(1)}, u32[]{:S(2)}, u32[]{:S(2)}) collective-permute-start(bf16[128,384]{1,0:T(8,128)(2,1)S(1)} %bitcast.25), channel_id=1, source_target_pairs={{0,6},{2,4},{4,2},{6,0},{1,7},{3,5},{5,3},{7,1},{8,14},{10,12},{12... | collective-permute-start | bytes 294920 | tf_op jit(solution)/shard_map/ppermute | solution.py:360
  7.2 16.1 %slice-start.2 = ((s8[4718592]{0:T(1024)(128)(4,1)}), s8[524288]{0:T(1024)(128)(4,1)S(1)}, s32[]{:S(2)}) async-start(s8[4718592]{0:T(1024)(128)(4,1)} %bitcast.15), calls=%async_computation.2 | async-start | bytes 1048576
  7.3 9.2 %collective-permute-start = (bf16[160,384]{1,0:T(8,128)(2,1)S(1)}, bf16[160,384]{1,0:T(8,128)(2,1)S(1)}, u32[]{:S(2)}, u32[]{:S(2)}) collective-permute-start(bf16[160,384]{1,0:T(8,128)(2,1)S(1)} %get-tuple-element.63), channel_id=1, source_target_pairs={{0,2},{2,0},{4,6},{6,4},{1,3},{3,1},{5,7},{7,5},{8,10},{10,8},{12,... | collective-permute-start | bytes 368648 | tf_op jit(solution)/shard_map/ppermute | solution.py:360
  9.3 7.7 %collective-permute-start.1 = (bf16[160,384]{1,0:T(8,128)(2,1)S(1)}, bf16[160,384]{1,0:T(8,128)(2,1)S(1)}, u32[]{:S(2)}, u32[]{:S(2)}) collective-permute-start(bf16[160,384]{1,0:T(8,128)(2,1)S(1)} %get-tuple-element.64), channel_id=1, source_target_pairs={{0,4},{2,6},{4,0},{6,2},{1,5},{3,7},{5,1},{7,3},{8,12},{10,14},{12... | collective-permute-start | bytes 368648 | tf_op jit(solution)/shard_map/ppermute | solution.py:360
  10.8 12.5 %slice-start.3 = ((s8[4718592]{0:T(1024)(128)(4,1)}), s8[4194304]{0:T(1024)(128)(4,1)S(1)}, s32[]{:S(2)}) async-start(s8[4718592]{0:T(1024)(128)(4,1)} %bitcast.15), calls=%async_computation.3 | async-start | bytes 8388608
  10.8 6.2 %collective-permute-start.2 = (bf16[160,384]{1,0:T(8,128)(2,1)S(1)}, bf16[160,384]{1,0:T(8,128)(2,1)S(1)}, u32[]{:S(2)}, u32[]{:S(2)}) collective-permute-start(bf16[160,384]{1,0:T(8,128)(2,1)S(1)} %get-tuple-element.62), channel_id=1, source_target_pairs={{0,6},{2,4},{4,2},{6,0},{1,7},{3,5},{5,3},{7,1},{8,14},{10,12},{12... | collective-permute-start | bytes 368648 | tf_op jit(solution)/shard_map/ppermute | solution.py:360
  12.9 10.4 %slice-start = ((s8[4718592]{0:T(1024)(128)(4,1)}), s8[4194304]{0:T(1024)(128)(4,1)S(1)}, s32[]{:S(2)}) async-start(s8[4718592]{0:T(1024)(128)(4,1)} %bitcast.13), calls=%async_computation | async-start | bytes 8388608
  16.4 6.9 %collective-permute-start.7 = (f32[512,384]{1,0:T(8,128)S(1)}, f32[512,384]{1,0:T(8,128)S(1)}, u32[]{:S(2)}, u32[]{:S(2)}) collective-permute-start(f32[512,384]{1,0:T(8,128)S(1)} %get-tuple-element.32.refs_0_), channel_id=1, source_target_pairs={{0,1},{1,0},{2,3},{3,2},{4,5},{5,4},{6,7},{7,6},{8,9},{9,8},{10,11... | collective-permute-start | bytes 2359304 | tf_op jit(solution)/shard_map/ppermute | solution.py:360
  17.0 6.3 %slice-start.1 = ((s8[4718592]{0:T(1024)(128)(4,1)}), s8[524288]{0:T(1024)(128)(4,1)S(1)}, s32[]{:S(2)}) async-start(s8[4718592]{0:T(1024)(128)(4,1)} %bitcast.13), calls=%async_computation.1 | async-start | bytes 1048576
  17.0 6.3 %copy-start.2 = (bf16[1536]{0:T(1024)(128)(2,1)S(1)}, bf16[1536]{0:T(1024)(128)(2,1)}, u32[]{:S(2)}) copy-start(bf16[1536]{0:T(1024)(128)(2,1)} %refs_6_.3) | copy-start | bytes 9220
  17.0 6.3 %copy-start.3 = (bf16[1536]{0:T(1024)(128)(2,1)S(1)}, bf16[1536]{0:T(1024)(128)(2,1)}, u32[]{:S(2)}) copy-start(bf16[1536]{0:T(1024)(128)(2,1)} %refs_7_.3) | copy-start | bytes 9220
  20.5 2.8 %collective-permute-start.8 = (f32[512,384]{1,0:T(8,128)S(1)}, f32[512,384]{1,0:T(8,128)S(1)}, u32[]{:S(2)}, u32[]{:S(2)}) collective-permute-start(f32[512,384]{1,0:T(8,128)S(1)} %get-tuple-element.34.refs_1_), channel_id=1, source_target_pairs={{0,1},{1,0},{2,3},{3,2},{4,5},{5,4},{6,7},{7,6},{8,9},{9,8},{10,11... | collective-permute-start | bytes 2359304 | tf_op jit(solution)/shard_map/ppermute | solution.py:360
  20.6 6.8 %collective-permute-start.6 = (bf16[128,256]{1,0:T(8,128)(2,1)S(1)}, bf16[128,256]{1,0:T(8,128)(2,1)S(1)}, u32[]{:S(2)}, u32[]{:S(2)}) collective-permute-start(bf16[128,256]{1,0:T(8,128)(2,1)S(1)} %shard_map.135.refs_0_), channel_id=1, source_target_pairs={{0,16},{8,24},{16,0},{24,8},{1,17},{9,25},{17,1},{25,9},{2,18},{10... | collective-permute-start | bytes 196616 | tf_op jit(solution)/shard_map/ppermute | solution.py:360
  23.3 11.9 %slice-start.4 = ((s8[4718592]{0:T(1024)(128)(4,1)}), s8[4194304]{0:T(1024)(128)(4,1)S(1)}, s32[]{:S(2)}) async-start(s8[4718592]{0:T(1024)(128)(4,1)} %bitcast.17), calls=%async_computation.4 | async-start | bytes 8388608
  27.2 8.0 %slice-start.5 = ((s8[4718592]{0:T(1024)(128)(4,1)}), s8[524288]{0:T(1024)(128)(4,1)S(1)}, s32[]{:S(2)}) async-start(s8[4718592]{0:T(1024)(128)(4,1)} %bitcast.17), calls=%async_computation.5 | async-start | bytes 1048576
  27.2 6.1 %collective-permute-start.10 = (f32[256,1536]{1,0:T(8,128)S(1)}, f32[256,1536]{1,0:T(8,128)S(1)}, u32[]{:S(2)}, u32[]{:S(2)}) collective-permute-start(f32[256,1536]{1,0:T(8,128)S(1)} %shard_map.136.z_ref), channel_id=1, source_target_pairs={{0,1},{1,0},{2,3},{3,2},{4,5},{5,4},{6,7},{7,6},{8,9},{9,8},{10,11... | collective-permute-start | bytes 4718600 | tf_op jit(solution)/shard_map/ppermute | solution.py:360
  27.4 5.9 %copy-start = (bf16[1536,1024]{1,0:T(8,128)(2,1)S(1)}, bf16[1536,1024]{1,0:T(8,128)(2,1)}, u32[]{:S(2)}) copy-start(bf16[1536,1024]{1,0:T(8,128)(2,1)} %pe_ref.3) | copy-start | bytes 9437188
  31.2 4.0 %collective-permute-start.9 = (f32[256,1536]{1,0:T(8,128)S(1)}, f32[256,1536]{1,0:T(8,128)S(1)}, u32[]{:S(2)}, u32[]{:S(2)}) collective-permute-start(f32[256,1536]{1,0:T(8,128)S(1)} %shard_map.137.z_ref), channel_id=1, source_target_pairs={{0,1},{1,0},{2,3},{3,2},{4,5},{5,4},{6,7},{7,6},{8,9},{9,8},{10,11... | collective-permute-start | bytes 4718600 | tf_op jit(solution)/shard_map/ppermute | solution.py:360
  31.7 6.4 %collective-permute-start.15 = (bf16[256,256]{1,0:T(8,128)(2,1)S(1)}, bf16[256,256]{1,0:T(8,128)(2,1)S(1)}, u32[]{:S(2)}, u32[]{:S(2)}) collective-permute-start(bf16[256,256]{1,0:T(8,128)(2,1)S(1)} %shard_map.143), channel_id=1, source_target_pairs={{0,8},{8,0},{16,24},{24,16},{1,9},{9,1},{17,25},{25,17},{2,10},{10... | collective-permute-start | bytes 393224 | tf_op jit(solution)/shard_map/ppermute | solution.py:360
  35.2 3.5 %copy-start.5 = (s32[4,64]{1,0:T(4,128)S(1)}, s32[4,64]{1,0:T(4,128)}, u32[]{:S(2)}) copy-start(s32[4,64]{1,0:T(4,128)} %refs_5_.1) | copy-start | bytes 3076
  35.2 3.5 %copy-start.6 = (s32[1,256]{1,0:T(1,128)S(1)}, s32[1,256]{1,0:T(1,128)}, u32[]{:S(2)}) copy-start(s32[1,256]{1,0:T(1,128)} %refs_4_.5) | copy-start | bytes 3076
  38.1 5.3 %collective-permute-start.16 = (bf16[512,256]{1,0:T(8,128)(2,1)S(1)}, bf16[512,256]{1,0:T(8,128)(2,1)S(1)}, u32[]{:S(2)}, u32[]{:S(2)}) collective-permute-start(bf16[512,256]{1,0:T(8,128)(2,1)S(1)} %shard_map.144), channel_id=1, source_target_pairs={{0,1},{1,0},{2,3},{3,2},{4,5},{5,4},{6,7},{7,6},{8,9},{9,8},{10,11... | collective-permute-start | bytes 786440 | tf_op jit(solution)/shard_map/ppermute | solution.py:360
  38.2 1.6 %collective-permute-start.11 = (f32[64,256]{1,0:T(8,128)S(1)}, f32[64,256]{1,0:T(8,128)S(1)}, u32[]{:S(2)}, u32[]{:S(2)}) collective-permute-start(f32[64,256]{1,0:T(8,128)S(1)} %shard_map.140.a_ref), channel_id=1, source_target_pairs={{0,1},{1,0},{2,3},{3,2},{4,5},{5,4},{6,7},{7,6},{8,9},{9,8},{10,11... | collective-permute-start | bytes 196616 | tf_op jit(solution)/shard_map/ppermute | solution.py:360
  39.8 4.0 %collective-permute-start.12 = (bf16[64,256]{1,0:T(8,128)(2,1)S(1)}, bf16[64,256]{1,0:T(8,128)(2,1)S(1)}, u32[]{:S(2)}, u32[]{:S(2)}) collective-permute-start(bf16[64,256]{1,0:T(8,128)(2,1)S(1)} %get-tuple-element.45), channel_id=1, source_target_pairs={{0,2},{2,0},{4,6},{6,4},{1,3},{3,1},{5,7},{7,5},{8,10},{10,8},{12,... | collective-permute-start | bytes 98312 | tf_op jit(solution)/shard_map/ppermute | solution.py:360
  40.9 3.9 %collective-permute-start.13 = (bf16[64,256]{1,0:T(8,128)(2,1)S(1)}, bf16[64,256]{1,0:T(8,128)(2,1)S(1)}, u32[]{:S(2)}, u32[]{:S(2)}) collective-permute-start(bf16[64,256]{1,0:T(8,128)(2,1)S(1)} %get-tuple-element.45), channel_id=1, source_target_pairs={{0,4},{2,6},{4,0},{6,2},{1,5},{3,7},{5,1},{7,3},{8,12},{10,14},{12... | collective-permute-start | bytes 98312 | tf_op jit(solution)/shard_map/ppermute | solution.py:360
  41.8 4.8 %collective-permute-start.14 = (bf16[64,256]{1,0:T(8,128)(2,1)S(1)}, bf16[64,256]{1,0:T(8,128)(2,1)S(1)}, u32[]{:S(2)}, u32[]{:S(2)}) collective-permute-start(bf16[64,256]{1,0:T(8,128)(2,1)S(1)} %get-tuple-element.45), channel_id=1, source_target_pairs={{0,6},{2,4},{4,2},{6,0},{1,7},{3,5},{5,3},{7,1},{8,14},{10,12},{12... | collective-permute-start | bytes 98312 | tf_op jit(solution)/shard_map/ppermute | solution.py:360

commit v2 on v1

--- a/solution.py
+++ b/solution.py
@@ -173,7 +173,7 @@
             for side, value in ((section, values[c]), (1 - section, values[chunks + c])):
                 start = pl.multiple_of(side * half + starts[c], LANES)
                 normed[to, pl.ds(start, widths[c])] = value
-    step = 256
+    step = 512
 
     def widen(i):
         cols = slice(i * step, (i + 1) * step)
@@ -184,6 +184,7 @@
         if i + 1 < hid // step:
             wide[(i + 1) % 2] = widen(i + 1)
         inner[:, i * step : (i + 1) * step] = gelu(wide[i % 2]).astype(bf16)
+    step = half
 
     def image(start):
         found = []
@@ -203,7 +204,7 @@
 
 def expand_kernel(z_ref, other_ref, pe_ref, out_ref, block):
     block[...] = (z_ref[...] + other_ref[...]).astype(bf16)
-    step = 256
+    step = 512
     for i in range(pe_ref.shape[1] // step):
         cols = slice(i * step, (i + 1) * step)
         out_ref[:, cols] = jnp.maximum(dot(block[...], pe_ref[:, cols]), 0.0).astype(bf16)
@@ -477,7 +478,7 @@
             [
                 pltpu.VMEM((part_pixels, chans), bf16),
                 pltpu.VMEM((part_pixels, hid), bf16),
-                pltpu.VMEM((2, part_pixels, 256), f32),
+                pltpu.VMEM((2, part_pixels, 512), f32),
             ],
             8 * mib,
             4 * part_pixels * hid * chans,

time: 48.6 us -> 48.6 us (level)
  no operation moved by 1% of the time
where the time goes in v2:
time: 48.6 us; the launch traced here: 48.4 us
  Pallas kernels  22.9 us (47%)
  starting transfers between devices  17.8 us (37%)
  waiting for transfers between devices  5.24 us (11%)
  local copies, waits for them, and re-layouts  1.48 us (3%)
  between operations  0.98 us (2%)
    ppermute x17, starting transfers between devices, swap(): lax.ppermute(x, axis, [(i, i ^ bit) for i in range(lax.axis_size(axis))])  17.8 us
    pallas_call x2, Pallas kernels, body(): call(functools.partial(block_kernel, (p * part_pixels, part_pixels, [w fo...  7.62 us
    pallas_call x2, Pallas kernels, body(): call(functools.partial(conv_kernel, (order, shard_rows, width, out_rows,...  6.96 us
    ppermute x17, waiting for transfers between devices, swap(): lax.ppermute(x, axis, [(i, i ^ bit) for i in range(lax.axis_size(axis))])  5.24 us
    pallas_call x1, Pallas kernels, body(): call(project_kernel, [jax.ShapeDtypeStruct((REG, out_dim), f32)], [VMEM]...  2.86 us
    pallas_call x1, Pallas kernels, body(): call(functools.partial(loss_kernel, (shards, parts)), [jax.ShapeDtypeStru...  1.78 us
    dynamic_slice x1, local copies, waits for them, and re-layouts, body(): part = lax.dynamic_slice(features, place, (1, shard_rows, width, span))  1.32 us
    pallas_call x1, Pallas kernels, body(): call(expand_kernel, [jax.ShapeDtypeStruct((part_pixels, hidden), bf16)],...  0.98 us
  transfers between devices with their start and end apart: 17, of which 6 were waited for; matrix products, arithmetic and copies ran while one was open for 0% of the time, Pallas kernels for 44%

profile of v2, /device:TPU:0, one launch (start us, length us, event | category | flops | bytes accessed | tf_op | source)
XLA Modules:
  0.0 48.4 jit_solution(16146840390783470017)
XLA Ops:
  0.7 1.3 %constant_dynamic-slice_fusion = (bf16[1,4,32,384]{3,2,1,0:T(8,128)(2,1)S(1)}, bf16[1,4,32,384]{3,2,1,0:T(8,128)(2,1)S(1)}, bf16[1,4,32,384]{3,2,1,0:T(8,128)(2,...) fusion(bf16[4,4,32,1536]{3,2,1,0:T(8,128)(2,1)} %param.12, ...), kind=kLoop, calls=%fused_computation.4 | loop fusion | bytes 1572888 | tf_op jit(solution)/shard_map/dynamic_slice | solution.py:411
  2.0 0.0 copy-start.1
  2.0 0.0 copy-start.4
  2.0 0.0 copy-start.7
  2.0 3.0 %collective-permute-start.3 = (bf16[128,384]{1,0:T(8,128)(2,1)S(1)}, bf16[128,384]{1,0:T(8,128)(2,1)S(1)}, u32[]{:S(2)}, u32[]{:S(2)}) collective-permute-start(bf16[128,384]{1,0:T(8,128)(2,1)S(1)} %bitcast.27), channel_id=1, source_target_pairs={{0,2},{2,0},{4,6},{6,4},{1,3},{3,1},{5,7},{7,5},{8,10},{10,8},{12,... | collective-permute-start | bytes 294920 | tf_op jit(solution)/shard_map/ppermute | solution.py:361
  5.0 1.5 %collective-permute-start.4 = (bf16[128,384]{1,0:T(8,128)(2,1)S(1)}, bf16[128,384]{1,0:T(8,128)(2,1)S(1)}, u32[]{:S(2)}, u32[]{:S(2)}) collective-permute-start(bf16[128,384]{1,0:T(8,128)(2,1)S(1)} %bitcast.26), channel_id=1, source_target_pairs={{0,4},{2,6},{4,0},{6,2},{1,5},{3,7},{5,1},{7,3},{8,12},{10,14},{12... | collective-permute-start | bytes 294920 | tf_op jit(solution)/shard_map/ppermute | solution.py:361
  6.5 0.0 collective-permute-start.5
  6.6 0.1 stack.20.pos_ref.refs_0_
  6.6 0.0 copy-done.1
  6.7 0.0 copy-done.4
  6.7 0.6 %shard_map.132 = bf16[32,384]{1,0:T(8,128)(2,1)S(1)} custom-call(s32[6]{0:T(128)S(1)} %stack.20.pos_ref.refs_0_, s32[4,4,32]{2,1,0:T(4,128)S(1)} %copy-done.4, bf16[64,256]{1,0:T(8,128)(2,1)S(1)} %copy-done.1, f32[32,128]{1,0:T(8,128)S(1)} %shard_map.131.blank_ref), custom_call_target="tpu_custom_call" | custom-call | bytes 1000000 | tf_op jit(solution)/shard_map/pallas_call | solution.py:418
  7.2 0.0 slice-start.2
  7.2 0.1 pad_maximum_fusion
  7.3 2.0 %collective-permute-start = (bf16[160,384]{1,0:T(8,128)(2,1)S(1)}, bf16[160,384]{1,0:T(8,128)(2,1)S(1)}, u32[]{:S(2)}, u32[]{:S(2)}) collective-permute-start(bf16[160,384]{1,0:T(8,128)(2,1)S(1)} %get-tuple-element.63), channel_id=1, source_target_pairs={{0,2},{2,0},{4,6},{6,4},{1,3},{3,1},{5,7},{7,5},{8,10},{10,8},{12,... | collective-permute-start | bytes 368648 | tf_op jit(solution)/shard_map/ppermute | solution.py:361
  9.3 1.5 %collective-permute-start.1 = (bf16[160,384]{1,0:T(8,128)(2,1)S(1)}, bf16[160,384]{1,0:T(8,128)(2,1)S(1)}, u32[]{:S(2)}, u32[]{:S(2)}) collective-permute-start(bf16[160,384]{1,0:T(8,128)(2,1)S(1)} %get-tuple-element.64), channel_id=1, source_target_pairs={{0,4},{2,6},{4,0},{6,2},{1,5},{3,7},{5,1},{7,3},{8,12},{10,14},{12... | collective-permute-start | bytes 368648 | tf_op jit(solution)/shard_map/ppermute | solution.py:361
  10.8 0.0 collective-permute-done.3.refs_1_
  10.8 0.5 %collective-permute-start.2 = (bf16[160,384]{1,0:T(8,128)(2,1)S(1)}, bf16[160,384]{1,0:T(8,128)(2,1)S(1)}, u32[]{:S(2)}, u32[]{:S(2)}) collective-permute-start(bf16[160,384]{1,0:T(8,128)(2,1)S(1)} %get-tuple-element.62), channel_id=1, source_target_pairs={{0,6},{2,4},{4,2},{6,0},{1,7},{3,5},{5,3},{7,1},{8,14},{10,12},{12... | collective-permute-start | bytes 368648 | tf_op jit(solution)/shard_map/ppermute | solution.py:361
  11.3 0.0 collective-permute-done.4.refs_2_
  11.3 1.5 %collective-permute-done.5.refs_3_ = bf16[128,384]{1,0:T(8,128)(2,1)S(1)} collective-permute-done((bf16[128,384]{1,0:T(8,128)(2,1)S(1)}, bf16[128,384]{1,0:T(8,128)(2,1)S(1)}, u32[]{:S(2)}, u32[]{:S(2)}) %collective-permute-start.5) | collective-permute-done | bytes 98336 | tf_op jit(solution)/shard_map/ppermute | solution.py:361
  12.9 0.0 copy-done.7
  12.9 3.5 %shard_map.133 = (f32[512,384]{1,0:T(8,128)S(1)}, bf16[512,384]{1,0:T(8,128)(2,1)S(1)}) custom-call(s32[6]{0:T(128)S(1)} %stack.20.pos_ref.refs_0_, bf16[128,384]{1,0:T(8,128)(2,1)S(1)} %bitcast.20, bf16[128,384]{1,0:T(8,128)(2,1)S(1)} %collective-permute-done.3.refs_1_, bf16[128,384]{1,0:T(8,128)(2,1)S(1)} %collective-permute-done.4.refs_2_, ...), custom_call_target="tpu_custom_call" | custom-call | flops 1926758400 | bytes 1966080 | tf_op jit(solution)/shard_map/pallas_call | solution.py:438
  16.4 0.1 collective-permute-start.7
  16.4 0.0 collective-permute-done.refs_1_
  16.5 0.6 %collective-permute-done.1.refs_2_ = bf16[160,384]{1,0:T(8,128)(2,1)S(1)} collective-permute-done((bf16[160,384]{1,0:T(8,128)(2,1)S(1)}, bf16[160,384]{1,0:T(8,128)(2,1)S(1)}, u32[]{:S(2)}, u32[]{:S(2)}) %collective-permute-start.1) | collective-permute-done | bytes 122912 | tf_op jit(solution)/shard_map/ppermute | solution.py:361
  17.0 0.0 collective-permute-done.2.refs_3_
  17.0 3.5 %shard_map.134 = (f32[512,384]{1,0:T(8,128)S(1)}, bf16[512,384]{1,0:T(8,128)(2,1)S(1)}) custom-call(s32[6]{0:T(128)S(1)} %stack.20.pos_ref.refs_0_, bf16[160,384]{1,0:T(8,128)(2,1)S(1)} %get-tuple-element.35.refs_0_, bf16[160,384]{1,0:T(8,128)(2,1)S(1)} %collective-permute-done.refs_1_, bf16[160,384]{1,0:T(8,128)(2,1)S(1)} %collective-permute-done.1.refs_2_, ...), custom_call_target="tpu_custom_call" | custom-call | flops 1926758400 | bytes 1966080 | tf_op jit(solution)/shard_map/pallas_call | solution.py:438
  20.5 0.1 collective-permute-start.8
  20.6 2.7 %collective-permute-start.6 = (bf16[128,256]{1,0:T(8,128)(2,1)S(1)}, bf16[128,256]{1,0:T(8,128)(2,1)S(1)}, u32[]{:S(2)}, u32[]{:S(2)}) collective-permute-start(bf16[128,256]{1,0:T(8,128)(2,1)S(1)} %shard_map.135.refs_0_), channel_id=1, source_target_pairs={{0,16},{8,24},{16,0},{24,8},{1,17},{9,25},{17,1},{25,9},{2,18},{10... | collective-permute-start | bytes 196616 | tf_op jit(solution)/shard_map/ppermute | solution.py:361
  23.3 0.0 collective-permute-done.7.refs_2_
  23.3 0.0 collective-permute-done.8.refs_3_
  23.3 0.0 slice-done.2
  23.3 0.0 slice-done.3
  23.3 0.0 slice-start.4
  23.4 3.8 %shard_map.136.z_ref = f32[256,1536]{1,0:T(8,128)S(1)} custom-call(s32[6]{0:T(128)S(1)} %stack.20.pos_ref.refs_0_, f32[512,384]{1,0:T(8,128)S(1)} %get-tuple-element.32.refs_0_, f32[512,384]{1,0:T(8,128)S(1)} %get-tuple-element.34.refs_1_, f32[512,384]{1,0:T(8,128)S(1)} %collective-permute-done.7.refs_2_, f32[512,384]{1,0:T(8,128)S(1)} %collective-permute-done.8.refs_3_, ...), custom_call_target="tpu_custom_call" | custom-call | flops 2415919104 | bytes 9437184 | tf_op jit(solution)/shard_map/pallas_call | solution.py:474
  27.2 0.0 slice-start.5
  27.2 0.2 collective-permute-start.10
  27.4 0.0 collective-permute-done.6.refs_1_
  27.4 3.8 %shard_map.137.z_ref = f32[256,1536]{1,0:T(8,128)S(1)} custom-call(s32[6]{0:T(128)S(1)} %stack.20.pos_ref.refs_0_, f32[512,384]{1,0:T(8,128)S(1)} %get-tuple-element.32.refs_0_, f32[512,384]{1,0:T(8,128)S(1)} %get-tuple-element.34.refs_1_, f32[512,384]{1,0:T(8,128)S(1)} %collective-permute-done.7.refs_2_, f32[512,384]{1,0:T(8,128)S(1)} %collective-permute-done.8.refs_3_, ...), custom_call_target="tpu_custom_call" | custom-call | flops 2415919104 | bytes 9437184 | tf_op jit(solution)/shard_map/pallas_call | solution.py:474
  31.2 0.4 collective-permute-start.9
  31.7 1.6 %collective-permute-start.15 = (bf16[256,256]{1,0:T(8,128)(2,1)S(1)}, bf16[256,256]{1,0:T(8,128)(2,1)S(1)}, u32[]{:S(2)}, u32[]{:S(2)}) collective-permute-start(bf16[256,256]{1,0:T(8,128)(2,1)S(1)} %shard_map.143), channel_id=1, source_target_pairs={{0,8},{8,0},{16,24},{24,16},{1,9},{9,1},{17,25},{25,17},{2,10},{10... | collective-permute-start | bytes 393224 | tf_op jit(solution)/shard_map/ppermute | solution.py:361
  33.3 0.0 collective-permute-done.10.other_ref
  33.3 1.0 %shard_map.138.first_ref = bf16[256,1024]{1,0:T(8,128)(2,1)S(1)} custom-call(f32[256,1536]{1,0:T(8,128)S(1)} %shard_map.136.z_ref, f32[256,1536]{1,0:T(8,128)S(1)} %collective-permute-done.10.other_ref, bf16[1536,1024]{1,0:T(8,128)(2,1)S(1)} %copy-done), custom_call_target="tpu_custom_call" | custom-call | flops 805306368 | bytes 3145728 | tf_op jit(solution)/shard_map/pallas_call | solution.py:493
  34.3 0.9 %shard_map.139.hot_ref = bf16[576,512]{1,0:T(8,128)(2,1)S(1)} custom-call(s32[6]{0:T(128)S(1)} %stack.20.pos_ref.refs_0_, bf16[160,384]{1,0:T(8,128)(2,1)S(1)} %get-tuple-element.35.refs_0_, bf16[160,384]{1,0:T(8,128)(2,1)S(1)} %collective-permute-done.refs_1_, bf16[160,384]{1,0:T(8,128)(2,1)S(1)} %collective-permute-done.1.refs_2_, ...), custom_call_target="tpu_custom_call" | custom-call | flops 100000000 | bytes 1000000 | tf_op jit(solution)/shard_map/pallas_call | solution.py:502
  35.2 0.0 copy-start.5
  35.2 0.0 copy-start.6
  35.2 0.0 collective-permute-done.9.other_ref
  35.2 0.0 slice-done.4
  35.2 0.0 slice-done.5
  35.2 2.9 %shard_map.140.a_ref = f32[64,256]{1,0:T(8,128)S(1)} custom-call(f32[256,1536]{1,0:T(8,128)S(1)} %shard_map.137.z_ref, f32[256,1536]{1,0:T(8,128)S(1)} %collective-permute-done.9.other_ref, bf16[256,1024]{1,0:T(8,128)(2,1)S(1)} %shard_map.138.first_ref, bf16[1536,1024]{1,0:T(8,128)(2,1)S(1)} %copy-done, bf16[9,1024,256]{2,1,0:T(8,128)(2,1)S(1)} %bitcast.18, ...), custom_call_target="tpu_custom_call" | custom-call | flops 2013265920 | bytes 6291456 | tf_op jit(solution)/shard_map/pallas_call | solution.py:511
  38.1 0.0 collective-permute-done.15.refs_2_
  38.1 0.1 collective-permute-start.16
  38.2 0.5 %collective-permute-start.11 = (f32[64,256]{1,0:T(8,128)S(1)}, f32[64,256]{1,0:T(8,128)S(1)}, u32[]{:S(2)}, u32[]{:S(2)}) collective-permute-start(f32[64,256]{1,0:T(8,128)S(1)} %shard_map.140.a_ref), channel_id=1, source_target_pairs={{0,1},{1,0},{2,3},{3,2},{4,5},{5,4},{6,7},{7,6},{8,9},{9,8},{10,11... | collective-permute-start | bytes 196616 | tf_op jit(solution)/shard_map/ppermute | solution.py:361
  38.7 0.0 copy-done.5
  38.7 1.0 %shard_map.142 = (bf16[64,256]{1,0:T(8,128)(2,1)S(1)}, f32[64,128]{1,0:T(8,128)S(1)}) custom-call(s32[6]{0:T(128)S(1)} %stack.20.pos_ref.refs_0_, bf16[160,384]{1,0:T(8,128)(2,1)S(1)} %get-tuple-element.35.refs_0_, bf16[160,384]{1,0:T(8,128)(2,1)S(1)} %collective-permute-done.refs_1_, bf16[160,384]{1,0:T(8,128)(2,1)S(1)} %collective-permute-done.1.refs_2_, ...), custom_call_target="tpu_custom_call" | custom-call | flops 100000000 | bytes 1000000 | tf_op jit(solution)/shard_map/pallas_call | solution.py:523
  39.7 0.1 collective-permute-done.11.b_ref
  39.8 1.0 %collective-permute-start.12 = (bf16[64,256]{1,0:T(8,128)(2,1)S(1)}, bf16[64,256]{1,0:T(8,128)(2,1)S(1)}, u32[]{:S(2)}, u32[]{:S(2)}) collective-permute-start(bf16[64,256]{1,0:T(8,128)(2,1)S(1)} %get-tuple-element.45), channel_id=1, source_target_pairs={{0,2},{2,0},{4,6},{6,4},{1,3},{3,1},{5,7},{7,5},{8,10},{10,8},{12,... | collective-permute-start | bytes 98312 | tf_op jit(solution)/shard_map/ppermute | solution.py:361
  40.9 1.0 %collective-permute-start.13 = (bf16[64,256]{1,0:T(8,128)(2,1)S(1)}, bf16[64,256]{1,0:T(8,128)(2,1)S(1)}, u32[]{:S(2)}, u32[]{:S(2)}) collective-permute-start(bf16[64,256]{1,0:T(8,128)(2,1)S(1)} %get-tuple-element.45), channel_id=1, source_target_pairs={{0,4},{2,6},{4,0},{6,2},{1,5},{3,7},{5,1},{7,3},{8,12},{10,14},{12... | collective-permute-start | bytes 98312 | tf_op jit(solution)/shard_map/ppermute | solution.py:361
  41.8 1.6 %collective-permute-start.14 = (bf16[64,256]{1,0:T(8,128)(2,1)S(1)}, bf16[64,256]{1,0:T(8,128)(2,1)S(1)}, u32[]{:S(2)}, u32[]{:S(2)}) collective-permute-start(bf16[64,256]{1,0:T(8,128)(2,1)S(1)} %get-tuple-element.45), channel_id=1, source_target_pairs={{0,6},{2,4},{4,2},{6,0},{1,7},{3,5},{5,3},{7,1},{8,14},{10,12},{12... | collective-permute-start | bytes 98312 | tf_op jit(solution)/shard_map/ppermute | solution.py:361
  43.4 0.0 collective-permute-done.16.refs_3_
  43.4 0.2 shard_map.145
  43.6 0.2 collective-permute-done.12.refs_2_
  43.8 0.9 %collective-permute-done.13.refs_3_ = bf16[64,256]{1,0:T(8,128)(2,1)S(1)} collective-permute-done((bf16[64,256]{1,0:T(8,128)(2,1)S(1)}, bf16[64,256]{1,0:T(8,128)(2,1)S(1)}, u32[]{:S(2)}, u32[]{:S(2)}) %collective-permute-start.13) | collective-permute-done | bytes 32800 | tf_op jit(solution)/shard_map/ppermute | solution.py:361
  44.8 1.9 %collective-permute-done.14.refs_4_ = bf16[64,256]{1,0:T(8,128)(2,1)S(1)} collective-permute-done((bf16[64,256]{1,0:T(8,128)(2,1)S(1)}, bf16[64,256]{1,0:T(8,128)(2,1)S(1)}, u32[]{:S(2)}, u32[]{:S(2)}) %collective-permute-start.14) | collective-permute-done | bytes 32800 | tf_op jit(solution)/shard_map/ppermute | solution.py:361
  46.6 1.8 %shard_map.146 = (f32[64,256]{1,0:T(8,128)}, f32[1,64]{1,0:T(1,128)}) custom-call(s32[6]{0:T(128)S(1)} %stack.20.pos_ref.refs_0_, f32[64,256]{1,0:T(8,128)S(1)} %get-tuple-element.44.refs_1_, bf16[64,256]{1,0:T(8,128)(2,1)S(1)} %collective-permute-done.12.refs_2_, bf16[64,256]{1,0:T(8,128)(2,1)S(1)} %collective-permute-done.13.refs_3_, ...), custom_call_target="tpu_custom_call" | custom-call | flops 100000000 | bytes 1000000 | tf_op jit(solution)/shard_map/pallas_call | solution.py:555
  (20 shorter events, 0.1 us)
Async XLA Ops:
  2.0 4.7 %copy-start.1 = (bf16[64,256]{1,0:T(8,128)(2,1)S(1)}, bf16[64,256]{1,0:T(8,128)(2,1)}, u32[]{:S(2)}) copy-start(bf16[64,256]{1,0:T(8,128)(2,1)} %key_ref.1) | copy-start | bytes 98308
  2.0 4.7 %copy-start.4 = (s32[4,4,32]{2,1,0:T(4,128)S(1)}, s32[4,4,32]{2,1,0:T(4,128)}, u32[]{:S(2)}) copy-start(s32[4,4,32]{2,1,0:T(4,128)} %ids_ref.1) | copy-start | bytes 6148
  2.0 10.9 %copy-start.7 = (bf16[7,7,1536]{2,1,0:T(8,128)(2,1)S(1)}, bf16[7,7,1536]{2,1,0:T(8,128)(2,1)}, u32[]{:S(2)}) copy-start(bf16[7,7,1536]{2,1,0:T(8,128)(2,1)} %refs_4_.4) | copy-start | bytes 451588
  2.0 8.8 %collective-permute-start.3 = (bf16[128,384]{1,0:T(8,128)(2,1)S(1)}, bf16[128,384]{1,0:T(8,128)(2,1)S(1)}, u32[]{:S(2)}, u32[]{:S(2)}) collective-permute-start(bf16[128,384]{1,0:T(8,128)(2,1)S(1)} %bitcast.27), channel_id=1, source_target_pairs={{0,2},{2,0},{4,6},{6,4},{1,3},{3,1},{5,7},{7,5},{8,10},{10,8},{12,... | collective-permute-start | bytes 294920 | tf_op jit(solution)/shard_map/ppermute | solution.py:361
  5.0 6.3 %collective-permute-start.4 = (bf16[128,384]{1,0:T(8,128)(2,1)S(1)}, bf16[128,384]{1,0:T(8,128)(2,1)S(1)}, u32[]{:S(2)}, u32[]{:S(2)}) collective-permute-start(bf16[128,384]{1,0:T(8,128)(2,1)S(1)} %bitcast.26), channel_id=1, source_target_pairs={{0,4},{2,6},{4,0},{6,2},{1,5},{3,7},{5,1},{7,3},{8,12},{10,14},{12... | collective-permute-start | bytes 294920 | tf_op jit(solution)/shard_map/ppermute | solution.py:361
  6.5 6.3 %collective-permute-start.5 = (bf16[128,384]{1,0:T(8,128)(2,1)S(1)}, bf16[128,384]{1,0:T(8,128)(2,1)S(1)}, u32[]{:S(2)}, u32[]{:S(2)}) collective-permute-start(bf16[128,384]{1,0:T(8,128)(2,1)S(1)} %bitcast.25), channel_id=1, source_target_pairs={{0,6},{2,4},{4,2},{6,0},{1,7},{3,5},{5,3},{7,1},{8,14},{10,12},{12... | collective-permute-start | bytes 294920 | tf_op jit(solution)/shard_map/ppermute | solution.py:361
  7.2 16.1 %slice-start.2 = ((s8[4718592]{0:T(1024)(128)(4,1)}), s8[524288]{0:T(1024)(128)(4,1)S(1)}, s32[]{:S(2)}) async-start(s8[4718592]{0:T(1024)(128)(4,1)} %bitcast.15), calls=%async_computation.2 | async-start | bytes 1048576
  7.3 9.2 %collective-permute-start = (bf16[160,384]{1,0:T(8,128)(2,1)S(1)}, bf16[160,384]{1,0:T(8,128)(2,1)S(1)}, u32[]{:S(2)}, u32[]{:S(2)}) collective-permute-start(bf16[160,384]{1,0:T(8,128)(2,1)S(1)} %get-tuple-element.63), channel_id=1, source_target_pairs={{0,2},{2,0},{4,6},{6,4},{1,3},{3,1},{5,7},{7,5},{8,10},{10,8},{12,... | collective-permute-start | bytes 368648 | tf_op jit(solution)/shard_map/ppermute | solution.py:361
  9.3 7.7 %collective-permute-start.1 = (bf16[160,384]{1,0:T(8,128)(2,1)S(1)}, bf16[160,384]{1,0:T(8,128)(2,1)S(1)}, u32[]{:S(2)}, u32[]{:S(2)}) collective-permute-start(bf16[160,384]{1,0:T(8,128)(2,1)S(1)} %get-tuple-element.64), channel_id=1, source_target_pairs={{0,4},{2,6},{4,0},{6,2},{1,5},{3,7},{5,1},{7,3},{8,12},{10,14},{12... | collective-permute-start | bytes 368648 | tf_op jit(solution)/shard_map/ppermute | solution.py:361
  10.8 12.5 %slice-start.3 = ((s8[4718592]{0:T(1024)(128)(4,1)}), s8[4194304]{0:T(1024)(128)(4,1)S(1)}, s32[]{:S(2)}) async-start(s8[4718592]{0:T(1024)(128)(4,1)} %bitcast.15), calls=%async_computation.3 | async-start | bytes 8388608
  10.8 6.2 %collective-permute-start.2 = (bf16[160,384]{1,0:T(8,128)(2,1)S(1)}, bf16[160,384]{1,0:T(8,128)(2,1)S(1)}, u32[]{:S(2)}, u32[]{:S(2)}) collective-permute-start(bf16[160,384]{1,0:T(8,128)(2,1)S(1)} %get-tuple-element.62), channel_id=1, source_target_pairs={{0,6},{2,4},{4,2},{6,0},{1,7},{3,5},{5,3},{7,1},{8,14},{10,12},{12... | collective-permute-start | bytes 368648 | tf_op jit(solution)/shard_map/ppermute | solution.py:361
  12.9 10.4 %slice-start = ((s8[4718592]{0:T(1024)(128)(4,1)}), s8[4194304]{0:T(1024)(128)(4,1)S(1)}, s32[]{:S(2)}) async-start(s8[4718592]{0:T(1024)(128)(4,1)} %bitcast.13), calls=%async_computation | async-start | bytes 8388608
  16.4 6.9 %collective-permute-start.7 = (f32[512,384]{1,0:T(8,128)S(1)}, f32[512,384]{1,0:T(8,128)S(1)}, u32[]{:S(2)}, u32[]{:S(2)}) collective-permute-start(f32[512,384]{1,0:T(8,128)S(1)} %get-tuple-element.32.refs_0_), channel_id=1, source_target_pairs={{0,1},{1,0},{2,3},{3,2},{4,5},{5,4},{6,7},{7,6},{8,9},{9,8},{10,11... | collective-permute-start | bytes 2359304 | tf_op jit(solution)/shard_map/ppermute | solution.py:361
  17.0 6.3 %slice-start.1 = ((s8[4718592]{0:T(1024)(128)(4,1)}), s8[524288]{0:T(1024)(128)(4,1)S(1)}, s32[]{:S(2)}) async-start(s8[4718592]{0:T(1024)(128)(4,1)} %bitcast.13), calls=%async_computation.1 | async-start | bytes 1048576
  17.0 6.3 %copy-start.2 = (bf16[1536]{0:T(1024)(128)(2,1)S(1)}, bf16[1536]{0:T(1024)(128)(2,1)}, u32[]{:S(2)}) copy-start(bf16[1536]{0:T(1024)(128)(2,1)} %refs_6_.3) | copy-start | bytes 9220
  17.0 6.3 %copy-start.3 = (bf16[1536]{0:T(1024)(128)(2,1)S(1)}, bf16[1536]{0:T(1024)(128)(2,1)}, u32[]{:S(2)}) copy-start(bf16[1536]{0:T(1024)(128)(2,1)} %refs_7_.3) | copy-start | bytes 9220
  20.5 2.8 %collective-permute-start.8 = (f32[512,384]{1,0:T(8,128)S(1)}, f32[512,384]{1,0:T(8,128)S(1)}, u32[]{:S(2)}, u32[]{:S(2)}) collective-permute-start(f32[512,384]{1,0:T(8,128)S(1)} %get-tuple-element.34.refs_1_), channel_id=1, source_target_pairs={{0,1},{1,0},{2,3},{3,2},{4,5},{5,4},{6,7},{7,6},{8,9},{9,8},{10,11... | collective-permute-start | bytes 2359304 | tf_op jit(solution)/shard_map/ppermute | solution.py:361
  20.6 6.8 %collective-permute-start.6 = (bf16[128,256]{1,0:T(8,128)(2,1)S(1)}, bf16[128,256]{1,0:T(8,128)(2,1)S(1)}, u32[]{:S(2)}, u32[]{:S(2)}) collective-permute-start(bf16[128,256]{1,0:T(8,128)(2,1)S(1)} %shard_map.135.refs_0_), channel_id=1, source_target_pairs={{0,16},{8,24},{16,0},{24,8},{1,17},{9,25},{17,1},{25,9},{2,18},{10... | collective-permute-start | bytes 196616 | tf_op jit(solution)/shard_map/ppermute | solution.py:361
  23.3 11.9 %slice-start.4 = ((s8[4718592]{0:T(1024)(128)(4,1)}), s8[4194304]{0:T(1024)(128)(4,1)S(1)}, s32[]{:S(2)}) async-start(s8[4718592]{0:T(1024)(128)(4,1)} %bitcast.17), calls=%async_computation.4 | async-start | bytes 8388608
  27.2 8.0 %slice-start.5 = ((s8[4718592]{0:T(1024)(128)(4,1)}), s8[524288]{0:T(1024)(128)(4,1)S(1)}, s32[]{:S(2)}) async-start(s8[4718592]{0:T(1024)(128)(4,1)} %bitcast.17), calls=%async_computation.5 | async-start | bytes 1048576
  27.2 6.1 %collective-permute-start.10 = (f32[256,1536]{1,0:T(8,128)S(1)}, f32[256,1536]{1,0:T(8,128)S(1)}, u32[]{:S(2)}, u32[]{:S(2)}) collective-permute-start(f32[256,1536]{1,0:T(8,128)S(1)} %shard_map.136.z_ref), channel_id=1, source_target_pairs={{0,1},{1,0},{2,3},{3,2},{4,5},{5,4},{6,7},{7,6},{8,9},{9,8},{10,11... | collective-permute-start | bytes 4718600 | tf_op jit(solution)/shard_map/ppermute | solution.py:361
  27.4 5.9 %copy-start = (bf16[1536,1024]{1,0:T(8,128)(2,1)S(1)}, bf16[1536,1024]{1,0:T(8,128)(2,1)}, u32[]{:S(2)}) copy-start(bf16[1536,1024]{1,0:T(8,128)(2,1)} %pe_ref.3) | copy-start | bytes 9437188
  31.2 4.0 %collective-permute-start.9 = (f32[256,1536]{1,0:T(8,128)S(1)}, f32[256,1536]{1,0:T(8,128)S(1)}, u32[]{:S(2)}, u32[]{:S(2)}) collective-permute-start(f32[256,1536]{1,0:T(8,128)S(1)} %shard_map.137.z_ref), channel_id=1, source_target_pairs={{0,1},{1,0},{2,3},{3,2},{4,5},{5,4},{6,7},{7,6},{8,9},{9,8},{10,11... | collective-permute-start | bytes 4718600 | tf_op jit(solution)/shard_map/ppermute | solution.py:361
  31.7 6.4 %collective-permute-start.15 = (bf16[256,256]{1,0:T(8,128)(2,1)S(1)}, bf16[256,256]{1,0:T(8,128)(2,1)S(1)}, u32[]{:S(2)}, u32[]{:S(2)}) collective-permute-start(bf16[256,256]{1,0:T(8,128)(2,1)S(1)} %shard_map.143), channel_id=1, source_target_pairs={{0,8},{8,0},{16,24},{24,16},{1,9},{9,1},{17,25},{25,17},{2,10},{10... | collective-permute-start | bytes 393224 | tf_op jit(solution)/shard_map/ppermute | solution.py:361
  35.2 3.5 %copy-start.5 = (s32[4,64]{1,0:T(4,128)S(1)}, s32[4,64]{1,0:T(4,128)}, u32[]{:S(2)}) copy-start(s32[4,64]{1,0:T(4,128)} %refs_5_.1) | copy-start | bytes 3076
  35.2 3.5 %copy-start.6 = (s32[1,256]{1,0:T(1,128)S(1)}, s32[1,256]{1,0:T(1,128)}, u32[]{:S(2)}) copy-start(s32[1,256]{1,0:T(1,128)} %refs_4_.5) | copy-start | bytes 3076
  38.1 5.3 %collective-permute-start.16 = (bf16[512,256]{1,0:T(8,128)(2,1)S(1)}, bf16[512,256]{1,0:T(8,128)(2,1)S(1)}, u32[]{:S(2)}, u32[]{:S(2)}) collective-permute-start(bf16[512,256]{1,0:T(8,128)(2,1)S(1)} %shard_map.144), channel_id=1, source_target_pairs={{0,1},{1,0},{2,3},{3,2},{4,5},{5,4},{6,7},{7,6},{8,9},{9,8},{10,11... | collective-permute-start | bytes 786440 | tf_op jit(solution)/shard_map/ppermute | solution.py:361
  38.2 1.6 %collective-permute-start.11 = (f32[64,256]{1,0:T(8,128)S(1)}, f32[64,256]{1,0:T(8,128)S(1)}, u32[]{:S(2)}, u32[]{:S(2)}) collective-permute-start(f32[64,256]{1,0:T(8,128)S(1)} %shard_map.140.a_ref), channel_id=1, source_target_pairs={{0,1},{1,0},{2,3},{3,2},{4,5},{5,4},{6,7},{7,6},{8,9},{9,8},{10,11... | collective-permute-start | bytes 196616 | tf_op jit(solution)/shard_map/ppermute | solution.py:361
  39.8 4.0 %collective-permute-start.12 = (bf16[64,256]{1,0:T(8,128)(2,1)S(1)}, bf16[64,256]{1,0:T(8,128)(2,1)S(1)}, u32[]{:S(2)}, u32[]{:S(2)}) collective-permute-start(bf16[64,256]{1,0:T(8,128)(2,1)S(1)} %get-tuple-element.45), channel_id=1, source_target_pairs={{0,2},{2,0},{4,6},{6,4},{1,3},{3,1},{5,7},{7,5},{8,10},{10,8},{12,... | collective-permute-start | bytes 98312 | tf_op jit(solution)/shard_map/ppermute | solution.py:361
  40.9 3.9 %collective-permute-start.13 = (bf16[64,256]{1,0:T(8,128)(2,1)S(1)}, bf16[64,256]{1,0:T(8,128)(2,1)S(1)}, u32[]{:S(2)}, u32[]{:S(2)}) collective-permute-start(bf16[64,256]{1,0:T(8,128)(2,1)S(1)} %get-tuple-element.45), channel_id=1, source_target_pairs={{0,4},{2,6},{4,0},{6,2},{1,5},{3,7},{5,1},{7,3},{8,12},{10,14},{12... | collective-permute-start | bytes 98312 | tf_op jit(solution)/shard_map/ppermute | solution.py:361
  41.8 4.8 %collective-permute-start.14 = (bf16[64,256]{1,0:T(8,128)(2,1)S(1)}, bf16[64,256]{1,0:T(8,128)(2,1)S(1)}, u32[]{:S(2)}, u32[]{:S(2)}) collective-permute-start(bf16[64,256]{1,0:T(8,128)(2,1)S(1)} %get-tuple-element.45), channel_id=1, source_target_pairs={{0,6},{2,4},{4,2},{6,0},{1,7},{3,5},{5,3},{7,1},{8,14},{10,12},{12... | collective-permute-start | bytes 98312 | tf_op jit(solution)/shard_map/ppermute | solution.py:361

commit v3 on v2

--- a/solution.py
+++ b/solution.py
@@ -431,10 +431,12 @@
     order = list(range(shards))
     last = [got[-1][k] for k in order]
 
-    cuts = [(c, 0, span) for c in range(CHUNKS)]
+    late = span - LANES
+    cuts = [(c, 0, span) for c in range(CHUNKS - 1)]
+    cuts += [(CHUNKS - 1, 0, late), (CHUNKS - 1, late, span - late)]
     own, other, img = [], [], []
     for c, lane0, wide in cuts:
-        here = after(spot, *own) if own else spot
+        here = after(spot, *own) if own else after(spot, *parcels[-1])
         taps, image = call(
             functools.partial(conv_kernel, (order, shard_rows, width, out_rows, c * span + lane0, lane0)),
             [
@@ -447,7 +449,7 @@
                 pltpu.VMEM((49, 8, LANES), f32),
             ],
             3 * mib,
-            out_pixels * wide * 98 * 100,
+            out_pixels * span * 98 * 100,
             out_pixels * wide * 10,
         )(here, *[got[c][k] for k in order], dw_kernel)
         own.append(taps)

time: 48.6 us -> 49.8 us (1.025)
  Pallas kernels: 22.9 us -> 23.5 us
  starting transfers between devices: 17.8 us -> 18.3 us
    pallas_call x2 -> x3, Pallas kernels: 6.96 us -> 7.48 us  [body(): call(functools.partial(conv_kernel, (order, shard_rows, width, out_rows,...]
    ppermute x17 -> x18, starting transfers between devices: 17.8 us -> 18.3 us  [swap(): lax.ppermute(x, axis, [(i, i ^ bit) for i in range(lax.axis_size(axis))])]
    ppermute x17 -> x18, waiting for transfers between devices: 5.24 us -> 5.24 us  [swap(): lax.ppermute(x, axis, [(i, i ^ bit) for i in range(lax.axis_size(axis))])]
  transfers between devices with their start and end apart: 17 -> 18, of which waited for: 6 -> 6; matrix products, arithmetic and copies ran while one was open for 0% -> 0% of each run, Pallas kernels for 44% -> 44%
where the time goes in v3:
time: 49.8 us; the launch traced here: 49.6 us
  Pallas kernels  23.5 us (47%)
  starting transfers between devices  18.3 us (37%)
  waiting for transfers between devices  5.24 us (11%)
  local copies, waits for them, and re-layouts  1.49 us (3%)
  between operations  1.03 us (2%)
    ppermute x18, starting transfers between devices, swap(): lax.ppermute(x, axis, [(i, i ^ bit) for i in range(lax.axis_size(axis))])  18.3 us
    pallas_call x2, Pallas kernels, body(): call(functools.partial(block_kernel, (p * part_pixels, part_pixels, [w fo...  7.74 us
    pallas_call x3, Pallas kernels, body(): call(functools.partial(conv_kernel, (order, shard_rows, width, out_rows,...  7.48 us
    ppermute x18, waiting for transfers between devices, swap(): lax.ppermute(x, axis, [(i, i ^ bit) for i in range(lax.axis_size(axis))])  5.24 us
    pallas_call x1, Pallas kernels, body(): call(project_kernel, [jax.ShapeDtypeStruct((REG, out_dim), f32)], [VMEM]...  2.86 us
    pallas_call x1, Pallas kernels, body(): call(functools.partial(loss_kernel, (shards, parts)), [jax.ShapeDtypeStru...  1.78 us
    dynamic_slice x1, local copies, waits for them, and re-layouts, body(): part = lax.dynamic_slice(features, place, (1, shard_rows, width, span))  1.32 us
  transfers between devices with their start and end apart: 18, of which 6 were waited for; matrix products, arithmetic and copies ran while one was open for 0% of the time, Pallas kernels for 44%

profile of v3, /device:TPU:0, one launch (start us, length us, event | category | flops | bytes accessed | tf_op | source)
XLA Modules:
  0.0 49.6 jit_solution(17665995185402993198)
XLA Ops:
  0.7 1.3 %constant_dynamic-slice_fusion = (bf16[1,4,32,384]{3,2,1,0:T(8,128)(2,1)S(1)}, bf16[1,4,32,384]{3,2,1,0:T(8,128)(2,1)S(1)}, bf16[1,4,32,384]{3,2,1,0:T(8,128)(2,...) fusion(bf16[4,4,32,1536]{3,2,1,0:T(8,128)(2,1)} %param.12, ...), kind=kLoop, calls=%fused_computation.4 | loop fusion | bytes 1572888 | tf_op jit(solution)/shard_map/dynamic_slice | solution.py:411
  2.0 0.0 copy-start.1
  2.0 0.0 copy-start.4
  2.0 0.0 copy-start.7
  2.0 3.0 %collective-permute-start.3 = (bf16[128,384]{1,0:T(8,128)(2,1)S(1)}, bf16[128,384]{1,0:T(8,128)(2,1)S(1)}, u32[]{:S(2)}, u32[]{:S(2)}) collective-permute-start(bf16[128,384]{1,0:T(8,128)(2,1)S(1)} %bitcast.27), channel_id=1, source_target_pairs={{0,2},{2,0},{4,6},{6,4},{1,3},{3,1},{5,7},{7,5},{8,10},{10,8},{12,... | collective-permute-start | bytes 294920 | tf_op jit(solution)/shard_map/ppermute | solution.py:361
  5.0 1.5 %collective-permute-start.4 = (bf16[128,384]{1,0:T(8,128)(2,1)S(1)}, bf16[128,384]{1,0:T(8,128)(2,1)S(1)}, u32[]{:S(2)}, u32[]{:S(2)}) collective-permute-start(bf16[128,384]{1,0:T(8,128)(2,1)S(1)} %bitcast.26), channel_id=1, source_target_pairs={{0,4},{2,6},{4,0},{6,2},{1,5},{3,7},{5,1},{7,3},{8,12},{10,14},{12... | collective-permute-start | bytes 294920 | tf_op jit(solution)/shard_map/ppermute | solution.py:361
  6.5 0.0 collective-permute-start.5
  6.6 0.1 stack.20.pos_ref.refs_0_
  6.6 0.0 copy-done.1
  6.7 0.6 %shard_map.132 = bf16[32,384]{1,0:T(8,128)(2,1)S(1)} custom-call(s32[6]{0:T(128)S(1)} %stack.20.pos_ref.refs_0_, s32[4,4,32]{2,1,0:T(4,128)S(1)} %copy-done.4, bf16[64,256]{1,0:T(8,128)(2,1)S(1)} %copy-done.1, f32[32,128]{1,0:T(8,128)S(1)} %shard_map.131.blank_ref), custom_call_target="tpu_custom_call" | custom-call | bytes 1000000 | tf_op jit(solution)/shard_map/pallas_call | solution.py:418
  7.2 0.1 pad_maximum_fusion
  7.3 2.0 %collective-permute-start = (bf16[160,384]{1,0:T(8,128)(2,1)S(1)}, bf16[160,384]{1,0:T(8,128)(2,1)S(1)}, u32[]{:S(2)}, u32[]{:S(2)}) collective-permute-start(bf16[160,384]{1,0:T(8,128)(2,1)S(1)} %get-tuple-element.71), channel_id=1, source_target_pairs={{0,2},{2,0},{4,6},{6,4},{1,3},{3,1},{5,7},{7,5},{8,10},{10,8},{12,... | collective-permute-start | bytes 368648 | tf_op jit(solution)/shard_map/ppermute | solution.py:361
  9.3 1.5 %collective-permute-start.1 = (bf16[160,384]{1,0:T(8,128)(2,1)S(1)}, bf16[160,384]{1,0:T(8,128)(2,1)S(1)}, u32[]{:S(2)}, u32[]{:S(2)}) collective-permute-start(bf16[160,384]{1,0:T(8,128)(2,1)S(1)} %get-tuple-element.72), channel_id=1, source_target_pairs={{0,4},{2,6},{4,0},{6,2},{1,5},{3,7},{5,1},{7,3},{8,12},{10,14},{12... | collective-permute-start | bytes 368648 | tf_op jit(solution)/shard_map/ppermute | solution.py:361
  10.8 0.0 collective-permute-done.3.refs_1_
  10.8 0.5 %collective-permute-start.2 = (bf16[160,384]{1,0:T(8,128)(2,1)S(1)}, bf16[160,384]{1,0:T(8,128)(2,1)S(1)}, u32[]{:S(2)}, u32[]{:S(2)}) collective-permute-start(bf16[160,384]{1,0:T(8,128)(2,1)S(1)} %get-tuple-element.70), channel_id=1, source_target_pairs={{0,6},{2,4},{4,2},{6,0},{1,7},{3,5},{5,3},{7,1},{8,14},{10,12},{12... | collective-permute-start | bytes 368648 | tf_op jit(solution)/shard_map/ppermute | solution.py:361
  11.3 0.0 collective-permute-done.4.refs_2_
  11.3 1.5 %collective-permute-done.5.refs_3_ = bf16[128,384]{1,0:T(8,128)(2,1)S(1)} collective-permute-done((bf16[128,384]{1,0:T(8,128)(2,1)S(1)}, bf16[128,384]{1,0:T(8,128)(2,1)S(1)}, u32[]{:S(2)}, u32[]{:S(2)}) %collective-permute-start.5) | collective-permute-done | bytes 98336 | tf_op jit(solution)/shard_map/ppermute | solution.py:361
  12.9 3.5 %shard_map.133 = (f32[512,384]{1,0:T(8,128)S(1)}, bf16[512,384]{1,0:T(8,128)(2,1)S(1)}) custom-call(s32[6]{0:T(128)S(1)} %stack.20.pos_ref.refs_0_, bf16[128,384]{1,0:T(8,128)(2,1)S(1)} %bitcast.20, bf16[128,384]{1,0:T(8,128)(2,1)S(1)} %collective-permute-done.3.refs_1_, bf16[128,384]{1,0:T(8,128)(2,1)S(1)} %collective-permute-done.4.refs_2_, ...), custom_call_target="tpu_custom_call" | custom-call | flops 1926758400 | bytes 1966080 | tf_op jit(solution)/shard_map/pallas_call | solution.py:440
  16.4 0.0 slice-start.3
  16.4 0.1 collective-permute-start.7
  16.5 0.0 collective-permute-done.refs_1_
  16.5 0.5 %collective-permute-done.1.refs_2_ = bf16[160,384]{1,0:T(8,128)(2,1)S(1)} collective-permute-done((bf16[160,384]{1,0:T(8,128)(2,1)S(1)}, bf16[160,384]{1,0:T(8,128)(2,1)S(1)}, u32[]{:S(2)}, u32[]{:S(2)}) %collective-permute-start.1) | collective-permute-done | bytes 122912 | tf_op jit(solution)/shard_map/ppermute | solution.py:361
  17.0 0.0 collective-permute-done.2.refs_3_
  17.0 2.5 %shard_map.134 = (f32[512,256]{1,0:T(8,128)S(1)}, bf16[512,256]{1,0:T(8,128)(2,1)S(1)}) custom-call(s32[6]{0:T(128)S(1)} %stack.20.pos_ref.refs_0_, bf16[160,384]{1,0:T(8,128)(2,1)S(1)} %get-tuple-element.42.refs_0_, bf16[160,384]{1,0:T(8,128)(2,1)S(1)} %collective-permute-done.refs_1_, bf16[160,384]{1,0:T(8,128)(2,1)S(1)} %collective-permute-done.1.refs_2_, ...), custom_call_target="tpu_custom_call" | custom-call | flops 1926758400 | bytes 1310720 | tf_op jit(solution)/shard_map/pallas_call | solution.py:440
  19.5 0.0 slice-start.1
  19.5 0.0 copy-start.2
  19.5 0.0 copy-start.3
  19.6 0.1 collective-permute-start.8
  19.6 1.5 %shard_map.135 = (f32[512,128]{1,0:T(8,128)S(1)}, bf16[512,128]{1,0:T(8,128)(2,1)S(1)}) custom-call(s32[6]{0:T(128)S(1)} %stack.20.pos_ref.refs_0_, bf16[160,384]{1,0:T(8,128)(2,1)S(1)} %get-tuple-element.42.refs_0_, bf16[160,384]{1,0:T(8,128)(2,1)S(1)} %collective-permute-done.refs_1_, bf16[160,384]{1,0:T(8,128)(2,1)S(1)} %collective-permute-done.1.refs_2_, ...), custom_call_target="tpu_custom_call" | custom-call | flops 1926758400 | bytes 655360 | tf_op jit(solution)/shard_map/pallas_call | solution.py:440
  21.2 0.6 %collective-permute-start.9 = (f32[512,128]{1,0:T(8,128)S(1)}, f32[512,128]{1,0:T(8,128)S(1)}, u32[]{:S(2)}, u32[]{:S(2)}) collective-permute-start(f32[512,128]{1,0:T(8,128)S(1)} %get-tuple-element.41.refs_2_), channel_id=1, source_target_pairs={{0,1},{1,0},{2,3},{3,2},{4,5},{5,4},{6,7},{7,6},{8,9},{9,8},{10,11... | collective-permute-start | bytes 786440 | tf_op jit(solution)/shard_map/ppermute | solution.py:361
  21.7 2.6 %collective-permute-start.6 = (bf16[128,256]{1,0:T(8,128)(2,1)S(1)}, bf16[128,256]{1,0:T(8,128)(2,1)S(1)}, u32[]{:S(2)}, u32[]{:S(2)}) collective-permute-start(bf16[128,256]{1,0:T(8,128)(2,1)S(1)} %shard_map.136.refs_0_), channel_id=1, source_target_pairs={{0,16},{8,24},{16,0},{24,8},{1,17},{9,25},{17,1},{25,9},{2,18},{10... | collective-permute-start | bytes 196616 | tf_op jit(solution)/shard_map/ppermute | solution.py:361
  24.3 0.0 collective-permute-done.9.refs_5_
  24.3 0.0 collective-permute-done.8.refs_4_
  24.3 0.0 collective-permute-done.7.refs_3_
  24.4 0.0 slice-start.4
  24.4 3.9 %shard_map.137.z_ref = f32[256,1536]{1,0:T(8,128)S(1)} custom-call(s32[6]{0:T(128)S(1)} %stack.20.pos_ref.refs_0_, f32[512,384]{1,0:T(8,128)S(1)} %get-tuple-element.37.refs_0_, f32[512,256]{1,0:T(8,128)S(1)} %get-tuple-element.39.refs_1_, f32[512,128]{1,0:T(8,128)S(1)} %get-tuple-element.41.refs_2_, f32[512,384]{1,0:T(8,128)S(1)} %collective-permute-done.7.refs_3_, ...), custom_call_target="tpu_custom_call" | custom-call | flops 2415919104 | bytes 9437184 | tf_op jit(solution)/shard_map/pallas_call | solution.py:476
  28.3 0.0 slice-start.5
  28.3 0.1 collective-permute-start.11
  28.4 0.0 collective-permute-done.6.refs_1_
  28.4 0.0 copy-start
  28.4 3.9 %shard_map.138.z_ref = f32[256,1536]{1,0:T(8,128)S(1)} custom-call(s32[6]{0:T(128)S(1)} %stack.20.pos_ref.refs_0_, f32[512,384]{1,0:T(8,128)S(1)} %get-tuple-element.37.refs_0_, f32[512,256]{1,0:T(8,128)S(1)} %get-tuple-element.39.refs_1_, f32[512,128]{1,0:T(8,128)S(1)} %get-tuple-element.41.refs_2_, f32[512,384]{1,0:T(8,128)S(1)} %collective-permute-done.7.refs_3_, ...), custom_call_target="tpu_custom_call" | custom-call | flops 2415919104 | bytes 9437184 | tf_op jit(solution)/shard_map/pallas_call | solution.py:476
  32.3 0.5 %collective-permute-start.10 = (f32[256,1536]{1,0:T(8,128)S(1)}, f32[256,1536]{1,0:T(8,128)S(1)}, u32[]{:S(2)}, u32[]{:S(2)}) collective-permute-start(f32[256,1536]{1,0:T(8,128)S(1)} %shard_map.138.z_ref), channel_id=1, source_target_pairs={{0,1},{1,0},{2,3},{3,2},{4,5},{5,4},{6,7},{7,6},{8,9},{9,8},{10,11... | collective-permute-start | bytes 4718600 | tf_op jit(solution)/shard_map/ppermute | solution.py:361
  32.8 1.6 %collective-permute-start.16 = (bf16[256,256]{1,0:T(8,128)(2,1)S(1)}, bf16[256,256]{1,0:T(8,128)(2,1)S(1)}, u32[]{:S(2)}, u32[]{:S(2)}) collective-permute-start(bf16[256,256]{1,0:T(8,128)(2,1)S(1)} %shard_map.144), channel_id=1, source_target_pairs={{0,8},{8,0},{16,24},{24,16},{1,9},{9,1},{17,25},{25,17},{2,10},{10... | collective-permute-start | bytes 393224 | tf_op jit(solution)/shard_map/ppermute | solution.py:361
  34.5 0.0 collective-permute-done.11.other_ref
  34.5 1.0 %shard_map.139.first_ref = bf16[256,1024]{1,0:T(8,128)(2,1)S(1)} custom-call(f32[256,1536]{1,0:T(8,128)S(1)} %shard_map.137.z_ref, f32[256,1536]{1,0:T(8,128)S(1)} %collective-permute-done.11.other_ref, bf16[1536,1024]{1,0:T(8,128)(2,1)S(1)} %copy-done), custom_call_target="tpu_custom_call" | custom-call | flops 805306368 | bytes 3145728 | tf_op jit(solution)/shard_map/pallas_call | solution.py:495
  35.5 0.9 %shard_map.140.hot_ref = bf16[576,512]{1,0:T(8,128)(2,1)S(1)} custom-call(s32[6]{0:T(128)S(1)} %stack.20.pos_ref.refs_0_, bf16[160,384]{1,0:T(8,128)(2,1)S(1)} %get-tuple-element.42.refs_0_, bf16[160,384]{1,0:T(8,128)(2,1)S(1)} %collective-permute-done.refs_1_, bf16[160,384]{1,0:T(8,128)(2,1)S(1)} %collective-permute-done.1.refs_2_, ...), custom_call_target="tpu_custom_call" | custom-call | flops 100000000 | bytes 1000000 | tf_op jit(solution)/shard_map/pallas_call | solution.py:504
  36.3 0.0 copy-start.5
  36.4 0.0 copy-start.6
  36.4 0.0 collective-permute-done.10.other_ref
  36.4 2.9 %shard_map.141.a_ref = f32[64,256]{1,0:T(8,128)S(1)} custom-call(f32[256,1536]{1,0:T(8,128)S(1)} %shard_map.138.z_ref, f32[256,1536]{1,0:T(8,128)S(1)} %collective-permute-done.10.other_ref, bf16[256,1024]{1,0:T(8,128)(2,1)S(1)} %shard_map.139.first_ref, bf16[1536,1024]{1,0:T(8,128)(2,1)S(1)} %copy-done, bf16[9,1024,256]{2,1,0:T(8,128)(2,1)S(1)} %bitcast.18, ...), custom_call_target="tpu_custom_call" | custom-call | flops 2013265920 | bytes 6291456 | tf_op jit(solution)/shard_map/pallas_call | solution.py:513
  39.3 0.0 collective-permute-done.16.refs_2_
  39.3 0.1 collective-permute-start.17
  39.4 0.5 %collective-permute-start.12 = (f32[64,256]{1,0:T(8,128)S(1)}, f32[64,256]{1,0:T(8,128)S(1)}, u32[]{:S(2)}, u32[]{:S(2)}) collective-permute-start(f32[64,256]{1,0:T(8,128)S(1)} %shard_map.141.a_ref), channel_id=1, source_target_pairs={{0,1},{1,0},{2,3},{3,2},{4,5},{5,4},{6,7},{7,6},{8,9},{9,8},{10,11... | collective-permute-start | bytes 196616 | tf_op jit(solution)/shard_map/ppermute | solution.py:361
  39.9 1.0 %shard_map.143 = (bf16[64,256]{1,0:T(8,128)(2,1)S(1)}, f32[64,128]{1,0:T(8,128)S(1)}) custom-call(s32[6]{0:T(128)S(1)} %stack.20.pos_ref.refs_0_, bf16[160,384]{1,0:T(8,128)(2,1)S(1)} %get-tuple-element.42.refs_0_, bf16[160,384]{1,0:T(8,128)(2,1)S(1)} %collective-permute-done.refs_1_, bf16[160,384]{1,0:T(8,128)(2,1)S(1)} %collective-permute-done.1.refs_2_, ...), custom_call_target="tpu_custom_call" | custom-call | flops 100000000 | bytes 1000000 | tf_op jit(solution)/shard_map/pallas_call | solution.py:525
  40.9 0.1 collective-permute-done.12.b_ref
  41.0 1.0 %collective-permute-start.13 = (bf16[64,256]{1,0:T(8,128)(2,1)S(1)}, bf16[64,256]{1,0:T(8,128)(2,1)S(1)}, u32[]{:S(2)}, u32[]{:S(2)}) collective-permute-start(bf16[64,256]{1,0:T(8,128)(2,1)S(1)} %get-tuple-element.53), channel_id=1, source_target_pairs={{0,2},{2,0},{4,6},{6,4},{1,3},{3,1},{5,7},{7,5},{8,10},{10,8},{12,... | collective-permute-start | bytes 98312 | tf_op jit(solution)/shard_map/ppermute | solution.py:361
  42.0 1.0 %collective-permute-start.14 = (bf16[64,256]{1,0:T(8,128)(2,1)S(1)}, bf16[64,256]{1,0:T(8,128)(2,1)S(1)}, u32[]{:S(2)}, u32[]{:S(2)}) collective-permute-start(bf16[64,256]{1,0:T(8,128)(2,1)S(1)} %get-tuple-element.53), channel_id=1, source_target_pairs={{0,4},{2,6},{4,0},{6,2},{1,5},{3,7},{5,1},{7,3},{8,12},{10,14},{12... | collective-permute-start | bytes 98312 | tf_op jit(solution)/shard_map/ppermute | solution.py:361
  43.0 1.6 %collective-permute-start.15 = (bf16[64,256]{1,0:T(8,128)(2,1)S(1)}, bf16[64,256]{1,0:T(8,128)(2,1)S(1)}, u32[]{:S(2)}, u32[]{:S(2)}) collective-permute-start(bf16[64,256]{1,0:T(8,128)(2,1)S(1)} %get-tuple-element.53), channel_id=1, source_target_pairs={{0,6},{2,4},{4,2},{6,0},{1,7},{3,5},{5,3},{7,1},{8,14},{10,12},{12... | collective-permute-start | bytes 98312 | tf_op jit(solution)/shard_map/ppermute | solution.py:361
  44.6 0.0 collective-permute-done.17.refs_3_
  44.6 0.2 shard_map.146
  44.8 0.2 collective-permute-done.13.refs_2_
  45.0 1.0 %collective-permute-done.14.refs_3_ = bf16[64,256]{1,0:T(8,128)(2,1)S(1)} collective-permute-done((bf16[64,256]{1,0:T(8,128)(2,1)S(1)}, bf16[64,256]{1,0:T(8,128)(2,1)S(1)}, u32[]{:S(2)}, u32[]{:S(2)}) %collective-permute-start.14) | collective-permute-done | bytes 32800 | tf_op jit(solution)/shard_map/ppermute | solution.py:361
  46.0 1.9 %collective-permute-done.15.refs_4_ = bf16[64,256]{1,0:T(8,128)(2,1)S(1)} collective-permute-done((bf16[64,256]{1,0:T(8,128)(2,1)S(1)}, bf16[64,256]{1,0:T(8,128)(2,1)S(1)}, u32[]{:S(2)}, u32[]{:S(2)}) %collective-permute-start.15) | collective-permute-done | bytes 32800 | tf_op jit(solution)/shard_map/ppermute | solution.py:361
  47.8 1.8 %shard_map.147 = (f32[64,256]{1,0:T(8,128)}, f32[1,64]{1,0:T(1,128)}) custom-call(s32[6]{0:T(128)S(1)} %stack.20.pos_ref.refs_0_, f32[64,256]{1,0:T(8,128)S(1)} %get-tuple-element.52.refs_1_, bf16[64,256]{1,0:T(8,128)(2,1)S(1)} %collective-permute-done.13.refs_2_, bf16[64,256]{1,0:T(8,128)(2,1)S(1)} %collective-permute-done.14.refs_3_, ...), custom_call_target="tpu_custom_call" | custom-call | flops 100000000 | bytes 1000000 | tf_op jit(solution)/shard_map/pallas_call | solution.py:557
  (23 shorter events, 0.1 us)
Async XLA Ops:
  2.0 4.7 %copy-start.1 = (bf16[64,256]{1,0:T(8,128)(2,1)S(1)}, bf16[64,256]{1,0:T(8,128)(2,1)}, u32[]{:S(2)}) copy-start(bf16[64,256]{1,0:T(8,128)(2,1)} %key_ref.1) | copy-start | bytes 98308
  2.0 4.7 %copy-start.4 = (s32[4,4,32]{2,1,0:T(4,128)S(1)}, s32[4,4,32]{2,1,0:T(4,128)}, u32[]{:S(2)}) copy-start(s32[4,4,32]{2,1,0:T(4,128)} %ids_ref.1) | copy-start | bytes 6148
  2.0 10.9 %copy-start.7 = (bf16[7,7,1536]{2,1,0:T(8,128)(2,1)S(1)}, bf16[7,7,1536]{2,1,0:T(8,128)(2,1)}, u32[]{:S(2)}) copy-start(bf16[7,7,1536]{2,1,0:T(8,128)(2,1)} %refs_4_.6) | copy-start | bytes 451588
  2.0 8.8 %collective-permute-start.3 = (bf16[128,384]{1,0:T(8,128)(2,1)S(1)}, bf16[128,384]{1,0:T(8,128)(2,1)S(1)}, u32[]{:S(2)}, u32[]{:S(2)}) collective-permute-start(bf16[128,384]{1,0:T(8,128)(2,1)S(1)} %bitcast.27), channel_id=1, source_target_pairs={{0,2},{2,0},{4,6},{6,4},{1,3},{3,1},{5,7},{7,5},{8,10},{10,8},{12,... | collective-permute-start | bytes 294920 | tf_op jit(solution)/shard_map/ppermute | solution.py:361
  5.0 6.3 %collective-permute-start.4 = (bf16[128,384]{1,0:T(8,128)(2,1)S(1)}, bf16[128,384]{1,0:T(8,128)(2,1)S(1)}, u32[]{:S(2)}, u32[]{:S(2)}) collective-permute-start(bf16[128,384]{1,0:T(8,128)(2,1)S(1)} %bitcast.26), channel_id=1, source_target_pairs={{0,4},{2,6},{4,0},{6,2},{1,5},{3,7},{5,1},{7,3},{8,12},{10,14},{12... | collective-permute-start | bytes 294920 | tf_op jit(solution)/shard_map/ppermute | solution.py:361
  6.5 6.3 %collective-permute-start.5 = (bf16[128,384]{1,0:T(8,128)(2,1)S(1)}, bf16[128,384]{1,0:T(8,128)(2,1)S(1)}, u32[]{:S(2)}, u32[]{:S(2)}) collective-permute-start(bf16[128,384]{1,0:T(8,128)(2,1)S(1)} %bitcast.25), channel_id=1, source_target_pairs={{0,6},{2,4},{4,2},{6,0},{1,7},{3,5},{5,3},{7,1},{8,14},{10,12},{12... | collective-permute-start | bytes 294920 | tf_op jit(solution)/shard_map/ppermute | solution.py:361
  7.3 9.2 %collective-permute-start = (bf16[160,384]{1,0:T(8,128)(2,1)S(1)}, bf16[160,384]{1,0:T(8,128)(2,1)S(1)}, u32[]{:S(2)}, u32[]{:S(2)}) collective-permute-start(bf16[160,384]{1,0:T(8,128)(2,1)S(1)} %get-tuple-element.71), channel_id=1, source_target_pairs={{0,2},{2,0},{4,6},{6,4},{1,3},{3,1},{5,7},{7,5},{8,10},{10,8},{12,... | collective-permute-start | bytes 368648 | tf_op jit(solution)/shard_map/ppermute | solution.py:361
  9.3 7.7 %collective-permute-start.1 = (bf16[160,384]{1,0:T(8,128)(2,1)S(1)}, bf16[160,384]{1,0:T(8,128)(2,1)S(1)}, u32[]{:S(2)}, u32[]{:S(2)}) collective-permute-start(bf16[160,384]{1,0:T(8,128)(2,1)S(1)} %get-tuple-element.72), channel_id=1, source_target_pairs={{0,4},{2,6},{4,0},{6,2},{1,5},{3,7},{5,1},{7,3},{8,12},{10,14},{12... | collective-permute-start | bytes 368648 | tf_op jit(solution)/shard_map/ppermute | solution.py:361
  10.8 6.2 %collective-permute-start.2 = (bf16[160,384]{1,0:T(8,128)(2,1)S(1)}, bf16[160,384]{1,0:T(8,128)(2,1)S(1)}, u32[]{:S(2)}, u32[]{:S(2)}) collective-permute-start(bf16[160,384]{1,0:T(8,128)(2,1)S(1)} %get-tuple-element.70), channel_id=1, source_target_pairs={{0,6},{2,4},{4,2},{6,0},{1,7},{3,5},{5,3},{7,1},{8,14},{10,12},{12... | collective-permute-start | bytes 368648 | tf_op jit(solution)/shard_map/ppermute | solution.py:361
  12.9 11.4 %slice-start.2 = ((s8[4718592]{0:T(1024)(128)(4,1)}), s8[4194304]{0:T(1024)(128)(4,1)S(1)}, s32[]{:S(2)}) async-start(s8[4718592]{0:T(1024)(128)(4,1)} %bitcast.15), calls=%async_computation.2 | async-start | bytes 8388608
  16.4 8.0 %slice-start.3 = ((s8[4718592]{0:T(1024)(128)(4,1)}), s8[524288]{0:T(1024)(128)(4,1)S(1)}, s32[]{:S(2)}) async-start(s8[4718592]{0:T(1024)(128)(4,1)} %bitcast.15), calls=%async_computation.3 | async-start | bytes 1048576
  16.4 7.9 %collective-permute-start.7 = (f32[512,384]{1,0:T(8,128)S(1)}, f32[512,384]{1,0:T(8,128)S(1)}, u32[]{:S(2)}, u32[]{:S(2)}) collective-permute-start(f32[512,384]{1,0:T(8,128)S(1)} %get-tuple-element.37.refs_0_), channel_id=1, source_target_pairs={{0,1},{1,0},{2,3},{3,2},{4,5},{5,4},{6,7},{7,6},{8,9},{9,8},{10,11... | collective-permute-start | bytes 2359304 | tf_op jit(solution)/shard_map/ppermute | solution.py:361
  17.0 7.3 %slice-start = ((s8[4718592]{0:T(1024)(128)(4,1)}), s8[4194304]{0:T(1024)(128)(4,1)S(1)}, s32[]{:S(2)}) async-start(s8[4718592]{0:T(1024)(128)(4,1)} %bitcast.13), calls=%async_computation | async-start | bytes 8388608
  19.5 4.8 %slice-start.1 = ((s8[4718592]{0:T(1024)(128)(4,1)}), s8[524288]{0:T(1024)(128)(4,1)S(1)}, s32[]{:S(2)}) async-start(s8[4718592]{0:T(1024)(128)(4,1)} %bitcast.13), calls=%async_computation.1 | async-start | bytes 1048576
  19.5 4.8 %copy-start.2 = (bf16[1536]{0:T(1024)(128)(2,1)S(1)}, bf16[1536]{0:T(1024)(128)(2,1)}, u32[]{:S(2)}) copy-start(bf16[1536]{0:T(1024)(128)(2,1)} %refs_9_.3) | copy-start | bytes 9220
  19.5 4.8 %copy-start.3 = (bf16[1536]{0:T(1024)(128)(2,1)S(1)}, bf16[1536]{0:T(1024)(128)(2,1)}, u32[]{:S(2)}) copy-start(bf16[1536]{0:T(1024)(128)(2,1)} %refs_10_.3) | copy-start | bytes 9220
  19.6 4.8 %collective-permute-start.8 = (f32[512,256]{1,0:T(8,128)S(1)}, f32[512,256]{1,0:T(8,128)S(1)}, u32[]{:S(2)}, u32[]{:S(2)}) collective-permute-start(f32[512,256]{1,0:T(8,128)S(1)} %get-tuple-element.39.refs_1_), channel_id=1, source_target_pairs={{0,1},{1,0},{2,3},{3,2},{4,5},{5,4},{6,7},{7,6},{8,9},{9,8},{10,11... | collective-permute-start | bytes 1572872 | tf_op jit(solution)/shard_map/ppermute | solution.py:361
  21.2 3.2 %collective-permute-start.9 = (f32[512,128]{1,0:T(8,128)S(1)}, f32[512,128]{1,0:T(8,128)S(1)}, u32[]{:S(2)}, u32[]{:S(2)}) collective-permute-start(f32[512,128]{1,0:T(8,128)S(1)} %get-tuple-element.41.refs_2_), channel_id=1, source_target_pairs={{0,1},{1,0},{2,3},{3,2},{4,5},{5,4},{6,7},{7,6},{8,9},{9,8},{10,11... | collective-permute-start | bytes 786440 | tf_op jit(solution)/shard_map/ppermute | solution.py:361
  21.7 6.7 %collective-permute-start.6 = (bf16[128,256]{1,0:T(8,128)(2,1)S(1)}, bf16[128,256]{1,0:T(8,128)(2,1)S(1)}, u32[]{:S(2)}, u32[]{:S(2)}) collective-permute-start(bf16[128,256]{1,0:T(8,128)(2,1)S(1)} %shard_map.136.refs_0_), channel_id=1, source_target_pairs={{0,16},{8,24},{16,0},{24,8},{1,17},{9,25},{17,1},{25,9},{2,18},{10... | collective-permute-start | bytes 196616 | tf_op jit(solution)/shard_map/ppermute | solution.py:361
  24.4 12.0 %slice-start.4 = ((s8[4718592]{0:T(1024)(128)(4,1)}), s8[4194304]{0:T(1024)(128)(4,1)S(1)}, s32[]{:S(2)}) async-start(s8[4718592]{0:T(1024)(128)(4,1)} %bitcast.17), calls=%async_computation.4 | async-start | bytes 8388608
  28.3 8.1 %slice-start.5 = ((s8[4718592]{0:T(1024)(128)(4,1)}), s8[524288]{0:T(1024)(128)(4,1)S(1)}, s32[]{:S(2)}) async-start(s8[4718592]{0:T(1024)(128)(4,1)} %bitcast.17), calls=%async_computation.5 | async-start | bytes 1048576
  28.3 6.2 %collective-permute-start.11 = (f32[256,1536]{1,0:T(8,128)S(1)}, f32[256,1536]{1,0:T(8,128)S(1)}, u32[]{:S(2)}, u32[]{:S(2)}) collective-permute-start(f32[256,1536]{1,0:T(8,128)S(1)} %shard_map.137.z_ref), channel_id=1, source_target_pairs={{0,1},{1,0},{2,3},{3,2},{4,5},{5,4},{6,7},{7,6},{8,9},{9,8},{10,11... | collective-permute-start | bytes 4718600 | tf_op jit(solution)/shard_map/ppermute | solution.py:361
  28.4 6.1 %copy-start = (bf16[1536,1024]{1,0:T(8,128)(2,1)S(1)}, bf16[1536,1024]{1,0:T(8,128)(2,1)}, u32[]{:S(2)}) copy-start(bf16[1536,1024]{1,0:T(8,128)(2,1)} %pe_ref.3) | copy-start | bytes 9437188
  32.3 4.1 %collective-permute-start.10 = (f32[256,1536]{1,0:T(8,128)S(1)}, f32[256,1536]{1,0:T(8,128)S(1)}, u32[]{:S(2)}, u32[]{:S(2)}) collective-permute-start(f32[256,1536]{1,0:T(8,128)S(1)} %shard_map.138.z_ref), channel_id=1, source_target_pairs={{0,1},{1,0},{2,3},{3,2},{4,5},{5,4},{6,7},{7,6},{8,9},{9,8},{10,11... | collective-permute-start | bytes 4718600 | tf_op jit(solution)/shard_map/ppermute | solution.py:361
  32.8 6.4 %collective-permute-start.16 = (bf16[256,256]{1,0:T(8,128)(2,1)S(1)}, bf16[256,256]{1,0:T(8,128)(2,1)S(1)}, u32[]{:S(2)}, u32[]{:S(2)}) collective-permute-start(bf16[256,256]{1,0:T(8,128)(2,1)S(1)} %shard_map.144), channel_id=1, source_target_pairs={{0,8},{8,0},{16,24},{24,16},{1,9},{9,1},{17,25},{25,17},{2,10},{10... | collective-permute-start | bytes 393224 | tf_op jit(solution)/shard_map/ppermute | solution.py:361
  36.3 3.5 %copy-start.5 = (s32[4,64]{1,0:T(4,128)S(1)}, s32[4,64]{1,0:T(4,128)}, u32[]{:S(2)}) copy-start(s32[4,64]{1,0:T(4,128)} %refs_5_.1) | copy-start | bytes 3076
  36.4 3.5 %copy-start.6 = (s32[1,256]{1,0:T(1,128)S(1)}, s32[1,256]{1,0:T(1,128)}, u32[]{:S(2)}) copy-start(s32[1,256]{1,0:T(1,128)} %refs_4_.7) | copy-start | bytes 3076
  39.3 5.3 %collective-permute-start.17 = (bf16[512,256]{1,0:T(8,128)(2,1)S(1)}, bf16[512,256]{1,0:T(8,128)(2,1)S(1)}, u32[]{:S(2)}, u32[]{:S(2)}) collective-permute-start(bf16[512,256]{1,0:T(8,128)(2,1)S(1)} %shard_map.145), channel_id=1, source_target_pairs={{0,1},{1,0},{2,3},{3,2},{4,5},{5,4},{6,7},{7,6},{8,9},{9,8},{10,11... | collective-permute-start | bytes 786440 | tf_op jit(solution)/shard_map/ppermute | solution.py:361
  39.4 1.6 %collective-permute-start.12 = (f32[64,256]{1,0:T(8,128)S(1)}, f32[64,256]{1,0:T(8,128)S(1)}, u32[]{:S(2)}, u32[]{:S(2)}) collective-permute-start(f32[64,256]{1,0:T(8,128)S(1)} %shard_map.141.a_ref), channel_id=1, source_target_pairs={{0,1},{1,0},{2,3},{3,2},{4,5},{5,4},{6,7},{7,6},{8,9},{9,8},{10,11... | collective-permute-start | bytes 196616 | tf_op jit(solution)/shard_map/ppermute | solution.py:361
  41.0 4.0 %collective-permute-start.13 = (bf16[64,256]{1,0:T(8,128)(2,1)S(1)}, bf16[64,256]{1,0:T(8,128)(2,1)S(1)}, u32[]{:S(2)}, u32[]{:S(2)}) collective-permute-start(bf16[64,256]{1,0:T(8,128)(2,1)S(1)} %get-tuple-element.53), channel_id=1, source_target_pairs={{0,2},{2,0},{4,6},{6,4},{1,3},{3,1},{5,7},{7,5},{8,10},{10,8},{12,... | collective-permute-start | bytes 98312 | tf_op jit(solution)/shard_map/ppermute | solution.py:361
  42.0 3.9 %collective-permute-start.14 = (bf16[64,256]{1,0:T(8,128)(2,1)S(1)}, bf16[64,256]{1,0:T(8,128)(2,1)S(1)}, u32[]{:S(2)}, u32[]{:S(2)}) collective-permute-start(bf16[64,256]{1,0:T(8,128)(2,1)S(1)} %get-tuple-element.53), channel_id=1, source_target_pairs={{0,4},{2,6},{4,0},{6,2},{1,5},{3,7},{5,1},{7,3},{8,12},{10,14},{12... | collective-permute-start | bytes 98312 | tf_op jit(solution)/shard_map/ppermute | solution.py:361
  43.0 4.8 %collective-permute-start.15 = (bf16[64,256]{1,0:T(8,128)(2,1)S(1)}, bf16[64,256]{1,0:T(8,128)(2,1)S(1)}, u32[]{:S(2)}, u32[]{:S(2)}) collective-permute-start(bf16[64,256]{1,0:T(8,128)(2,1)S(1)} %get-tuple-element.53), channel_id=1, source_target_pairs={{0,6},{2,4},{4,2},{6,0},{1,7},{3,5},{5,3},{7,1},{8,14},{10,12},{12... | collective-permute-start | bytes 98312 | tf_op jit(solution)/shard_map/ppermute | solution.py:361

commit v4 on v2

--- a/solution.py
+++ b/solution.py
@@ -305,7 +305,7 @@
     pixels = z_ref.shape[0]
     taps = pk_ref.shape[0]
     block[...] = (z_ref[...] + other_ref[...]).astype(bf16)
-    step = 256
+    step = 512
     acc = jnp.zeros((2 * REG, out_ref.shape[1]), f32)
     for i in range(pe_ref.shape[1] // step):
         cols = slice(i * step, (i + 1) * step)
@@ -514,7 +514,7 @@
         [VMEM] * 6,
         [
             pltpu.VMEM((part_pixels, chans), bf16),
-            pltpu.VMEM((hidden // 256, out_pixels, 256), bf16),
+            pltpu.VMEM((hidden // 512, out_pixels, 512), bf16),
         ],
         8 * mib,
         2 * part_pixels * hidden * chans + 4 * 9 * REG * hidden * out_pixels,

time: 48.6 us -> 48.6 us (level)
  no operation moved by 1% of the time
where the time goes in v4:
time: 48.6 us; the launch traced here: 48.4 us
  Pallas kernels  22.9 us (47%)
  starting transfers between devices  17.8 us (37%)
  waiting for transfers between devices  5.24 us (11%)
  local copies, waits for them, and re-layouts  1.48 us (3%)
  between operations  0.98 us (2%)
    ppermute x17, starting transfers between devices, swap(): lax.ppermute(x, axis, [(i, i ^ bit) for i in range(lax.axis_size(axis))])  17.8 us
    pallas_call x2, Pallas kernels, body(): call(functools.partial(block_kernel, (p * part_pixels, part_pixels, [w fo...  7.62 us
    pallas_call x2, Pallas kernels, body(): call(functools.partial(conv_kernel, (order, shard_rows, width, out_rows,...  6.96 us
    ppermute x17, waiting for transfers between devices, swap(): lax.ppermute(x, axis, [(i, i ^ bit) for i in range(lax.axis_size(axis))])  5.24 us
    pallas_call x1, Pallas kernels, body(): call(project_kernel, [jax.ShapeDtypeStruct((REG, out_dim), f32)], [VMEM]...  2.88 us
    pallas_call x1, Pallas kernels, body(): call(functools.partial(loss_kernel, (shards, parts)), [jax.ShapeDtypeStru...  1.78 us
    dynamic_slice x1, local copies, waits for them, and re-layouts, body(): part = lax.dynamic_slice(features, place, (1, shard_rows, width, span))  1.32 us
    pallas_call x1, Pallas kernels, body(): call(expand_kernel, [jax.ShapeDtypeStruct((part_pixels, hidden), bf16)],...  0.98 us
  transfers between devices with their start and end apart: 17, of which 6 were waited for; matrix products, arithmetic and copies ran while one was open for 0% of the time, Pallas kernels for 44%

profile of v4, /device:TPU:0, one launch (start us, length us, event | category | flops | bytes accessed | tf_op | source)
XLA Modules:
  0.0 48.4 jit_solution(10412850247487471581)
XLA Ops:
  0.7 1.3 %constant_dynamic-slice_fusion = (bf16[1,4,32,384]{3,2,1,0:T(8,128)(2,1)S(1)}, bf16[1,4,32,384]{3,2,1,0:T(8,128)(2,1)S(1)}, bf16[1,4,32,384]{3,2,1,0:T(8,128)(2,...) fusion(bf16[4,4,32,1536]{3,2,1,0:T(8,128)(2,1)} %param.12, ...), kind=kLoop, calls=%fused_computation.4 | loop fusion | bytes 1572888 | tf_op jit(solution)/shard_map/dynamic_slice | solution.py:411
  2.0 0.0 copy-start.1
  2.0 0.0 copy-start.4
  2.0 0.0 copy-start.7
  2.0 3.0 %collective-permute-start.3 = (bf16[128,384]{1,0:T(8,128)(2,1)S(1)}, bf16[128,384]{1,0:T(8,128)(2,1)S(1)}, u32[]{:S(2)}, u32[]{:S(2)}) collective-permute-start(bf16[128,384]{1,0:T(8,128)(2,1)S(1)} %bitcast.27), channel_id=1, source_target_pairs={{0,2},{2,0},{4,6},{6,4},{1,3},{3,1},{5,7},{7,5},{8,10},{10,8},{12,... | collective-permute-start | bytes 294920 | tf_op jit(solution)/shard_map/ppermute | solution.py:361
  5.0 1.5 %collective-permute-start.4 = (bf16[128,384]{1,0:T(8,128)(2,1)S(1)}, bf16[128,384]{1,0:T(8,128)(2,1)S(1)}, u32[]{:S(2)}, u32[]{:S(2)}) collective-permute-start(bf16[128,384]{1,0:T(8,128)(2,1)S(1)} %bitcast.26), channel_id=1, source_target_pairs={{0,4},{2,6},{4,0},{6,2},{1,5},{3,7},{5,1},{7,3},{8,12},{10,14},{12... | collective-permute-start | bytes 294920 | tf_op jit(solution)/shard_map/ppermute | solution.py:361
  6.5 0.0 collective-permute-start.5
  6.6 0.1 stack.20.pos_ref.refs_0_
  6.6 0.0 copy-done.1
  6.7 0.0 copy-done.4
  6.7 0.6 %shard_map.132 = bf16[32,384]{1,0:T(8,128)(2,1)S(1)} custom-call(s32[6]{0:T(128)S(1)} %stack.20.pos_ref.refs_0_, s32[4,4,32]{2,1,0:T(4,128)S(1)} %copy-done.4, bf16[64,256]{1,0:T(8,128)(2,1)S(1)} %copy-done.1, f32[32,128]{1,0:T(8,128)S(1)} %shard_map.131.blank_ref), custom_call_target="tpu_custom_call" | custom-call | bytes 1000000 | tf_op jit(solution)/shard_map/pallas_call | solution.py:418
  7.2 0.0 slice-start.2
  7.2 0.1 pad_maximum_fusion
  7.3 2.0 %collective-permute-start = (bf16[160,384]{1,0:T(8,128)(2,1)S(1)}, bf16[160,384]{1,0:T(8,128)(2,1)S(1)}, u32[]{:S(2)}, u32[]{:S(2)}) collective-permute-start(bf16[160,384]{1,0:T(8,128)(2,1)S(1)} %get-tuple-element.63), channel_id=1, source_target_pairs={{0,2},{2,0},{4,6},{6,4},{1,3},{3,1},{5,7},{7,5},{8,10},{10,8},{12,... | collective-permute-start | bytes 368648 | tf_op jit(solution)/shard_map/ppermute | solution.py:361
  9.3 1.5 %collective-permute-start.1 = (bf16[160,384]{1,0:T(8,128)(2,1)S(1)}, bf16[160,384]{1,0:T(8,128)(2,1)S(1)}, u32[]{:S(2)}, u32[]{:S(2)}) collective-permute-start(bf16[160,384]{1,0:T(8,128)(2,1)S(1)} %get-tuple-element.64), channel_id=1, source_target_pairs={{0,4},{2,6},{4,0},{6,2},{1,5},{3,7},{5,1},{7,3},{8,12},{10,14},{12... | collective-permute-start | bytes 368648 | tf_op jit(solution)/shard_map/ppermute | solution.py:361
  10.8 0.0 collective-permute-done.3.refs_1_
  10.8 0.5 %collective-permute-start.2 = (bf16[160,384]{1,0:T(8,128)(2,1)S(1)}, bf16[160,384]{1,0:T(8,128)(2,1)S(1)}, u32[]{:S(2)}, u32[]{:S(2)}) collective-permute-start(bf16[160,384]{1,0:T(8,128)(2,1)S(1)} %get-tuple-element.62), channel_id=1, source_target_pairs={{0,6},{2,4},{4,2},{6,0},{1,7},{3,5},{5,3},{7,1},{8,14},{10,12},{12... | collective-permute-start | bytes 368648 | tf_op jit(solution)/shard_map/ppermute | solution.py:361
  11.3 0.0 collective-permute-done.4.refs_2_
  11.3 1.5 %collective-permute-done.5.refs_3_ = bf16[128,384]{1,0:T(8,128)(2,1)S(1)} collective-permute-done((bf16[128,384]{1,0:T(8,128)(2,1)S(1)}, bf16[128,384]{1,0:T(8,128)(2,1)S(1)}, u32[]{:S(2)}, u32[]{:S(2)}) %collective-permute-start.5) | collective-permute-done | bytes 98336 | tf_op jit(solution)/shard_map/ppermute | solution.py:361
  12.9 3.5 %shard_map.133 = (f32[512,384]{1,0:T(8,128)S(1)}, bf16[512,384]{1,0:T(8,128)(2,1)S(1)}) custom-call(s32[6]{0:T(128)S(1)} %stack.20.pos_ref.refs_0_, bf16[128,384]{1,0:T(8,128)(2,1)S(1)} %bitcast.20, bf16[128,384]{1,0:T(8,128)(2,1)S(1)} %collective-permute-done.3.refs_1_, bf16[128,384]{1,0:T(8,128)(2,1)S(1)} %collective-permute-done.4.refs_2_, ...), custom_call_target="tpu_custom_call" | custom-call | flops 1926758400 | bytes 1966080 | tf_op jit(solution)/shard_map/pallas_call | solution.py:438
  16.4 0.1 collective-permute-start.7
  16.4 0.0 collective-permute-done.refs_1_
  16.5 0.6 %collective-permute-done.1.refs_2_ = bf16[160,384]{1,0:T(8,128)(2,1)S(1)} collective-permute-done((bf16[160,384]{1,0:T(8,128)(2,1)S(1)}, bf16[160,384]{1,0:T(8,128)(2,1)S(1)}, u32[]{:S(2)}, u32[]{:S(2)}) %collective-permute-start.1) | collective-permute-done | bytes 122912 | tf_op jit(solution)/shard_map/ppermute | solution.py:361
  17.0 0.0 collective-permute-done.2.refs_3_
  17.0 3.5 %shard_map.134 = (f32[512,384]{1,0:T(8,128)S(1)}, bf16[512,384]{1,0:T(8,128)(2,1)S(1)}) custom-call(s32[6]{0:T(128)S(1)} %stack.20.pos_ref.refs_0_, bf16[160,384]{1,0:T(8,128)(2,1)S(1)} %get-tuple-element.35.refs_0_, bf16[160,384]{1,0:T(8,128)(2,1)S(1)} %collective-permute-done.refs_1_, bf16[160,384]{1,0:T(8,128)(2,1)S(1)} %collective-permute-done.1.refs_2_, ...), custom_call_target="tpu_custom_call" | custom-call | flops 1926758400 | bytes 1966080 | tf_op jit(solution)/shard_map/pallas_call | solution.py:438
  20.5 0.1 collective-permute-start.8
  20.6 2.7 %collective-permute-start.6 = (bf16[128,256]{1,0:T(8,128)(2,1)S(1)}, bf16[128,256]{1,0:T(8,128)(2,1)S(1)}, u32[]{:S(2)}, u32[]{:S(2)}) collective-permute-start(bf16[128,256]{1,0:T(8,128)(2,1)S(1)} %shard_map.135.refs_0_), channel_id=1, source_target_pairs={{0,16},{8,24},{16,0},{24,8},{1,17},{9,25},{17,1},{25,9},{2,18},{10... | collective-permute-start | bytes 196616 | tf_op jit(solution)/shard_map/ppermute | solution.py:361
  23.3 0.0 collective-permute-done.7.refs_2_
  23.3 0.0 collective-permute-done.8.refs_3_
  23.3 0.0 slice-done.3
  23.3 0.0 slice-done
  23.3 0.0 slice-done.1
  23.3 0.0 copy-done.2
  23.3 0.0 copy-done.3
  23.3 0.0 slice-start.4
  23.4 3.8 %shard_map.136.z_ref = f32[256,1536]{1,0:T(8,128)S(1)} custom-call(s32[6]{0:T(128)S(1)} %stack.20.pos_ref.refs_0_, f32[512,384]{1,0:T(8,128)S(1)} %get-tuple-element.32.refs_0_, f32[512,384]{1,0:T(8,128)S(1)} %get-tuple-element.34.refs_1_, f32[512,384]{1,0:T(8,128)S(1)} %collective-permute-done.7.refs_2_, f32[512,384]{1,0:T(8,128)S(1)} %collective-permute-done.8.refs_3_, ...), custom_call_target="tpu_custom_call" | custom-call | flops 2415919104 | bytes 9437184 | tf_op jit(solution)/shard_map/pallas_call | solution.py:474
  27.2 0.0 slice-start.5
  27.2 0.2 collective-permute-start.10
  27.4 0.0 collective-permute-done.6.refs_1_
  27.4 3.8 %shard_map.137.z_ref = f32[256,1536]{1,0:T(8,128)S(1)} custom-call(s32[6]{0:T(128)S(1)} %stack.20.pos_ref.refs_0_, f32[512,384]{1,0:T(8,128)S(1)} %get-tuple-element.32.refs_0_, f32[512,384]{1,0:T(8,128)S(1)} %get-tuple-element.34.refs_1_, f32[512,384]{1,0:T(8,128)S(1)} %collective-permute-done.7.refs_2_, f32[512,384]{1,0:T(8,128)S(1)} %collective-permute-done.8.refs_3_, ...), custom_call_target="tpu_custom_call" | custom-call | flops 2415919104 | bytes 9437184 | tf_op jit(solution)/shard_map/pallas_call | solution.py:474
  31.2 0.4 collective-permute-start.9
  31.7 1.6 %collective-permute-start.15 = (bf16[256,256]{1,0:T(8,128)(2,1)S(1)}, bf16[256,256]{1,0:T(8,128)(2,1)S(1)}, u32[]{:S(2)}, u32[]{:S(2)}) collective-permute-start(bf16[256,256]{1,0:T(8,128)(2,1)S(1)} %shard_map.143), channel_id=1, source_target_pairs={{0,8},{8,0},{16,24},{24,16},{1,9},{9,1},{17,25},{25,17},{2,10},{10... | collective-permute-start | bytes 393224 | tf_op jit(solution)/shard_map/ppermute | solution.py:361
  33.3 0.0 collective-permute-done.10.other_ref
  33.3 0.0 copy-done
  33.3 1.0 %shard_map.138.first_ref = bf16[256,1024]{1,0:T(8,128)(2,1)S(1)} custom-call(f32[256,1536]{1,0:T(8,128)S(1)} %shard_map.136.z_ref, f32[256,1536]{1,0:T(8,128)S(1)} %collective-permute-done.10.other_ref, bf16[1536,1024]{1,0:T(8,128)(2,1)S(1)} %copy-done), custom_call_target="tpu_custom_call" | custom-call | flops 805306368 | bytes 3145728 | tf_op jit(solution)/shard_map/pallas_call | solution.py:493
  34.3 0.9 %shard_map.139.hot_ref = bf16[576,512]{1,0:T(8,128)(2,1)S(1)} custom-call(s32[6]{0:T(128)S(1)} %stack.20.pos_ref.refs_0_, bf16[160,384]{1,0:T(8,128)(2,1)S(1)} %get-tuple-element.35.refs_0_, bf16[160,384]{1,0:T(8,128)(2,1)S(1)} %collective-permute-done.refs_1_, bf16[160,384]{1,0:T(8,128)(2,1)S(1)} %collective-permute-done.1.refs_2_, ...), custom_call_target="tpu_custom_call" | custom-call | flops 100000000 | bytes 1000000 | tf_op jit(solution)/shard_map/pallas_call | solution.py:502
  35.2 0.0 copy-start.5
  35.2 0.0 copy-start.6
  35.2 0.0 collective-permute-done.9.other_ref
  35.2 2.9 %shard_map.140.a_ref = f32[64,256]{1,0:T(8,128)S(1)} custom-call(f32[256,1536]{1,0:T(8,128)S(1)} %shard_map.137.z_ref, f32[256,1536]{1,0:T(8,128)S(1)} %collective-permute-done.9.other_ref, bf16[256,1024]{1,0:T(8,128)(2,1)S(1)} %shard_map.138.first_ref, bf16[1536,1024]{1,0:T(8,128)(2,1)S(1)} %copy-done, bf16[9,1024,256]{2,1,0:T(8,128)(2,1)S(1)} %bitcast.18, ...), custom_call_target="tpu_custom_call" | custom-call | flops 2013265920 | bytes 6291456 | tf_op jit(solution)/shard_map/pallas_call | solution.py:511
  38.1 0.0 collective-permute-done.15.refs_2_
  38.2 0.1 collective-permute-start.16
  38.2 0.5 %collective-permute-start.11 = (f32[64,256]{1,0:T(8,128)S(1)}, f32[64,256]{1,0:T(8,128)S(1)}, u32[]{:S(2)}, u32[]{:S(2)}) collective-permute-start(f32[64,256]{1,0:T(8,128)S(1)} %shard_map.140.a_ref), channel_id=1, source_target_pairs={{0,1},{1,0},{2,3},{3,2},{4,5},{5,4},{6,7},{7,6},{8,9},{9,8},{10,11... | collective-permute-start | bytes 196616 | tf_op jit(solution)/shard_map/ppermute | solution.py:361
  38.7 1.0 %shard_map.142 = (bf16[64,256]{1,0:T(8,128)(2,1)S(1)}, f32[64,128]{1,0:T(8,128)S(1)}) custom-call(s32[6]{0:T(128)S(1)} %stack.20.pos_ref.refs_0_, bf16[160,384]{1,0:T(8,128)(2,1)S(1)} %get-tuple-element.35.refs_0_, bf16[160,384]{1,0:T(8,128)(2,1)S(1)} %collective-permute-done.refs_1_, bf16[160,384]{1,0:T(8,128)(2,1)S(1)} %collective-permute-done.1.refs_2_, ...), custom_call_target="tpu_custom_call" | custom-call | flops 100000000 | bytes 1000000 | tf_op jit(solution)/shard_map/pallas_call | solution.py:523
  39.7 0.1 collective-permute-done.11.b_ref
  39.9 1.0 %collective-permute-start.12 = (bf16[64,256]{1,0:T(8,128)(2,1)S(1)}, bf16[64,256]{1,0:T(8,128)(2,1)S(1)}, u32[]{:S(2)}, u32[]{:S(2)}) collective-permute-start(bf16[64,256]{1,0:T(8,128)(2,1)S(1)} %get-tuple-element.45), channel_id=1, source_target_pairs={{0,2},{2,0},{4,6},{6,4},{1,3},{3,1},{5,7},{7,5},{8,10},{10,8},{12,... | collective-permute-start | bytes 98312 | tf_op jit(solution)/shard_map/ppermute | solution.py:361
  40.9 1.0 %collective-permute-start.13 = (bf16[64,256]{1,0:T(8,128)(2,1)S(1)}, bf16[64,256]{1,0:T(8,128)(2,1)S(1)}, u32[]{:S(2)}, u32[]{:S(2)}) collective-permute-start(bf16[64,256]{1,0:T(8,128)(2,1)S(1)} %get-tuple-element.45), channel_id=1, source_target_pairs={{0,4},{2,6},{4,0},{6,2},{1,5},{3,7},{5,1},{7,3},{8,12},{10,14},{12... | collective-permute-start | bytes 98312 | tf_op jit(solution)/shard_map/ppermute | solution.py:361
  41.8 1.6 %collective-permute-start.14 = (bf16[64,256]{1,0:T(8,128)(2,1)S(1)}, bf16[64,256]{1,0:T(8,128)(2,1)S(1)}, u32[]{:S(2)}, u32[]{:S(2)}) collective-permute-start(bf16[64,256]{1,0:T(8,128)(2,1)S(1)} %get-tuple-element.45), channel_id=1, source_target_pairs={{0,6},{2,4},{4,2},{6,0},{1,7},{3,5},{5,3},{7,1},{8,14},{10,12},{12... | collective-permute-start | bytes 98312 | tf_op jit(solution)/shard_map/ppermute | solution.py:361
  43.4 0.0 collective-permute-done.16.refs_3_
  43.4 0.2 shard_map.145
  43.7 0.2 collective-permute-done.12.refs_2_
  43.8 0.9 %collective-permute-done.13.refs_3_ = bf16[64,256]{1,0:T(8,128)(2,1)S(1)} collective-permute-done((bf16[64,256]{1,0:T(8,128)(2,1)S(1)}, bf16[64,256]{1,0:T(8,128)(2,1)S(1)}, u32[]{:S(2)}, u32[]{:S(2)}) %collective-permute-start.13) | collective-permute-done | bytes 32800 | tf_op jit(solution)/shard_map/ppermute | solution.py:361
  44.8 1.9 %collective-permute-done.14.refs_4_ = bf16[64,256]{1,0:T(8,128)(2,1)S(1)} collective-permute-done((bf16[64,256]{1,0:T(8,128)(2,1)S(1)}, bf16[64,256]{1,0:T(8,128)(2,1)S(1)}, u32[]{:S(2)}, u32[]{:S(2)}) %collective-permute-start.14) | collective-permute-done | bytes 32800 | tf_op jit(solution)/shard_map/ppermute | solution.py:361
  46.7 1.8 %shard_map.146 = (f32[64,256]{1,0:T(8,128)}, f32[1,64]{1,0:T(1,128)}) custom-call(s32[6]{0:T(128)S(1)} %stack.20.pos_ref.refs_0_, f32[64,256]{1,0:T(8,128)S(1)} %get-tuple-element.44.refs_1_, bf16[64,256]{1,0:T(8,128)(2,1)S(1)} %collective-permute-done.12.refs_2_, bf16[64,256]{1,0:T(8,128)(2,1)S(1)} %collective-permute-done.13.refs_3_, ...), custom_call_target="tpu_custom_call" | custom-call | flops 100000000 | bytes 1000000 | tf_op jit(solution)/shard_map/pallas_call | solution.py:555
  (20 shorter events, 0.1 us)
Async XLA Ops:
  2.0 4.7 %copy-start.1 = (bf16[64,256]{1,0:T(8,128)(2,1)S(1)}, bf16[64,256]{1,0:T(8,128)(2,1)}, u32[]{:S(2)}) copy-start(bf16[64,256]{1,0:T(8,128)(2,1)} %key_ref.1) | copy-start | bytes 98308
  2.0 4.7 %copy-start.4 = (s32[4,4,32]{2,1,0:T(4,128)S(1)}, s32[4,4,32]{2,1,0:T(4,128)}, u32[]{:S(2)}) copy-start(s32[4,4,32]{2,1,0:T(4,128)} %ids_ref.1) | copy-start | bytes 6148
  2.0 10.9 %copy-start.7 = (bf16[7,7,1536]{2,1,0:T(8,128)(2,1)S(1)}, bf16[7,7,1536]{2,1,0:T(8,128)(2,1)}, u32[]{:S(2)}) copy-start(bf16[7,7,1536]{2,1,0:T(8,128)(2,1)} %refs_4_.4) | copy-start | bytes 451588
  2.0 8.8 %collective-permute-start.3 = (bf16[128,384]{1,0:T(8,128)(2,1)S(1)}, bf16[128,384]{1,0:T(8,128)(2,1)S(1)}, u32[]{:S(2)}, u32[]{:S(2)}) collective-permute-start(bf16[128,384]{1,0:T(8,128)(2,1)S(1)} %bitcast.27), channel_id=1, source_target_pairs={{0,2},{2,0},{4,6},{6,4},{1,3},{3,1},{5,7},{7,5},{8,10},{10,8},{12,... | collective-permute-start | bytes 294920 | tf_op jit(solution)/shard_map/ppermute | solution.py:361
  5.0 6.3 %collective-permute-start.4 = (bf16[128,384]{1,0:T(8,128)(2,1)S(1)}, bf16[128,384]{1,0:T(8,128)(2,1)S(1)}, u32[]{:S(2)}, u32[]{:S(2)}) collective-permute-start(bf16[128,384]{1,0:T(8,128)(2,1)S(1)} %bitcast.26), channel_id=1, source_target_pairs={{0,4},{2,6},{4,0},{6,2},{1,5},{3,7},{5,1},{7,3},{8,12},{10,14},{12... | collective-permute-start | bytes 294920 | tf_op jit(solution)/shard_map/ppermute | solution.py:361
  6.5 6.3 %collective-permute-start.5 = (bf16[128,384]{1,0:T(8,128)(2,1)S(1)}, bf16[128,384]{1,0:T(8,128)(2,1)S(1)}, u32[]{:S(2)}, u32[]{:S(2)}) collective-permute-start(bf16[128,384]{1,0:T(8,128)(2,1)S(1)} %bitcast.25), channel_id=1, source_target_pairs={{0,6},{2,4},{4,2},{6,0},{1,7},{3,5},{5,3},{7,1},{8,14},{10,12},{12... | collective-permute-start | bytes 294920 | tf_op jit(solution)/shard_map/ppermute | solution.py:361
  7.2 16.1 %slice-start.2 = ((s8[4718592]{0:T(1024)(128)(4,1)}), s8[524288]{0:T(1024)(128)(4,1)S(1)}, s32[]{:S(2)}) async-start(s8[4718592]{0:T(1024)(128)(4,1)} %bitcast.15), calls=%async_computation.2 | async-start | bytes 1048576
  7.3 9.2 %collective-permute-start = (bf16[160,384]{1,0:T(8,128)(2,1)S(1)}, bf16[160,384]{1,0:T(8,128)(2,1)S(1)}, u32[]{:S(2)}, u32[]{:S(2)}) collective-permute-start(bf16[160,384]{1,0:T(8,128)(2,1)S(1)} %get-tuple-element.63), channel_id=1, source_target_pairs={{0,2},{2,0},{4,6},{6,4},{1,3},{3,1},{5,7},{7,5},{8,10},{10,8},{12,... | collective-permute-start | bytes 368648 | tf_op jit(solution)/shard_map/ppermute | solution.py:361
  9.3 7.7 %collective-permute-start.1 = (bf16[160,384]{1,0:T(8,128)(2,1)S(1)}, bf16[160,384]{1,0:T(8,128)(2,1)S(1)}, u32[]{:S(2)}, u32[]{:S(2)}) collective-permute-start(bf16[160,384]{1,0:T(8,128)(2,1)S(1)} %get-tuple-element.64), channel_id=1, source_target_pairs={{0,4},{2,6},{4,0},{6,2},{1,5},{3,7},{5,1},{7,3},{8,12},{10,14},{12... | collective-permute-start | bytes 368648 | tf_op jit(solution)/shard_map/ppermute | solution.py:361
  10.8 12.5 %slice-start.3 = ((s8[4718592]{0:T(1024)(128)(4,1)}), s8[4194304]{0:T(1024)(128)(4,1)S(1)}, s32[]{:S(2)}) async-start(s8[4718592]{0:T(1024)(128)(4,1)} %bitcast.15), calls=%async_computation.3 | async-start | bytes 8388608
  10.8 6.2 %collective-permute-start.2 = (bf16[160,384]{1,0:T(8,128)(2,1)S(1)}, bf16[160,384]{1,0:T(8,128)(2,1)S(1)}, u32[]{:S(2)}, u32[]{:S(2)}) collective-permute-start(bf16[160,384]{1,0:T(8,128)(2,1)S(1)} %get-tuple-element.62), channel_id=1, source_target_pairs={{0,6},{2,4},{4,2},{6,0},{1,7},{3,5},{5,3},{7,1},{8,14},{10,12},{12... | collective-permute-start | bytes 368648 | tf_op jit(solution)/shard_map/ppermute | solution.py:361
  12.9 10.4 %slice-start = ((s8[4718592]{0:T(1024)(128)(4,1)}), s8[4194304]{0:T(1024)(128)(4,1)S(1)}, s32[]{:S(2)}) async-start(s8[4718592]{0:T(1024)(128)(4,1)} %bitcast.13), calls=%async_computation | async-start | bytes 8388608
  16.4 6.9 %collective-permute-start.7 = (f32[512,384]{1,0:T(8,128)S(1)}, f32[512,384]{1,0:T(8,128)S(1)}, u32[]{:S(2)}, u32[]{:S(2)}) collective-permute-start(f32[512,384]{1,0:T(8,128)S(1)} %get-tuple-element.32.refs_0_), channel_id=1, source_target_pairs={{0,1},{1,0},{2,3},{3,2},{4,5},{5,4},{6,7},{7,6},{8,9},{9,8},{10,11... | collective-permute-start | bytes 2359304 | tf_op jit(solution)/shard_map/ppermute | solution.py:361
  17.0 6.3 %slice-start.1 = ((s8[4718592]{0:T(1024)(128)(4,1)}), s8[524288]{0:T(1024)(128)(4,1)S(1)}, s32[]{:S(2)}) async-start(s8[4718592]{0:T(1024)(128)(4,1)} %bitcast.13), calls=%async_computation.1 | async-start | bytes 1048576
  17.0 6.3 %copy-start.2 = (bf16[1536]{0:T(1024)(128)(2,1)S(1)}, bf16[1536]{0:T(1024)(128)(2,1)}, u32[]{:S(2)}) copy-start(bf16[1536]{0:T(1024)(128)(2,1)} %refs_6_.3) | copy-start | bytes 9220
  17.0 6.3 %copy-start.3 = (bf16[1536]{0:T(1024)(128)(2,1)S(1)}, bf16[1536]{0:T(1024)(128)(2,1)}, u32[]{:S(2)}) copy-start(bf16[1536]{0:T(1024)(128)(2,1)} %refs_7_.3) | copy-start | bytes 9220
  20.5 2.8 %collective-permute-start.8 = (f32[512,384]{1,0:T(8,128)S(1)}, f32[512,384]{1,0:T(8,128)S(1)}, u32[]{:S(2)}, u32[]{:S(2)}) collective-permute-start(f32[512,384]{1,0:T(8,128)S(1)} %get-tuple-element.34.refs_1_), channel_id=1, source_target_pairs={{0,1},{1,0},{2,3},{3,2},{4,5},{5,4},{6,7},{7,6},{8,9},{9,8},{10,11... | collective-permute-start | bytes 2359304 | tf_op jit(solution)/shard_map/ppermute | solution.py:361
  20.6 6.8 %collective-permute-start.6 = (bf16[128,256]{1,0:T(8,128)(2,1)S(1)}, bf16[128,256]{1,0:T(8,128)(2,1)S(1)}, u32[]{:S(2)}, u32[]{:S(2)}) collective-permute-start(bf16[128,256]{1,0:T(8,128)(2,1)S(1)} %shard_map.135.refs_0_), channel_id=1, source_target_pairs={{0,16},{8,24},{16,0},{24,8},{1,17},{9,25},{17,1},{25,9},{2,18},{10... | collective-permute-start | bytes 196616 | tf_op jit(solution)/shard_map/ppermute | solution.py:361
  23.3 11.9 %slice-start.4 = ((s8[4718592]{0:T(1024)(128)(4,1)}), s8[4194304]{0:T(1024)(128)(4,1)S(1)}, s32[]{:S(2)}) async-start(s8[4718592]{0:T(1024)(128)(4,1)} %bitcast.17), calls=%async_computation.4 | async-start | bytes 8388608
  27.2 8.0 %slice-start.5 = ((s8[4718592]{0:T(1024)(128)(4,1)}), s8[524288]{0:T(1024)(128)(4,1)S(1)}, s32[]{:S(2)}) async-start(s8[4718592]{0:T(1024)(128)(4,1)} %bitcast.17), calls=%async_computation.5 | async-start | bytes 1048576
  27.2 6.1 %collective-permute-start.10 = (f32[256,1536]{1,0:T(8,128)S(1)}, f32[256,1536]{1,0:T(8,128)S(1)}, u32[]{:S(2)}, u32[]{:S(2)}) collective-permute-start(f32[256,1536]{1,0:T(8,128)S(1)} %shard_map.136.z_ref), channel_id=1, source_target_pairs={{0,1},{1,0},{2,3},{3,2},{4,5},{5,4},{6,7},{7,6},{8,9},{9,8},{10,11... | collective-permute-start | bytes 4718600 | tf_op jit(solution)/shard_map/ppermute | solution.py:361
  27.4 5.9 %copy-start = (bf16[1536,1024]{1,0:T(8,128)(2,1)S(1)}, bf16[1536,1024]{1,0:T(8,128)(2,1)}, u32[]{:S(2)}) copy-start(bf16[1536,1024]{1,0:T(8,128)(2,1)} %pe_ref.3) | copy-start | bytes 9437188
  31.2 4.0 %collective-permute-start.9 = (f32[256,1536]{1,0:T(8,128)S(1)}, f32[256,1536]{1,0:T(8,128)S(1)}, u32[]{:S(2)}, u32[]{:S(2)}) collective-permute-start(f32[256,1536]{1,0:T(8,128)S(1)} %shard_map.137.z_ref), channel_id=1, source_target_pairs={{0,1},{1,0},{2,3},{3,2},{4,5},{5,4},{6,7},{7,6},{8,9},{9,8},{10,11... | collective-permute-start | bytes 4718600 | tf_op jit(solution)/shard_map/ppermute | solution.py:361
  31.7 6.4 %collective-permute-start.15 = (bf16[256,256]{1,0:T(8,128)(2,1)S(1)}, bf16[256,256]{1,0:T(8,128)(2,1)S(1)}, u32[]{:S(2)}, u32[]{:S(2)}) collective-permute-start(bf16[256,256]{1,0:T(8,128)(2,1)S(1)} %shard_map.143), channel_id=1, source_target_pairs={{0,8},{8,0},{16,24},{24,16},{1,9},{9,1},{17,25},{25,17},{2,10},{10... | collective-permute-start | bytes 393224 | tf_op jit(solution)/shard_map/ppermute | solution.py:361
  35.2 3.6 %copy-start.5 = (s32[4,64]{1,0:T(4,128)S(1)}, s32[4,64]{1,0:T(4,128)}, u32[]{:S(2)}) copy-start(s32[4,64]{1,0:T(4,128)} %refs_5_.1) | copy-start | bytes 3076
  35.2 3.6 %copy-start.6 = (s32[1,256]{1,0:T(1,128)S(1)}, s32[1,256]{1,0:T(1,128)}, u32[]{:S(2)}) copy-start(s32[1,256]{1,0:T(1,128)} %refs_4_.5) | copy-start | bytes 3076
  38.2 5.3 %collective-permute-start.16 = (bf16[512,256]{1,0:T(8,128)(2,1)S(1)}, bf16[512,256]{1,0:T(8,128)(2,1)S(1)}, u32[]{:S(2)}, u32[]{:S(2)}) collective-permute-start(bf16[512,256]{1,0:T(8,128)(2,1)S(1)} %shard_map.144), channel_id=1, source_target_pairs={{0,1},{1,0},{2,3},{3,2},{4,5},{5,4},{6,7},{7,6},{8,9},{9,8},{10,11... | collective-permute-start | bytes 786440 | tf_op jit(solution)/shard_map/ppermute | solution.py:361
  38.2 1.6 %collective-permute-start.11 = (f32[64,256]{1,0:T(8,128)S(1)}, f32[64,256]{1,0:T(8,128)S(1)}, u32[]{:S(2)}, u32[]{:S(2)}) collective-permute-start(f32[64,256]{1,0:T(8,128)S(1)} %shard_map.140.a_ref), channel_id=1, source_target_pairs={{0,1},{1,0},{2,3},{3,2},{4,5},{5,4},{6,7},{7,6},{8,9},{9,8},{10,11... | collective-permute-start | bytes 196616 | tf_op jit(solution)/shard_map/ppermute | solution.py:361
  39.9 4.0 %collective-permute-start.12 = (bf16[64,256]{1,0:T(8,128)(2,1)S(1)}, bf16[64,256]{1,0:T(8,128)(2,1)S(1)}, u32[]{:S(2)}, u32[]{:S(2)}) collective-permute-start(bf16[64,256]{1,0:T(8,128)(2,1)S(1)} %get-tuple-element.45), channel_id=1, source_target_pairs={{0,2},{2,0},{4,6},{6,4},{1,3},{3,1},{5,7},{7,5},{8,10},{10,8},{12,... | collective-permute-start | bytes 98312 | tf_op jit(solution)/shard_map/ppermute | solution.py:361
  40.9 3.9 %collective-permute-start.13 = (bf16[64,256]{1,0:T(8,128)(2,1)S(1)}, bf16[64,256]{1,0:T(8,128)(2,1)S(1)}, u32[]{:S(2)}, u32[]{:S(2)}) collective-permute-start(bf16[64,256]{1,0:T(8,128)(2,1)S(1)} %get-tuple-element.45), channel_id=1, source_target_pairs={{0,4},{2,6},{4,0},{6,2},{1,5},{3,7},{5,1},{7,3},{8,12},{10,14},{12... | collective-permute-start | bytes 98312 | tf_op jit(solution)/shard_map/ppermute | solution.py:361
  41.8 4.8 %collective-permute-start.14 = (bf16[64,256]{1,0:T(8,128)(2,1)S(1)}, bf16[64,256]{1,0:T(8,128)(2,1)S(1)}, u32[]{:S(2)}, u32[]{:S(2)}) collective-permute-start(bf16[64,256]{1,0:T(8,128)(2,1)S(1)} %get-tuple-element.45), channel_id=1, source_target_pairs={{0,6},{2,4},{4,2},{6,0},{1,7},{3,5},{5,3},{7,1},{8,14},{10,12},{12... | collective-permute-start | bytes 98312 | tf_op jit(solution)/shard_map/ppermute | solution.py:361
